TPU v7x, 128 devices: a whole 4x4x4 slice. The times are simulated.
128 devices in a mesh: member: 8 (over z_hi, x), sector: 16 (over z_lo, y, core).
Axes of the slice: x: 4, y: 4, z: 4 (z_hi: 2, z_lo: 2; z = z_hi * 2 + z_lo), core: 2. Of those that a mesh axis runs over, the one named last changes fastest.
Arguments:
- ensemble: float32 [128, 5, 1440, 128], P('member', None, 'sector'), may hold values from -6 to 6
- ocean_depth: float32 [1440, 128], P('sector'), may hold values from 0.5 to 2
- planetary_vorticity: float32 [128], replicated, may hold values from -0.5 to 0.5
- land_mask: int32 [1440, 128], P('sector'), may hold values 0 or 1
- obs_values: float32 [1024], replicated, may hold values from -6 to 6
- obs_error: float32 [1024], replicated, may hold values from 0.2 to 2
- obs_lon: int32 [1024], replicated, may hold values from 0 to 1439
- obs_lat: int32 [1024], replicated, may hold values from 0 to 127
- obs_field: int32 [1024], replicated, may hold values from 2 to 4
- obs_order: int32 [1024], replicated, may hold values from 0 to 1023, each once
Outputs:
- analysis: float32 [5, 128, 1440, 128], P(None, 'member', 'sector')
Inputs may be any that keep to these rules, and one draw needn't show every extreme that they name: `obs_field`: observed fields are height, temperature or salinity. `obs_order`: each observation index appears once.
All inputs are finite; a program needn't handle non-finite values. No bound on the sum of `land_mask` on one device may be relied on, other than what follows from the above.
Results may differ from a plain program's by a relative error of at most 0.0001.
Values sent between devices are 32-bit elements; how exact they have to be, the bound alone decides.
No kernel may reach another device: no remote copies, remote signals or barrier semaphores. Data moves between devices by JAX's collectives and lax.ppermute only.
A program may use at most 128 MiB of HBM per device.

v0:
```python
import jax
import jax.numpy as jnp
from jax import lax
from jax.experimental import pallas as pl
from jax.experimental.pallas import tpu as pltpu
from jax.sharding import PartitionSpec as P

NLON = 1440
LAT = 128
FIELDS = 5
MEMBERS = 128
NOBS = 1024
BATCH = 512
BLOCKS = NOBS // LAT
RADIUS = 48
SHARE = 16
BANDS = 8
WIDTH = 90
EDGE = 4
INNER = 9
RIGHT = 80
INSIDE = FIELDS * INNER
OUTSIDE = 2 * FIELDS + 2
GROUPS = INSIDE + OUTSIDE
EDGE_ROWS = FIELDS * EDGE * SHARE
CUT = 48
SLOTS = 128
CHUNKS = BATCH // SLOTS
SCALE = 1.0 / (RADIUS * RADIUS)
F32 = jnp.float32
BF16 = jnp.bfloat16
SMEM = pl.BlockSpec(memory_space=pltpu.SMEM)
VMEM = pl.BlockSpec(memory_space=pltpu.VMEM)
ANY = pl.BlockSpec(memory_space=pl.ANY)
PARAMS = pltpu.CompilerParams(vmem_limit_bytes=56 * 1024 * 1024)


def edges_kernel(ens, depth, mask, west, east, sems):
    copies = []
    for i, (out, lon) in enumerate(((west, 0), (east, WIDTH - EDGE))):
        copies.append(
            pltpu.make_async_copy(ens.at[:, pl.ds(lon, EDGE)], out.at[pl.ds(0, FIELDS)], sems.at[i])
        )
        copies[-1].start()
        grids = jnp.concatenate(
            [depth[pl.ds(lon, EDGE), :], mask[pl.ds(lon, EDGE), :].astype(F32)], axis=0
        )
        out[FIELDS, 0, pl.ds(0, 8), :] = grids
    for c in copies:
        c.wait()


def edges(ens, depth, mask):
    side = jax.ShapeDtypeStruct((FIELDS + 1, EDGE, SHARE, LAT), F32)
    return pl.pallas_call(
        edges_kernel,
        out_shape=[side, side],
        in_specs=[ANY, VMEM, VMEM],
        out_specs=[VMEM, VMEM],
        scratch_shapes=[pltpu.SemaphoreType.DMA((2,))],
        compiler_params=PARAMS,
        name="pack_edges",
    )(ens, depth, mask)


def stepper(dep, sea, vort, flux):
    lane = lax.broadcasted_iota(jnp.int32, (SHARE, LAT), 1)
    first, last = lane == 0, lane == LAT - 1
    spin = jnp.broadcast_to(vort[...], (SHARE, LAT))

    def north(a):
        return jnp.where(last, 0.0, pltpu.roll(a, LAT - 1, 1))

    def south(a):
        return jnp.where(first, 0.0, pltpu.roll(a, 1, 1))

    def step(src, dst, lo, hi, row, unroll):
        def flow(e, _):
            u, v, h = src[0, e], src[1, e], src[2, e]
            m = sea[pl.ds(e + row, 1), :]
            un = m * (u + spin * v - 0.15 * (src[2, e + 1] - src[2, e - 1]))
            dst[0, e] = un
            dst[1, e] = m * (v - spin * u - 0.15 * (north(h) - south(h)))
            flux[e] = dep[pl.ds(e + row, 1), :] * un
            return 0

        def others(e, _):
            un, vn = dst[0, e], dst[1, e]
            dv = dep[pl.ds(e + row, 1), :] * vn
            dst[2, e] = src[2, e] - 0.15 * (flux[e + 1] - flux[e - 1] + (north(dv) - south(dv)))
            for c in (3, 4):
                a, ae, aw = src[c, e], src[c, e + 1], src[c, e - 1]
                an, ao = north(a), south(a)
                dst[c, e] = (
                    a
                    - 0.15 * (un * (ae - aw) + vn * (an - ao))
                    + 0.1 * (((ae + aw) + (an + ao)) - 4.0 * a)
                )
            return 0

        lax.fori_loop(lo, hi, flow, 0, unroll=2 * unroll)
        lax.fori_loop(lo + 1, hi - 1, others, 0, unroll=unroll)

    return step


def turn(tiles, out, g):
    tile = jnp.transpose(tiles.reshape(8 * SHARE, LAT))
    for b in range(BANDS):
        out[b, g] = tile[b * SHARE : (b + 1) * SHARE]


def inner_kernel(ens, depth, mask, vort, out, seen, now, nxt, flux, sea, made, sems):
    span = INNER * 8
    load = pltpu.make_async_copy(ens.at[:, pl.ds(EDGE, span + 2 * EDGE)], now, sems.at[0])
    load.start()
    sea[...] = mask[...].astype(F32)
    step = stepper(depth, sea, vort, flux)
    load.wait()
    step(now, nxt, 1, span + 7, EDGE, 4)
    step(nxt, now, 3, span + 5, EDGE, 4)
    keep = pltpu.make_async_copy(
        now.at[pl.ds(2, 3), pl.ds(EDGE, span)], seen.at[:, pl.ds(8, span)], sems.at[1]
    )
    keep.start()

    def field(f, _):
        for i in range(INNER):
            turn(now[f, pl.ds(EDGE + i * 8, 8)], made, f * INNER + i)
        return 0

    lax.fori_loop(0, FIELDS, field, 0)
    send = pltpu.make_async_copy(made, out.at[:, pl.ds(0, INSIDE)], sems.at[0])
    send.start()
    send.wait()
    keep.wait()


def forecast_inner(ens, depth, mask, vort):
    window = INNER * 8 + 2 * EDGE
    return pl.pallas_call(
        inner_kernel,
        out_shape=[
            jax.ShapeDtypeStruct((BANDS, GROUPS, SHARE, LAT), F32),
            jax.ShapeDtypeStruct((3, WIDTH, SHARE, LAT), F32),
        ],
        in_specs=[ANY, VMEM, VMEM, VMEM],
        out_specs=[ANY, ANY],
        scratch_shapes=[
            pltpu.VMEM((FIELDS, window, SHARE, LAT), F32),
            pltpu.VMEM((FIELDS, window, SHARE, LAT), F32),
            pltpu.VMEM((window, SHARE, LAT), F32),
            pltpu.VMEM((WIDTH, LAT), F32),
            pltpu.VMEM((BANDS, INSIDE, SHARE, LAT), F32),
            pltpu.SemaphoreType.DMA((2,)),
        ],
        compiler_params=PARAMS,
        name="forecast_inner",
    )(ens, depth, mask, vort)


def outer_kernel(
    ens, left, right, depth, mask, vort, _, _2, out, seen, now, nxt, flux, dep, sea, made, sems
):
    near, far = 3 * EDGE, 3 * EDGE + 2
    second = near + EDGE
    loads = [
        pltpu.make_async_copy(ens.at[:, pl.ds(0, near)], now.at[:, pl.ds(EDGE, near)], sems.at[0]),
        pltpu.make_async_copy(
            ens.at[:, pl.ds(WIDTH - far, far)], now.at[:, pl.ds(second, far)], sems.at[1]
        ),
        pltpu.make_async_copy(left.at[pl.ds(0, FIELDS)], now.at[:, pl.ds(0, EDGE)], sems.at[2]),
        pltpu.make_async_copy(
            right.at[pl.ds(0, FIELDS)], now.at[:, pl.ds(second + far, EDGE)], sems.at[3]
        ),
    ]
    for c in loads:
        c.start()
    for grid, own, at in ((dep, depth, 0), (sea, mask, EDGE)):
        grid[pl.ds(8, WIDTH), :] = own[...].astype(F32)
        grid[pl.ds(4, EDGE), :] = left[FIELDS, 0, pl.ds(at, EDGE), :]
        grid[pl.ds(8 + WIDTH, EDGE), :] = right[FIELDS, 0, pl.ds(at, EDGE), :]
    step = stepper(dep, sea, vort, flux)
    for c in loads:
        c.wait()
    end = second + far + EDGE
    skip = 8 + WIDTH - far - second
    step(now, nxt, 1, second - 1, 4, 4)
    step(now, nxt, second + 1, end - 1, skip, 4)
    step(nxt, now, 3, second - 3, 4, 4)
    step(nxt, now, second + 3, end - 3, skip, 5)
    right_at = second + EDGE
    keeps = [
        pltpu.make_async_copy(
            now.at[pl.ds(2, 3), pl.ds(EDGE, 8)], seen.at[:, pl.ds(0, 8)], sems.at[1]
        ),
        pltpu.make_async_copy(
            now.at[pl.ds(2, 3), pl.ds(right_at, WIDTH - RIGHT)],
            seen.at[:, pl.ds(RIGHT, WIDTH - RIGHT)],
            sems.at[2],
        ),
    ]
    for c in keeps:
        c.start()
    for f in range(FIELDS):
        turn(now[f, pl.ds(EDGE, 8)], made, 2 * f)
        turn(now[f, pl.ds(right_at, 8)], made, 2 * f + 1)
    turn(now[pl.ds(0, 4), pl.ds(right_at + 8, 2)], made, 2 * FIELDS)
    last = now[4, pl.ds(right_at + 8, 2)]
    turn(jnp.concatenate([last] * 4, axis=0), made, 2 * FIELDS + 1)
    send = pltpu.make_async_copy(made, out.at[:, pl.ds(INSIDE, OUTSIDE)], sems.at[0])
    send.start()
    send.wait()
    for c in keeps:
        c.wait()


def forecast_outer(ens, left, right, depth, mask, vort, messages, seen):
    window = 6 * EDGE + 2 + 2 * EDGE
    return pl.pallas_call(
        outer_kernel,
        out_shape=[
            jax.ShapeDtypeStruct(messages.shape, F32),
            jax.ShapeDtypeStruct(seen.shape, F32),
        ],
        in_specs=[ANY] + [VMEM] * 5 + [ANY] * 2,
        out_specs=[ANY, ANY],
        scratch_shapes=[
            pltpu.VMEM((FIELDS, window, SHARE, LAT), F32),
            pltpu.VMEM((FIELDS, window, SHARE, LAT), F32),
            pltpu.VMEM((window, SHARE, LAT), F32),
            pltpu.VMEM((112, LAT), F32),
            pltpu.VMEM((112, LAT), F32),
            pltpu.VMEM((BANDS, OUTSIDE, SHARE, LAT), F32),
            pltpu.SemaphoreType.DMA((4,)),
        ],
        input_output_aliases={6: 0, 7: 1},
        compiler_params=PARAMS,
        name="forecast_outer",
    )(ens, left, right, depth, mask, vort, messages, seen)


def list_kernel(order, cell, out, count):
    def one(j, n):
        at = cell[order[j]]
        out[n] = at + j * (1 << 16)
        return n + jnp.where(at >= 0, 1, 0)

    count[0] = lax.fori_loop(0, NOBS, one, 0, unroll=8)


def own_list(order, cell):
    return pl.pallas_call(
        list_kernel,
        out_shape=[
            jax.ShapeDtypeStruct((NOBS + LAT,), jnp.int32),
            jax.ShapeDtypeStruct((1,), jnp.int32),
        ],
        in_specs=[SMEM, SMEM],
        out_specs=[SMEM, SMEM],
        compiler_params=PARAMS,
        name="own_observations",
    )(order, cell)


def pick_kernel(own, count, seen, out):
    lane = lax.broadcasted_iota(jnp.int32, (SHARE, LAT), 1)
    out[...] = jnp.zeros_like(out)

    def one(i, _):
        code = own[i]
        j, at, lat = code >> 16, (code >> 7) & 511, code & 127
        tile = pltpu.roll(seen[at], (j - lat) & (LAT - 1), 1)
        b = j >> 7
        out[b] = jnp.where(lane == (j & 127), tile, out[b])
        return 0

    lax.fori_loop(0, count[0], one, 0)


def pick(own, count, seen):
    return pl.pallas_call(
        pick_kernel,
        out_shape=jax.ShapeDtypeStruct((BLOCKS, SHARE, LAT), F32),
        in_specs=[SMEM, SMEM, VMEM],
        out_specs=VMEM,
        compiler_params=PARAMS,
        name="pick_priors",
    )(own, count, seen)


def split(a):
    high = a.astype(BF16)
    return high, (a - high.astype(F32)).astype(BF16)


def sort_kernel(order, facts, out):
    data = facts[...]
    high, rest = split(data)
    left = data - high.astype(F32)
    mid, low = split(left)
    parts = jnp.concatenate([high, mid, low, jnp.zeros_like(rest)], axis=0)
    row = lax.broadcasted_iota(jnp.int32, (NOBS, LAT), 0)

    def block(b, _):
        hot = jnp.where(row == order[b], 1.0, 0.0).astype(BF16)
        got = jnp.dot(parts, hot, preferred_element_type=F32)
        out[b] = got[0:8] + got[8:16] + got[16:24]
        return 0

    lax.fori_loop(0, BLOCKS, block, 0)


def in_order(order, facts):
    return pl.pallas_call(
        sort_kernel,
        out_shape=jax.ShapeDtypeStruct((BLOCKS, 8, LAT), F32),
        in_specs=[VMEM, VMEM],
        out_specs=VMEM,
        compiler_params=PARAMS,
        name="obs_in_batch_order",
    )(order.reshape(BLOCKS, 1, LAT), facts)


def dot_nt(a, b):
    return lax.dot_general(a, b, (((1,), (1,)), ((), ())), preferred_element_type=F32)


def exact(a, b, dims):
    return lax.dot_general(
        a, b, (dims, ((), ())), precision=lax.Precision.HIGHEST, preferred_element_type=F32
    )


def paired(high, low):
    top = jnp.concatenate([high, low], axis=1)
    bottom = jnp.concatenate([high, jnp.zeros_like(low)], axis=1)
    return jnp.concatenate([top, bottom], axis=0).astype(BF16)


def filter_kernel(
    place, priors, facts, lead, link, gain, where, many_lead, many_gain, many_where, counts, roots, table
):
    me = place[2]
    for d in range(BANDS):
        at = pl.multiple_of((me ^ d) * SHARE, SHARE)
        for b in range(BLOCKS):
            table[pl.ds(at, SHARE), pl.ds(b * LAT, LAT)] = priors[d, b]
    west, south = place[0].astype(F32), place[1].astype(F32)
    fact = [jnp.concatenate([facts[b * 4 + i] for i in range(4)], axis=1) for b in range(2)]
    later_than = lax.broadcasted_iota(jnp.int32, (BATCH, BATCH), 0)
    later_than = later_than <= lax.broadcasted_iota(jnp.int32, (BATCH, BATCH), 1)
    upper = jnp.where(later_than, 1.0, 0.0).astype(BF16)

    def adjust(picked, b):
        values, errors = fact[b][2:3], fact[b][3:4]
        mean = jnp.sum(picked, axis=0, keepdims=True) * (1.0 / MEMBERS)
        anomalies = picked - mean
        variance = jnp.sum(anomalies * anomalies, axis=0, keepdims=True) / (MEMBERS - 1) + 1e-6
        innovation = values - mean
        ratio = jnp.sum(innovation * innovation, axis=1, keepdims=True) / jnp.sum(
            variance + errors, axis=1, keepdims=True
        )
        root = jnp.sqrt(ratio)
        inflated = ratio * variance
        spread = root * anomalies
        post_var = 1.0 / (1.0 / inflated + 1.0 / errors)
        post_mean = post_var * (mean / inflated + values / errors)
        increments = post_mean - mean + (jnp.sqrt(post_var / inflated) - 1.0) * spread
        return root, spread / ((MEMBERS - 1) * inflated), increments

    root1, scaled1, inc1 = adjust(table[:, pl.ds(0, BATCH)], 0)

    later = table[:, pl.ds(BATCH, BATCH)]
    mean = jnp.sum(later, axis=0, keepdims=True) * (1.0 / MEMBERS)
    spread = root1 * (later - mean)
    cov = exact(scaled1, spread, ((0,), (0,)))

    def column(a):
        tall = jnp.transpose(jnp.broadcast_to(a, (LAT, BATCH)))
        return jnp.concatenate([tall] * (BATCH // LAT), axis=1)

    east = jnp.abs(column(fact[0][0:1]) - fact[1][0:1])
    east = jnp.minimum(east, NLON - east)
    up = column(fact[0][1:2]) - fact[1][1:2]
    taper = jnp.maximum(1.0 - (east * east + up * up) * SCALE, 0.0)
    later = (mean + spread) + exact(inc1, taper * taper * cov, ((1,), (0,)))
    root2, scaled2, inc2 = adjust(later, 1)
    roots[0] = jnp.sum(root1)
    roots[1] = jnp.sum(root2)

    rel, lat = [], []
    for b in range(2):
        r = fact[b][0:1] - west
        r = jnp.where(r < -float(NLON // 2 - WIDTH // 2), r + NLON, r)
        r = jnp.where(r >= float(NLON // 2 + WIDTH // 2), r - NLON, r)
        rel.append(r)
        lat.append(fact[b][1:2] - south)

    def near(b, lo, hi):
        dl = jnp.maximum(jnp.maximum(lo - rel[b], rel[b] - hi), 0.0)
        dr = jnp.maximum(jnp.maximum(-lat[b], lat[b] - (SHARE - 1.0)), 0.0)
        flag = jnp.where(dl * dl + dr * dr < float(RADIUS * RADIUS), 1.0, 0.0)
        upto = jnp.dot(
            jnp.broadcast_to(flag, (16, BATCH)).astype(BF16), upper, preferred_element_type=F32
        )[0:1]
        return jnp.where(flag > 0.0, upto - 1.0, -float(NOBS)), jnp.sum(flag)

    number = lax.broadcasted_iota(jnp.int32, (SLOTS, BATCH), 0).astype(F32)
    lane = lax.broadcasted_iota(jnp.int32, (1, SLOTS), 1).astype(F32)
    row = lax.broadcasted_iota(jnp.int32, (SHARE, SLOTS), 0).astype(F32)

    def hot(slot, shift):
        return jnp.where(slot == number + shift, 1.0, 0.0).astype(BF16)

    def spot(b, h):
        both = jnp.concatenate(
            [jnp.broadcast_to(rel[b], (8, BATCH)), jnp.broadcast_to(lat[b], (8, BATCH))], axis=0
        )
        high, low = split(both)
        got = dot_nt(high, h) + dot_nt(low, h)
        return got[0:1], got[8:9]

    def placed(lon, up, used):
        gap = row - up
        base = jnp.where(lane < used, 1.0 - gap * gap * SCALE, -1.0)
        return jnp.concatenate([base, jnp.broadcast_to(lon, (8, SLOTS))], axis=0)

    sp1, sp2 = split(root1 * scaled1), split(root1 * root2 * scaled2)
    shift1 = jnp.sum(inc1, axis=0, keepdims=True) * (1.0 / MEMBERS)
    free1 = inc1 - shift1
    g1, g2 = split(root2 * free1 + shift1), split(inc2)
    f1, s2 = split(free1), split(root2 * scaled2)
    full = jnp.float32(0.0)
    for q, (lo, hi) in enumerate(((0.0, CUT - 1.0), (float(CUT), WIDTH - 1.0))):
        slot1, n1 = near(0, lo, hi)
        slot2, n2 = near(1, lo, hi)
        full = jnp.maximum(full, n1 + n2)
        h1, h2 = hot(slot1, 0.0), hot(slot2, -n1)
        lead[q] = paired(*[dot_nt(a, h1) + dot_nt(b, h2) for a, b in zip(sp1, sp2)])
        gain[q] = paired(*[dot_nt(h1, a) + dot_nt(h2, b) for a, b in zip(g1, g2)])
        one = dot_nt(h1, f1[0]) + dot_nt(h1, f1[1])
        two = dot_nt(h2, s2[0]) + dot_nt(h2, s2[1])
        link[q] = paired(*split(exact(one, two, ((1,), (1,)))))
        (lon1, lat1), (lon2, lat2) = spot(0, h1), spot(1, h2)
        where[q] = placed(lon1 + lon2, lat1 + lat2, n1 + n2)
    counts[0] = jnp.where(full > SLOTS, 1, 0)

    @pl.when(full > SLOTS)
    def _():
        for b, (sp, g) in enumerate(((split(scaled1), split(inc1)), (split(scaled2), g2))):
            slot, n = near(b, 0.0, WIDTH - 1.0)
            counts[1 + b] = (n.astype(jnp.int32) + SLOTS - 1) // SLOTS
            for c in range(CHUNKS):
                h = hot(slot, float(c * SLOTS))
                many_lead[b, c] = paired(dot_nt(sp[0], h), dot_nt(sp[1], h))
                many_gain[b, c] = paired(dot_nt(h, g[0]), dot_nt(h, g[1]))
                lon, up = spot(b, h)
                many_where[b, c] = placed(lon, up, n - float(c * SLOTS))


def filter_obs(place, priors, facts):
    square = (2 * SLOTS, 2 * MEMBERS)
    return pl.pallas_call(
        filter_kernel,
        out_shape=[jax.ShapeDtypeStruct((2,) + square, BF16)] * 3
        + [jax.ShapeDtypeStruct((2, SHARE + 8, SLOTS), F32)]
        + [jax.ShapeDtypeStruct((2, CHUNKS) + square, BF16)] * 2
        + [jax.ShapeDtypeStruct((2, CHUNKS, SHARE + 8, SLOTS), F32)]
        + [jax.ShapeDtypeStruct((3,), jnp.int32), jax.ShapeDtypeStruct((2,), F32)],
        in_specs=[SMEM, VMEM, VMEM],
        out_specs=[VMEM] * 7 + [SMEM] * 2,
        scratch_shapes=[pltpu.VMEM((MEMBERS, NOBS), F32)],
        compiler_params=PARAMS,
        name="filter_observations",
    )(place, priors, facts)


def gather_members(tiles, lane):
    v = list(tiles)
    for k in range(3):
        s = SHARE << k
        low = ((lane >> (4 + k)) & 1) == 0
        w = list(v)
        for i in range(8):
            if i & (1 << k):
                continue
            j = i | (1 << k)
            w[i] = jnp.where(low, v[i], pltpu.roll(v[j], s, 1))
            w[j] = jnp.where(low, pltpu.roll(v[i], LAT - s, 1), v[j])
        v = w
    return v


def regress_kernel(
    counts, roots, lead, link, gain, where, many_lead, many_gain, many_where, parts, out, state, made, big, sems
):
    load = pltpu.make_async_copy(parts, state, sems.at[0])
    load.start()
    lane = lax.broadcasted_iota(jnp.int32, (SHARE, LAT), 1)
    load.wait()

    def fetch(g):
        return gather_members([state[s, g] for s in range(8)], lane)

    def matrices(a):
        return jnp.concatenate(split(a), axis=1)

    def product(a, m):
        got = jnp.dot(matrices(a), m, preferred_element_type=F32)
        return got[:, :MEMBERS] + got[:, MEMBERS:]

    def taper(spots, lons):
        base, at = spots[0:SHARE], spots[SHARE : SHARE + 1]
        tiles = []
        for lon in lons:
            gap = at - lon
            t = jnp.maximum(base - gap * gap * SCALE, 0.0)
            tiles.append(t * t)
        return jnp.concatenate(tiles, axis=0)

    def centre(x):
        mean = jnp.sum(x, axis=1, keepdims=True) * (1.0 / MEMBERS)
        return mean, x - mean

    def short(x, lons, q):
        mean, anomaly = centre(x)
        cov = product(anomaly, lead[q])
        t = taper(where[q], lons)
        cov = cov + product(t * cov, link[q])
        return (mean + roots[0] * roots[1] * anomaly) + product(t * cov, gain[q])

    def block(groups, q):
        tiles, lons = [], []
        for g, at in groups:
            tiles += fetch(g)
            lons += [at + j for j in range(8)] if len(groups) > 0 and at is not None else []
        return jnp.concatenate(tiles, axis=0), lons

    def put(f, lon, x, n):
        made[f, pl.ds(lon, n)] = x.reshape(n, SHARE, MEMBERS)

    @pl.when(counts[0] == 0)
    def _():
        def field(f, _):
            for q, lo, n in ((0, 0, 5), (1, 5, 4)):
                groups = [(f * INNER + lo + i, 8.0 * (lo + i + 1)) for i in range(n)]
                x, lons = block(groups, q)
                put(f, 8 * (lo + 1), short(x, lons, q), 8 * n)
            for q, lon in ((0, 0), (1, RIGHT)):
                x, lons = block([(INSIDE + 2 * f + q, float(lon))], q)
                put(f, lon, short(x, lons, q), 8)
            return 0

        lax.fori_loop(0, FIELDS, field, 0)
        tail = [float(RIGHT + 8 + j % 2) for j in range(8)]
        x = short(jnp.concatenate(fetch(GROUPS - 2), axis=0), tail, 1)
        for f in range(4):
            put(f, RIGHT + 8, x[f * 2 * SHARE : (f + 1) * 2 * SHARE], 2)
        x = short(jnp.concatenate(fetch(GROUPS - 1)[:2], axis=0), tail[:2], 1)
        put(4, RIGHT + 8, x, 2)

    @pl.when(counts[0] != 0)
    def _():
        lons_of = [
            (f * INNER + i, f, 8 * (i + 1)) for f in range(FIELDS) for i in range(INNER)
        ]

        def long(x, lons):
            for b in range(2):
                mean, anomaly = centre(x)
                anomaly = roots[b] * anomaly
                big[pl.ds(0, x.shape[0]), :] = mean + anomaly

                def chunk(c, _):
                    t = taper(many_where[b, c], lons)
                    w = t * product(anomaly, many_lead[b, c])
                    big[pl.ds(0, x.shape[0]), :] += product(w, many_gain[b, c])
                    return 0

                lax.fori_loop(0, counts[1 + b], chunk, 0)
                x = big[pl.ds(0, x.shape[0]), :]
            return x

        def each(g, _):
            inside = g < INSIDE
            h = g - INSIDE
            f = jnp.where(inside, g // INNER, h // 2)
            lon = jnp.where(inside, 8 * (g % INNER + 1), RIGHT * (h % 2))
            at = lon.astype(F32)
            x = jnp.concatenate(fetch(g), axis=0)
            put(f, lon, long(x, [at + j for j in range(8)]), 8)
            return 0

        lax.fori_loop(0, GROUPS - 2, each, 0)
        tail = [float(RIGHT + 8 + j % 2) for j in range(8)]
        x = long(jnp.concatenate(fetch(GROUPS - 2), axis=0), tail)
        for f in range(4):
            put(f, RIGHT + 8, x[f * 2 * SHARE : (f + 1) * 2 * SHARE], 2)
        x = long(jnp.concatenate(fetch(GROUPS - 1)[:2], axis=0), tail[:2])
        put(4, RIGHT + 8, x, 2)

    store = pltpu.make_async_copy(made, out, sems.at[0])
    store.start()
    store.wait()


def regress(tables, parts):
    *tables, counts, roots = tables
    return pl.pallas_call(
        regress_kernel,
        out_shape=jax.ShapeDtypeStruct((FIELDS, WIDTH, SHARE, MEMBERS), F32),
        in_specs=[SMEM] * 2 + [VMEM] * 7 + [ANY],
        out_specs=ANY,
        scratch_shapes=[
            pltpu.VMEM((BANDS, GROUPS, SHARE, LAT), F32),
            pltpu.VMEM((FIELDS, WIDTH, SHARE, MEMBERS), F32),
            pltpu.VMEM((8 * SHARE, MEMBERS), F32),
            pltpu.SemaphoreType.DMA((1,)),
        ],
        compiler_params=PARAMS,
        name="regress_state",
    )(counts, roots, *tables, parts)


def across(x, axis, bits):
    count = lax.axis_size(axis)
    return lax.ppermute(x, axis, [(i, i ^ bits) for i in range(count)])


def shards(
    ensemble,
    ocean_depth,
    planetary_vorticity,
    land_mask,
    obs_values,
    obs_error,
    obs_lon,
    obs_lat,
    obs_field,
    obs_order,
):
    member, sector = lax.axis_index("member"), lax.axis_index("sector")
    sectors = lax.axis_size("sector")
    vort = planetary_vorticity.reshape(1, LAT)
    ens = jnp.transpose(ensemble, (1, 2, 0, 3))
    west_side, east_side = edges(ens, ocean_depth, land_mask)
    left = lax.ppermute(east_side, "sector", [(i, (i + 1) % sectors) for i in range(sectors)])
    right = lax.ppermute(west_side, "sector", [((i + 1) % sectors, i) for i in range(sectors)])

    lon_f, lat_f = obs_lon.astype(F32), obs_lat.astype(F32)
    facts = in_order(
        obs_order, jnp.stack([lon_f, lat_f, obs_values, obs_error] + [jnp.zeros_like(lon_f)] * 4)
    )
    west = sector * WIDTH
    here = obs_lon - west
    cell = ((obs_field - 2) * WIDTH + here) * LAT + obs_lat
    own, count = own_list(obs_order, jnp.where((here >= 0) & (here < WIDTH), cell, -1))

    messages, seen = forecast_inner(ens, ocean_depth, land_mask, vort)
    messages, seen = forecast_outer(
        ens, left, right, ocean_depth, land_mask, vort, messages, seen
    )
    parts = lax.all_to_all(messages, "member", split_axis=0, concat_axis=0, tiled=True)

    priors = pick(own, count, seen.reshape(3 * WIDTH, SHARE, LAT))
    for k in range(4):
        priors = priors + across(priors, "sector", 1 << k)
    priors = priors[None]
    for k in range(3):
        priors = jnp.concatenate([priors, across(priors, "member", 1 << k)])
    place = jnp.stack([west, member * SHARE, member])
    analysis = regress(filter_obs(place, priors, facts), parts)
    return jnp.transpose(analysis, (0, 2, 1, 3))


def solution(mesh):
    placed = (
        P("member", None, "sector", None),
        P("sector", None),
        P(),
        P("sector", None),
        P(),
        P(),
        P(),
        P(),
        P(),
        P(),
    )
    return jax.shard_map(
        shards,
        mesh=mesh,
        in_specs=placed,
        out_specs=P(None, "member", "sector", None),
        check_vma=False,
    )
```

profile of v0, /device:TPU:8, one launch (start us, length us, event | category | flops | bytes accessed | tf_op | source)
XLA Modules:
  0.0 133.4 jit_solution(4384809208655565543)
XLA Ops:
  0.0 2.6 %pack_edges.1 = (f32[6,4,16,128]{3,2,1,0:T(8,128)}, f32[6,4,16,128]{3,2,1,0:T(8,128)}) custom-call(f32[5,90,16,128]{3,2,1,0:T(8,128)} %bitcast.14, f32[90,128]{1,0:T(8,128)} %depth.5, s32[90,128]{1,0:T(8,128)} %mask.5), custom_call_target="tpu_custom_call" | custom-call | tf_op jit(solution)/shard_map/pack_edges/pallas_call | solution.py:55
  2.6 0.1 collective-permute-start
  2.7 1.7 %collective-permute-start.1 = (f32[6,4,16,128]{3,2,1,0:T(8,128)}, f32[6,4,16,128]{3,2,1,0:T(8,128)S(1)}, u32[]{:S(2)}, u32[]{:S(2)}) collective-permute-start(f32[6,4,16,128]{3,2,1,0:T(8,128)} %get-tuple-element.25), channel_id=1, source_target_pairs={{1,0},{2,1},{3,2},{4,3},{5,4},{6,5},{7,6},{8,7},{9,8},{10,9},{11,1... | collective-permute-start | bytes 589832 | tf_op jit(solution)/shard_map/ppermute | solution.py:649
  4.4 12.7 %forecast_inner.1 = (f32[8,57,16,128]{3,2,1,0:T(8,128)}, f32[3,90,16,128]{3,2,1,0:T(8,128)}) custom-call(f32[5,90,16,128]{3,2,1,0:T(8,128)} %bitcast.15, f32[90,128]{1,0:T(8,128)} %depth.5, s32[90,128]{1,0:T(8,128)} %mask.5, f32[1,128]{1,0:T(1,128)} %bitcast.23), custom_call_target="tpu_custom_call" | custom-call | tf_op jit(solution)/shard_map/forecast_inner/pallas_call | solution.py:141
  17.1 0.6 copy-done
  17.8 0.1 copy-done.1
  17.8 6.2 %forecast_outer.1 = (f32[8,57,16,128]{3,2,1,0:T(8,128)}, f32[3,90,16,128]{3,2,1,0:T(8,128)}) custom-call(f32[5,90,16,128]{3,2,1,0:T(8,128)} %bitcast.16, f32[6,4,16,128]{3,2,1,0:T(8,128)} %copy-done, f32[6,4,16,128]{3,2,1,0:T(8,128)} %copy-done.1, f32[90,128]{1,0:T(8,128)} %depth.5, s32[90,128]{1,0:T(8,128)} %mask.5, ...), custom_call_target="tpu_custom_call", output_to_operand_aliasing={{0}: (6, {}), {1}: (7, {})} | custom-call | tf_op jit(solution)/shard_map/forecast_outer/pallas_call | solution.py:220
  24.1 0.0 copy-start.2
  24.1 7.8 %all-to-all-start = ((f32[8,57,16,128]{3,2,1,0:T(8,128)}), f32[8,57,16,128]{3,2,1,0:T(8,128)}, u32[]{:S(2)}, u32[]{:S(2)}) async-start(f32[8,57,16,128]{3,2,1,0:T(8,128)} %get-tuple-element.38), calls=%async_computation | async-start | bytes 7471104 | tf_op jit(solution)/shard_map/all_to_all | solution.py:664
  31.9 0.6 fusion
  32.5 5.0 %own_observations.1 = (s32[1152]{0:T(1024)}, s32[1]{0:T(128)}) custom-call(s32[1024]{0:T(1024)} %order.1, s32[1024]{0:T(1024)} %get-tuple-element.40.cell), custom_call_target="tpu_custom_call" | custom-call | tf_op jit(solution)/shard_map/own_observations/pallas_call | solution.py:253
  37.5 8.1 %pick_priors.1 = f32[8,16,128]{2,1,0:T(8,128)} custom-call(s32[1152]{0:T(1024)} %get-tuple-element.22.own, s32[1]{0:T(128)} %get-tuple-element.23.count, f32[270,16,128]{2,1,0:T(8,128)} %bitcast.17), custom_call_target="tpu_custom_call" | custom-call | tf_op jit(solution)/shard_map/pick_priors/pallas_call | solution.py:282
  45.6 1.5 %collective-permute-done.2 = f32[8,16,128]{2,1,0:T(8,128)S(1)} collective-permute-done((f32[8,16,128]{2,1,0:T(8,128)}, f32[8,16,128]{2,1,0:T(8,128)S(1)}, u32[]{:S(2)}, u32[]{:S(2)}) %collective-permute-start.2) | collective-permute-done | bytes 65568 | tf_op jit(solution)/shard_map/ppermute | solution.py:628
  47.1 0.9 add.21
  47.9 2.5 %collective-permute-start.3 = (f32[8,16,128]{2,1,0:T(8,128)S(1)}, f32[8,16,128]{2,1,0:T(8,128)S(1)}, u32[]{:S(2)}, u32[]{:S(2)}) collective-permute-start(f32[8,16,128]{2,1,0:T(8,128)S(1)} %add.21), channel_id=1, source_target_pairs={{0,2},{1,3},{2,0},{3,1},{4,6},{5,7},{6,4},{7,5},{8,10},{9,11},{10,... | collective-permute-start | bytes 196616 | tf_op jit(solution)/shard_map/ppermute | solution.py:628
  50.4 2.4 %collective-permute-done.3 = f32[8,16,128]{2,1,0:T(8,128)S(1)} collective-permute-done((f32[8,16,128]{2,1,0:T(8,128)S(1)}, f32[8,16,128]{2,1,0:T(8,128)S(1)}, u32[]{:S(2)}, u32[]{:S(2)}) %collective-permute-start.3) | collective-permute-done | bytes 65568 | tf_op jit(solution)/shard_map/ppermute | solution.py:628
  52.8 1.0 collective-permute-start.4
  53.8 4.8 %collective-permute-done.4 = f32[8,16,128]{2,1,0:T(8,128)S(1)} collective-permute-done((f32[8,16,128]{2,1,0:T(8,128)S(1)}, f32[8,16,128]{2,1,0:T(8,128)S(1)}, u32[]{:S(2)}, u32[]{:S(2)}) %collective-permute-start.4) | collective-permute-done | bytes 65568 | tf_op jit(solution)/shard_map/ppermute | solution.py:628
  58.7 1.5 %collective-permute-start.5 = (f32[8,16,128]{2,1,0:T(8,128)S(1)}, f32[8,16,128]{2,1,0:T(8,128)S(1)}, u32[]{:S(2)}, u32[]{:S(2)}) collective-permute-start(f32[8,16,128]{2,1,0:T(8,128)S(1)} %add.23), channel_id=1, source_target_pairs={{0,8},{1,9},{2,10},{3,11},{4,12},{5,13},{6,14},{7,15},{8,0},{9,1},... | collective-permute-start | bytes 196616 | tf_op jit(solution)/shard_map/ppermute | solution.py:628
  60.2 5.6 %collective-permute-done.5 = f32[8,16,128]{2,1,0:T(8,128)S(1)} collective-permute-done((f32[8,16,128]{2,1,0:T(8,128)S(1)}, f32[8,16,128]{2,1,0:T(8,128)S(1)}, u32[]{:S(2)}, u32[]{:S(2)}) %collective-permute-start.5) | collective-permute-done | bytes 65568 | tf_op jit(solution)/shard_map/ppermute | solution.py:628
  65.8 12.0 %collective-permute-start.6 = (f32[1,8,16,128]{3,2,1,0:T(8,128)S(1)}, f32[1,8,16,128]{3,2,1,0:T(8,128)S(1)}, u32[]{:S(2)}, u32[]{:S(2)}) collective-permute-start(f32[1,8,16,128]{3,2,1,0:T(8,128)S(1)} %add_bitcast_fusion), channel_id=1, source_target_pairs={{0,16},{16,0},{32,48},{48,32},{64,80},{80,64},{96,112},{112,96},{1... | collective-permute-start | bytes 196616 | tf_op jit(solution)/shard_map/ppermute | solution.py:628
  77.8 11.2 %collective-permute-done.6 = f32[1,8,16,128]{3,2,1,0:T(8,128)S(1)} collective-permute-done((f32[1,8,16,128]{3,2,1,0:T(8,128)S(1)}, f32[1,8,16,128]{3,2,1,0:T(8,128)S(1)}, u32[]{:S(2)}, u32[]{:S(2)}) %collective-permute-start.6) | collective-permute-done | bytes 65568 | tf_op jit(solution)/shard_map/ppermute | solution.py:628
  89.0 0.1 collective-permute-start.7
  89.1 6.5 %collective-permute-done.7 = f32[2,8,16,128]{3,2,1,0:T(8,128)S(1)} collective-permute-done((f32[2,8,16,128]{3,2,1,0:T(8,128)S(1)}, f32[2,8,16,128]{3,2,1,0:T(8,128)S(1)}, u32[]{:S(2)}, u32[]{:S(2)}) %collective-permute-start.7) | collective-permute-done | bytes 131104 | tf_op jit(solution)/shard_map/ppermute | solution.py:628
  95.6 3.0 %collective-permute-start.8 = (f32[4,8,16,128]{3,2,1,0:T(8,128)S(1)}, f32[4,8,16,128]{3,2,1,0:T(8,128)S(1)}, u32[]{:S(2)}, u32[]{:S(2)}) collective-permute-start(f32[4,8,16,128]{3,2,1,0:T(8,128)S(1)} %pad_maximum_fusion.1), channel_id=1, source_target_pairs={{0,64},{16,80},{32,96},{48,112},{64,0},{80,16},{96,32},{112,48},{1... | collective-permute-start | bytes 786440 | tf_op jit(solution)/shard_map/ppermute | solution.py:628
  98.6 0.7 stack.39.facts
  99.3 2.8 %obs_in_batch_order.1.facts = f32[8,8,128]{2,1,0:T(8,128)} custom-call(s32[8,1,128]{2,1,0:T(1,128)} %bitcast.20, f32[8,1024]{1,0:T(8,128)} %stack.39.facts), custom_call_target="tpu_custom_call" | custom-call | tf_op jit(solution)/shard_map/obs_in_batch_order/pallas_call | solution.py:315
  102.0 0.7 pad_add_fusion.place
  102.7 0.8 collective-permute-done.8
  103.5 0.8 pad_maximum_fusion.priors
  104.4 7.1 %filter_observations.1 = (bf16[2,256,256]{2,1,0:T(8,128)(2,1)}, bf16[2,256,256]{2,1,0:T(8,128)(2,1)}, bf16[2,256,256]{2,1,0:T(8,128)(2,1)}, f32[2,24,128]{2,1,0:...) custom-call(s32[3]{0:T(128)} %pad_add_fusion.place, ...), custom_call_target="tpu_custom_call" | custom-call | tf_op jit(solution)/shard_map/filter_observations/pallas_call | solution.py:464
  111.4 21.8 %regress_state.1 = f32[5,90,16,128]{3,2,1,0:T(8,128)} custom-call(s32[3]{0:T(128)} %get-tuple-element.29.counts, f32[2]{0:T(128)} %get-tuple-element.30.roots, bf16[2,256,256]{2,1,0:T(8,128)(2,1)} %get-tuple-element.31.lead, bf16[2,256,256]{2,1,0:T(8,128)(2,1)} %get-tuple-element.32.link, bf16[2,256,256]{2,1,0:T(8,128)(2,1)} %get-tuple-element.33.gain, ...), custom_call_target="tpu_custom_call" | custom-call | tf_op jit(solution)/shard_map/regress_state/pallas_call | solution.py:610
  (21 shorter events, 0.1 us)
Async XLA Ops:
  2.6 14.5 %collective-permute-start = (f32[6,4,16,128]{3,2,1,0:T(8,128)}, f32[6,4,16,128]{3,2,1,0:T(8,128)S(1)}, u32[]{:S(2)}, u32[]{:S(2)}) collective-permute-start(f32[6,4,16,128]{3,2,1,0:T(8,128)} %get-tuple-element.24), channel_id=1, source_target_pairs={{0,1},{1,2},{2,3},{3,4},{4,5},{5,6},{6,7},{7,8},{8,9},{9,10},{10,1... | collective-permute-start | bytes 589832 | tf_op jit(solution)/shard_map/ppermute | solution.py:648
  2.7 14.4 %collective-permute-start.1 = (f32[6,4,16,128]{3,2,1,0:T(8,128)}, f32[6,4,16,128]{3,2,1,0:T(8,128)S(1)}, u32[]{:S(2)}, u32[]{:S(2)}) collective-permute-start(f32[6,4,16,128]{3,2,1,0:T(8,128)} %get-tuple-element.25), channel_id=1, source_target_pairs={{1,0},{2,1},{3,2},{4,3},{5,4},{6,5},{7,6},{8,7},{9,8},{10,9},{11,1... | collective-permute-start | bytes 589832 | tf_op jit(solution)/shard_map/ppermute | solution.py:649
  17.1 0.7 copy-start
  17.1 0.7 copy-start.1
  24.1 7.8 %copy-start.2 = (s32[1024]{0:T(1024)S(1)}, s32[1024]{0:T(1024)}, u32[]{:S(2)}) copy-start(s32[1024]{0:T(1024)} %param.17) | copy-start | bytes 12292
  24.1 7.8 %copy-start.3 = (s32[1024]{0:T(1024)S(1)}, s32[1024]{0:T(1024)}, u32[]{:S(2)}) copy-start(s32[1024]{0:T(1024)} %param.18) | copy-start | bytes 12292
  24.1 7.8 %copy-start.4 = (s32[1024]{0:T(1024)S(1)}, s32[1024]{0:T(1024)}, u32[]{:S(2)}) copy-start(s32[1024]{0:T(1024)} %param.16) | copy-start | bytes 12292
  24.1 87.3 %all-to-all-start = ((f32[8,57,16,128]{3,2,1,0:T(8,128)}), f32[8,57,16,128]{3,2,1,0:T(8,128)}, u32[]{:S(2)}, u32[]{:S(2)}) async-start(f32[8,57,16,128]{3,2,1,0:T(8,128)} %get-tuple-element.38), calls=%async_computation | async-start | bytes 7471104 | tf_op jit(solution)/shard_map/all_to_all | solution.py:664
  31.9 66.8 %copy-start.5 = (f32[1024]{0:T(1024)S(1)}, f32[1024]{0:T(1024)}, u32[]{:S(2)}) copy-start(f32[1024]{0:T(1024)} %param.14) | copy-start | bytes 12292
  31.9 66.8 %copy-start.6 = (f32[1024]{0:T(1024)S(1)}, f32[1024]{0:T(1024)}, u32[]{:S(2)}) copy-start(f32[1024]{0:T(1024)} %param.15) | copy-start | bytes 12292
  45.6 1.5 %collective-permute-start.2 = (f32[8,16,128]{2,1,0:T(8,128)}, f32[8,16,128]{2,1,0:T(8,128)S(1)}, u32[]{:S(2)}, u32[]{:S(2)}) collective-permute-start(f32[8,16,128]{2,1,0:T(8,128)} %pick_priors.1), channel_id=1, source_target_pairs={{0,1},{1,0},{2,3},{3,2},{4,5},{5,4},{6,7},{7,6},{8,9},{9,8},{10,11... | collective-permute-start | bytes 196616 | tf_op jit(solution)/shard_map/ppermute | solution.py:628
  47.9 4.9 %collective-permute-start.3 = (f32[8,16,128]{2,1,0:T(8,128)S(1)}, f32[8,16,128]{2,1,0:T(8,128)S(1)}, u32[]{:S(2)}, u32[]{:S(2)}) collective-permute-start(f32[8,16,128]{2,1,0:T(8,128)S(1)} %add.21), channel_id=1, source_target_pairs={{0,2},{1,3},{2,0},{3,1},{4,6},{5,7},{6,4},{7,5},{8,10},{9,11},{10,... | collective-permute-start | bytes 196616 | tf_op jit(solution)/shard_map/ppermute | solution.py:628
  52.8 5.8 %collective-permute-start.4 = (f32[8,16,128]{2,1,0:T(8,128)S(1)}, f32[8,16,128]{2,1,0:T(8,128)S(1)}, u32[]{:S(2)}, u32[]{:S(2)}) collective-permute-start(f32[8,16,128]{2,1,0:T(8,128)S(1)} %add.22), channel_id=1, source_target_pairs={{0,4},{1,5},{2,6},{3,7},{4,0},{5,1},{6,2},{7,3},{8,12},{9,13},{10,... | collective-permute-start | bytes 196616 | tf_op jit(solution)/shard_map/ppermute | solution.py:628
  58.7 7.1 %collective-permute-start.5 = (f32[8,16,128]{2,1,0:T(8,128)S(1)}, f32[8,16,128]{2,1,0:T(8,128)S(1)}, u32[]{:S(2)}, u32[]{:S(2)}) collective-permute-start(f32[8,16,128]{2,1,0:T(8,128)S(1)} %add.23), channel_id=1, source_target_pairs={{0,8},{1,9},{2,10},{3,11},{4,12},{5,13},{6,14},{7,15},{8,0},{9,1},... | collective-permute-start | bytes 196616 | tf_op jit(solution)/shard_map/ppermute | solution.py:628
  65.8 23.2 %collective-permute-start.6 = (f32[1,8,16,128]{3,2,1,0:T(8,128)S(1)}, f32[1,8,16,128]{3,2,1,0:T(8,128)S(1)}, u32[]{:S(2)}, u32[]{:S(2)}) collective-permute-start(f32[1,8,16,128]{3,2,1,0:T(8,128)S(1)} %add_bitcast_fusion), channel_id=1, source_target_pairs={{0,16},{16,0},{32,48},{48,32},{64,80},{80,64},{96,112},{112,96},{1... | collective-permute-start | bytes 196616 | tf_op jit(solution)/shard_map/ppermute | solution.py:628
  89.0 6.6 %collective-permute-start.7 = (f32[2,8,16,128]{3,2,1,0:T(8,128)S(1)}, f32[2,8,16,128]{3,2,1,0:T(8,128)S(1)}, u32[]{:S(2)}, u32[]{:S(2)}) collective-permute-start(f32[2,8,16,128]{3,2,1,0:T(8,128)S(1)} %pad_maximum_fusion.2), channel_id=1, source_target_pairs={{0,32},{16,48},{32,0},{48,16},{64,96},{80,112},{96,64},{112,80},{1... | collective-permute-start | bytes 393224 | tf_op jit(solution)/shard_map/ppermute | solution.py:628
  95.6 8.0 %collective-permute-start.8 = (f32[4,8,16,128]{3,2,1,0:T(8,128)S(1)}, f32[4,8,16,128]{3,2,1,0:T(8,128)S(1)}, u32[]{:S(2)}, u32[]{:S(2)}) collective-permute-start(f32[4,8,16,128]{3,2,1,0:T(8,128)S(1)} %pad_maximum_fusion.1), channel_id=1, source_target_pairs={{0,64},{16,80},{32,96},{48,112},{64,0},{80,16},{96,32},{112,48},{1... | collective-permute-start | bytes 786440 | tf_op jit(solution)/shard_map/ppermute | solution.py:628
where the time goes:
time: 134 us; the launch traced here: 133 us
  Pallas kernels  66.2 us (49%)
  waiting for transfers between devices  32.9 us (25%)
  starting transfers between devices  29.6 us (22%)
  other arithmetic  3.02 us (2%)
  local copies, waits for them, and re-layouts  1.4 us (1%)
    ppermute x7, waiting for transfers between devices, across(): return lax.ppermute(x, axis, [(i, i ^ bits) for i in range(count)])  32.9 us
    pallas_call x1, Pallas kernels, regress(): pl.pallas_call(regress_kernel, out_shape=jax.ShapeDtypeStruct((FIELDS, WI...  21.8 us
    ppermute x7, starting transfers between devices, across(): return lax.ppermute(x, axis, [(i, i ^ bits) for i in range(count)])  20.1 us
    pallas_call x1, Pallas kernels, forecast_inner(): pl.pallas_call(inner_kernel, out_shape=[jax.ShapeDtypeStruct((BANDS, GROU...  12.7 us
    pallas_call x1, Pallas kernels, pick(): pl.pallas_call(pick_kernel, out_shape=jax.ShapeDtypeStruct((BLOCKS, SHARE...  8.1 us
    all_to_all x1, starting transfers between devices, shards(): lax.all_to_all(messages, 'member', split_axis=0, concat_axis=0, tiled=True)  7.76 us
    pallas_call x1, Pallas kernels, filter_obs(): pl.pallas_call(filter_kernel, out_shape=[jax.ShapeDtypeStruct((2,) + squa...  7.05 us
    pallas_call x1, Pallas kernels, forecast_outer(): pl.pallas_call(outer_kernel, out_shape=[jax.ShapeDtypeStruct(messages.sha...  6.22 us
  transfers between devices with their start and end apart: 10, of which 7 were waited for; matrix products, arithmetic and copies ran while one was open for 3% of the time, Pallas kernels for 27%

commit v1 on v0

--- a/solution.py
+++ b/solution.py
@@ -22,10 +22,11 @@
 INSIDE = FIELDS * INNER
 OUTSIDE = 2 * FIELDS + 2
 GROUPS = INSIDE + OUTSIDE
-EDGE_ROWS = FIELDS * EDGE * SHARE
+SETS = (GROUPS + 7) // 8
 CUT = 48
 SLOTS = 128
 CHUNKS = BATCH // SLOTS
+FLOW, REST = 39, 38
 SCALE = 1.0 / (RADIUS * RADIUS)
 F32 = jnp.float32
 BF16 = jnp.bfloat16
@@ -63,45 +64,68 @@
     )(ens, depth, mask)
 
 
-def stepper(dep, sea, vort, flux):
-    lane = lax.broadcasted_iota(jnp.int32, (SHARE, LAT), 1)
-    first, last = lane == 0, lane == LAT - 1
+def split(a):
+    high = a.astype(BF16)
+    return high, (a - high.astype(F32)).astype(BF16)
+
+
+def bands(out):
+    row = lax.broadcasted_iota(jnp.int32, (2 * LAT, 2 * LAT), 0) % LAT
+    col = lax.broadcasted_iota(jnp.int32, (2 * LAT, 2 * LAT), 1)
+    gap = row - col % LAT
+    value = jnp.where(jnp.abs(gap) == 1, jnp.where(col < LAT, gap, 1), 0)
+    out[...] = value.astype(F32).astype(BF16)
+
+
+def stepper(dep, sea, vort, flux, band):
     spin = jnp.broadcast_to(vort[...], (SHARE, LAT))
 
-    def north(a):
-        return jnp.where(last, 0.0, pltpu.roll(a, LAT - 1, 1))
-
-    def south(a):
-        return jnp.where(first, 0.0, pltpu.roll(a, 1, 1))
-
-    def step(src, dst, lo, hi, row, unroll):
-        def flow(e, _):
-            u, v, h = src[0, e], src[1, e], src[2, e]
-            m = sea[pl.ds(e + row, 1), :]
+    def halves(tiles):
+        return jnp.concatenate(split(jnp.concatenate(tiles, axis=0)), axis=1)
+
+    def difference(tiles):
+        got = jnp.dot(halves(tiles), band[:, 0:LAT], preferred_element_type=F32)
+        return [got[i * SHARE : (i + 1) * SHARE] for i in range(len(tiles))]
+
+    def both(tiles):
+        got = jnp.dot(halves(tiles), band[...], preferred_element_type=F32)
+        rows = [got[i * SHARE : (i + 1) * SHARE] for i in range(len(tiles))]
+        return [r[:, 0:LAT] for r in rows], [r[:, LAT:] for r in rows]
+
+    def flow(src, dst, places):
+        slope = difference([src[2, e] for e, _ in places])
+        for (e, row), dh in zip(places, slope):
+            u, v = src[0, e], src[1, e]
+            m = sea[pl.ds(row, 1), :]
             un = m * (u + spin * v - 0.15 * (src[2, e + 1] - src[2, e - 1]))
             dst[0, e] = un
-            dst[1, e] = m * (v - spin * u - 0.15 * (north(h) - south(h)))
-            flux[e] = dep[pl.ds(e + row, 1), :] * un
-            return 0
-
-        def others(e, _):
-            un, vn = dst[0, e], dst[1, e]
-            dv = dep[pl.ds(e + row, 1), :] * vn
-            dst[2, e] = src[2, e] - 0.15 * (flux[e + 1] - flux[e - 1] + (north(dv) - south(dv)))
-            for c in (3, 4):
+            dst[1, e] = m * (v - spin * u - 0.15 * dh)
+            flux[e] = dep[pl.ds(row, 1), :] * un
+
+    def others(src, dst, places):
+        slope = difference([dep[pl.ds(row, 1), :] * dst[1, e] for e, row in places])
+        for (e, _), dv in zip(places, slope):
+            dst[2, e] = src[2, e] - 0.15 * (flux[e + 1] - flux[e - 1] + dv)
+        for c in (3, 4):
+            slope, total = both([src[c, e] for e, _ in places])
+            for (e, _), dc, around in zip(places, slope, total):
                 a, ae, aw = src[c, e], src[c, e + 1], src[c, e - 1]
-                an, ao = north(a), south(a)
                 dst[c, e] = (
                     a
-                    - 0.15 * (un * (ae - aw) + vn * (an - ao))
-                    + 0.1 * (((ae + aw) + (an + ao)) - 4.0 * a)
+                    - 0.15 * (dst[0, e] * (ae - aw) + dst[1, e] * dc)
+                    + 0.1 * (((ae + aw) + around) - 4.0 * a)
                 )
-            return 0
-
-        lax.fori_loop(lo, hi, flow, 0, unroll=2 * unroll)
-        lax.fori_loop(lo + 1, hi - 1, others, 0, unroll=unroll)
-
-    return step
+
+    return flow, others
+
+
+def in_blocks(stage, src, dst, lo, hi, row, n):
+    def block(i, _):
+        e = jnp.minimum(lo + i * n, hi - n)
+        stage(src, dst, [(e + k, e + k + row) for k in range(n)])
+        return 0
+
+    lax.fori_loop(0, (hi - lo + n - 1) // n, block, 0)
 
 
 def turn(tiles, out, g):
@@ -110,15 +134,18 @@
         out[b, g] = tile[b * SHARE : (b + 1) * SHARE]
 
 
-def inner_kernel(ens, depth, mask, vort, out, seen, now, nxt, flux, sea, made, sems):
+def inner_kernel(ens, depth, mask, vort, out, seen, now, nxt, flux, sea, band, made, sems):
     span = INNER * 8
     load = pltpu.make_async_copy(ens.at[:, pl.ds(EDGE, span + 2 * EDGE)], now, sems.at[0])
     load.start()
     sea[...] = mask[...].astype(F32)
-    step = stepper(depth, sea, vort, flux)
+    bands(band)
+    flow, others = stepper(depth, sea, vort, flux, band)
     load.wait()
-    step(now, nxt, 1, span + 7, EDGE, 4)
-    step(nxt, now, 3, span + 5, EDGE, 4)
+    in_blocks(flow, now, nxt, 1, span + 7, EDGE, FLOW)
+    in_blocks(others, now, nxt, 2, span + 6, EDGE, REST)
+    in_blocks(flow, nxt, now, 3, span + 5, EDGE, FLOW)
+    in_blocks(others, nxt, now, 4, span + 4, EDGE, REST)
     keep = pltpu.make_async_copy(
         now.at[pl.ds(2, 3), pl.ds(EDGE, span)], seen.at[:, pl.ds(8, span)], sems.at[1]
     )
@@ -151,6 +178,7 @@
             pltpu.VMEM((FIELDS, window, SHARE, LAT), F32),
             pltpu.VMEM((window, SHARE, LAT), F32),
             pltpu.VMEM((WIDTH, LAT), F32),
+            pltpu.VMEM((2 * LAT, 2 * LAT), BF16),
             pltpu.VMEM((BANDS, INSIDE, SHARE, LAT), F32),
             pltpu.SemaphoreType.DMA((2,)),
         ],
@@ -160,7 +188,7 @@
 
 
 def outer_kernel(
-    ens, left, right, depth, mask, vort, _, _2, out, seen, now, nxt, flux, dep, sea, made, sems
+    ens, left, right, depth, mask, vort, _, _2, out, seen, now, nxt, flux, dep, sea, band, made, sems
 ):
     near, far = 3 * EDGE, 3 * EDGE + 2
     second = near + EDGE
@@ -180,15 +208,20 @@
         grid[pl.ds(8, WIDTH), :] = own[...].astype(F32)
         grid[pl.ds(4, EDGE), :] = left[FIELDS, 0, pl.ds(at, EDGE), :]
         grid[pl.ds(8 + WIDTH, EDGE), :] = right[FIELDS, 0, pl.ds(at, EDGE), :]
-    step = stepper(dep, sea, vort, flux)
+    bands(band)
+    flow, others = stepper(dep, sea, vort, flux, band)
     for c in loads:
         c.wait()
     end = second + far + EDGE
     skip = 8 + WIDTH - far - second
-    step(now, nxt, 1, second - 1, 4, 4)
-    step(now, nxt, second + 1, end - 1, skip, 4)
-    step(nxt, now, 3, second - 3, 4, 4)
-    step(nxt, now, second + 3, end - 3, skip, 5)
+    for d, stage, src, dst in (
+        (1, flow, now, nxt),
+        (2, others, now, nxt),
+        (3, flow, nxt, now),
+        (4, others, nxt, now),
+    ):
+        places = [(e, e + 4) for e in range(d, second - d)]
+        stage(src, dst, places + [(e, e + skip) for e in range(second + d, end - d)])
     right_at = second + EDGE
     keeps = [
         pltpu.make_async_copy(
@@ -210,8 +243,7 @@
     turn(jnp.concatenate([last] * 4, axis=0), made, 2 * FIELDS + 1)
     send = pltpu.make_async_copy(made, out.at[:, pl.ds(INSIDE, OUTSIDE)], sems.at[0])
     send.start()
-    send.wait()
-    for c in keeps:
+    for c in [send] + keeps:
         c.wait()
 
 
@@ -231,6 +263,7 @@
             pltpu.VMEM((window, SHARE, LAT), F32),
             pltpu.VMEM((112, LAT), F32),
             pltpu.VMEM((112, LAT), F32),
+            pltpu.VMEM((2 * LAT, 2 * LAT), BF16),
             pltpu.VMEM((BANDS, OUTSIDE, SHARE, LAT), F32),
             pltpu.SemaphoreType.DMA((4,)),
         ],
@@ -240,58 +273,44 @@
     )(ens, left, right, depth, mask, vort, messages, seen)
 
 
-def list_kernel(order, cell, out, count):
-    def one(j, n):
-        at = cell[order[j]]
-        out[n] = at + j * (1 << 16)
-        return n + jnp.where(at >= 0, 1, 0)
-
-    count[0] = lax.fori_loop(0, NOBS, one, 0, unroll=8)
-
-
-def own_list(order, cell):
-    return pl.pallas_call(
-        list_kernel,
-        out_shape=[
-            jax.ShapeDtypeStruct((NOBS + LAT,), jnp.int32),
-            jax.ShapeDtypeStruct((1,), jnp.int32),
-        ],
-        in_specs=[SMEM, SMEM],
-        out_specs=[SMEM, SMEM],
-        compiler_params=PARAMS,
-        name="own_observations",
-    )(order, cell)
-
-
-def pick_kernel(own, count, seen, out):
+def pick_kernel(order, cell, seen, _, _2, out, own):
     lane = lax.broadcasted_iota(jnp.int32, (SHARE, LAT), 1)
+
+    def listed(i, n):
+        codes = [cell[order[i * 16 + k]] for k in range(16)]
+        for k, at in enumerate(codes):
+            own[n] = at + (i * 16 + k) * (1 << 16)
+            n = n + jnp.where(at >= 0, 1, 0)
+        return n
+
+    total = lax.fori_loop(0, NOBS // 16, listed, 0)
     out[...] = jnp.zeros_like(out)
 
-    def one(i, _):
-        code = own[i]
-        j, at, lat = code >> 16, (code >> 7) & 511, code & 127
-        tile = pltpu.roll(seen[at], (j - lat) & (LAT - 1), 1)
-        b = j >> 7
-        out[b] = jnp.where(lane == (j & 127), tile, out[b])
+    def some(i, _):
+        found = []
+        for k in range(8):
+            valid = i * 8 + k < total
+            code = jnp.where(valid, own[i * 8 + k], 0)
+            j, at, lat = code >> 16, (code >> 7) & 511, code & 127
+            tile = pltpu.roll(seen[at], (j - lat) & (LAT - 1), 1)
+            found.append((j >> 7, jnp.where(valid, j & 127, -1), tile))
+        for b, r, tile in found:
+            out[b] = jnp.where(lane == r, tile, out[b])
         return 0
 
-    lax.fori_loop(0, count[0], one, 0)
-
-
-def pick(own, count, seen):
+    lax.fori_loop(0, (total + 7) // 8, some, 0)
+
+
+def pick(order, cell, seen, before):
     return pl.pallas_call(
         pick_kernel,
         out_shape=jax.ShapeDtypeStruct((BLOCKS, SHARE, LAT), F32),
-        in_specs=[SMEM, SMEM, VMEM],
+        in_specs=[SMEM, SMEM, VMEM, ANY, ANY],
         out_specs=VMEM,
+        scratch_shapes=[pltpu.SMEM((NOBS + 16,), jnp.int32)],
         compiler_params=PARAMS,
         name="pick_priors",
-    )(own, count, seen)
-
-
-def split(a):
-    high = a.astype(BF16)
-    return high, (a - high.astype(F32)).astype(BF16)
+    )(order, cell, seen, *before)
 
 
 def sort_kernel(order, facts, out):
@@ -339,13 +358,14 @@
 
 
 def filter_kernel(
-    place, priors, facts, lead, link, gain, where, many_lead, many_gain, many_where, counts, roots, table
+    place, p0, p1, p2, p3, facts, _, lead, link, gain, where, many_lead, many_gain, many_where, counts, roots, table, long_lead, long_gain, long_where
 ):
     me = place[2]
-    for d in range(BANDS):
-        at = pl.multiple_of((me ^ d) * SHARE, SHARE)
-        for b in range(BLOCKS):
-            table[pl.ds(at, SHARE), pl.ds(b * LAT, LAT)] = priors[d, b]
+    for x, got in enumerate((p0, p1, p2, p3)):
+        for z in range(2):
+            at = pl.multiple_of((me ^ (4 * z + x)) * SHARE, SHARE)
+            for b in range(BLOCKS):
+                table[pl.ds(at, SHARE), pl.ds(b * LAT, LAT)] = got[z, b]
     west, south = place[0].astype(F32), place[1].astype(F32)
     fact = [jnp.concatenate([facts[b * 4 + i] for i in range(4)], axis=1) for b in range(2)]
     later_than = lax.broadcasted_iota(jnp.int32, (BATCH, BATCH), 0)
@@ -453,13 +473,16 @@
             counts[1 + b] = (n.astype(jnp.int32) + SLOTS - 1) // SLOTS
             for c in range(CHUNKS):
                 h = hot(slot, float(c * SLOTS))
-                many_lead[b, c] = paired(dot_nt(sp[0], h), dot_nt(sp[1], h))
-                many_gain[b, c] = paired(dot_nt(h, g[0]), dot_nt(h, g[1]))
+                long_lead[b, c] = paired(dot_nt(sp[0], h), dot_nt(sp[1], h))
+                long_gain[b, c] = paired(dot_nt(h, g[0]), dot_nt(h, g[1]))
                 lon, up = spot(b, h)
-                many_where[b, c] = placed(lon, up, n - float(c * SLOTS))
-
-
-def filter_obs(place, priors, facts):
+                long_where[b, c] = placed(lon, up, n - float(c * SLOTS))
+        pltpu.sync_copy(long_lead, many_lead)
+        pltpu.sync_copy(long_gain, many_gain)
+        pltpu.sync_copy(long_where, many_where)
+
+
+def filter_obs(place, priors, facts, before):
     square = (2 * SLOTS, 2 * MEMBERS)
     return pl.pallas_call(
         filter_kernel,
@@ -468,47 +491,105 @@
         + [jax.ShapeDtypeStruct((2, CHUNKS) + square, BF16)] * 2
         + [jax.ShapeDtypeStruct((2, CHUNKS, SHARE + 8, SLOTS), F32)]
         + [jax.ShapeDtypeStruct((3,), jnp.int32), jax.ShapeDtypeStruct((2,), F32)],
-        in_specs=[SMEM, VMEM, VMEM],
-        out_specs=[VMEM] * 7 + [SMEM] * 2,
-        scratch_shapes=[pltpu.VMEM((MEMBERS, NOBS), F32)],
+        in_specs=[SMEM] + [VMEM] * 5 + [ANY],
+        out_specs=[VMEM] * 4 + [ANY] * 3 + [SMEM] * 2,
+        scratch_shapes=[
+            pltpu.VMEM((MEMBERS, NOBS), F32),
+            pltpu.VMEM((2, CHUNKS) + square, BF16),
+            pltpu.VMEM((2, CHUNKS) + square, BF16),
+            pltpu.VMEM((2, CHUNKS, SHARE + 8, SLOTS), F32),
+        ],
         compiler_params=PARAMS,
         name="filter_observations",
-    )(place, priors, facts)
-
-
-def gather_members(tiles, lane):
-    v = list(tiles)
-    for k in range(3):
-        s = SHARE << k
-        low = ((lane >> (4 + k)) & 1) == 0
-        w = list(v)
-        for i in range(8):
-            if i & (1 << k):
-                continue
-            j = i | (1 << k)
-            w[i] = jnp.where(low, v[i], pltpu.roll(v[j], s, 1))
-            w[j] = jnp.where(low, pltpu.roll(v[i], LAT - s, 1), v[j])
-        v = w
-    return v
+    )(place, *priors, facts, before)
+
+
+def arrange_kernel(parts, full, free, state, mid, made, halves, sems, stores):
+    sets = [(g, min(8, GROUPS - g)) for g in range(0, GROUPS, 8)]
+    loads = [
+        pltpu.make_async_copy(parts.at[:, pl.ds(g, n)], state.at[:, pl.ds(g, n)], sems.at[t])
+        for t, (g, n) in enumerate(sets)
+    ]
+    for c in loads:
+        c.start()
+    saves = []
+    for t, (g, n) in enumerate(sets):
+        loads[t].wait()
+        for s in range(8):
+            tile = jnp.transpose(state[s, pl.ds(g, 8)].reshape(8 * SHARE, LAT))
+            for j in range(8):
+                mid[j, pl.ds(s * SHARE, SHARE), :] = tile[j * SHARE : (j + 1) * SHARE]
+        for j in range(8):
+            tile = mid[j]
+            mean = jnp.sum(tile, axis=0, keepdims=True) * (1.0 / MEMBERS)
+            value = jnp.transpose(tile)
+            pair = jnp.concatenate(split(jnp.transpose(tile - mean)), axis=1)
+            for i in range(n):
+                made[g + i, j] = value[i * SHARE : (i + 1) * SHARE]
+                halves[g + i, j] = pair[i * SHARE : (i + 1) * SHARE]
+        for k, (a, b) in enumerate(((made, full), (halves, free))):
+            saves.append(
+                pltpu.make_async_copy(a.at[pl.ds(g, n)], b.at[pl.ds(g, n)], stores.at[t, k])
+            )
+            saves[-1].start()
+    for c in saves:
+        c.wait()
+
+
+def arrange(parts):
+    shapes = [
+        jax.ShapeDtypeStruct((GROUPS, 8, SHARE, MEMBERS), F32),
+        jax.ShapeDtypeStruct((GROUPS, 8, SHARE, 2 * MEMBERS), BF16),
+    ]
+    return pl.pallas_call(
+        arrange_kernel,
+        out_shape=shapes,
+        in_specs=[ANY],
+        out_specs=[ANY, ANY],
+        scratch_shapes=[
+            pltpu.VMEM((BANDS, SETS * 8, SHARE, LAT), F32),
+            pltpu.VMEM((8, MEMBERS, LAT), F32),
+            pltpu.VMEM(shapes[0].shape, F32),
+            pltpu.VMEM(shapes[1].shape, BF16),
+            pltpu.SemaphoreType.DMA((SETS,)),
+            pltpu.SemaphoreType.DMA((SETS, 2)),
+        ],
+        compiler_params=PARAMS,
+        name="arrange_members",
+    )(parts)
 
 
 def regress_kernel(
-    counts, roots, lead, link, gain, where, many_lead, many_gain, many_where, parts, out, state, made, big, sems
+    counts, roots, lead, link, gain, where, many_lead, many_gain, many_where, full_all, free_all, out,
+    full, free, made, big, long_lead, long_gain, long_where, sems, stores
 ):
-    load = pltpu.make_async_copy(parts, state, sems.at[0])
-    load.start()
-    lane = lax.broadcasted_iota(jnp.int32, (SHARE, LAT), 1)
-    load.wait()
-
-    def fetch(g):
-        return gather_members([state[s, g] for s in range(8)], lane)
+    def copies(at, sem):
+        return (
+            pltpu.make_async_copy(full_all.at[at], full.at[at], sem.at[0]),
+            pltpu.make_async_copy(free_all.at[at], free.at[at], sem.at[1]),
+        )
+
+    def inside(f):
+        return copies(pl.ds(f * INNER, INNER), sems.at[f])
+
+    outside = copies(pl.ds(INSIDE, OUTSIDE), sems.at[FIELDS])
+    for c in outside:
+        c.start()
+    for f in range(FIELDS):
+        for c in inside(f):
+            c.start()
+    for c in outside:
+        c.wait()
 
     def matrices(a):
         return jnp.concatenate(split(a), axis=1)
 
+    def times(pair, m):
+        got = jnp.dot(pair, m, preferred_element_type=F32)
+        return got[:, :MEMBERS] + got[:, MEMBERS:]
+
     def product(a, m):
-        got = jnp.dot(matrices(a), m, preferred_element_type=F32)
-        return got[:, :MEMBERS] + got[:, MEMBERS:]
+        return times(matrices(a), m)
 
     def taper(spots, lons):
         base, at = spots[0:SHARE], spots[SHARE : SHARE + 1]
@@ -519,63 +600,70 @@
             tiles.append(t * t)
         return jnp.concatenate(tiles, axis=0)
 
-    def centre(x):
-        mean = jnp.sum(x, axis=1, keepdims=True) * (1.0 / MEMBERS)
-        return mean, x - mean
-
-    def short(x, lons, q):
-        mean, anomaly = centre(x)
-        cov = product(anomaly, lead[q])
+    def short(x, pair, lons, q):
+        cov = times(pair, lead[q])
         t = taper(where[q], lons)
         cov = cov + product(t * cov, link[q])
-        return (mean + roots[0] * roots[1] * anomaly) + product(t * cov, gain[q])
-
-    def block(groups, q):
-        tiles, lons = [], []
-        for g, at in groups:
-            tiles += fetch(g)
-            lons += [at + j for j in range(8)] if len(groups) > 0 and at is not None else []
-        return jnp.concatenate(tiles, axis=0), lons
+        anomaly = pair[:, :MEMBERS].astype(F32) + pair[:, MEMBERS:].astype(F32)
+        return (x + (roots[0] * roots[1] - 1.0) * anomaly) + product(t * cov, gain[q])
+
+    def block(g, n, lons=8):
+        rows = n * lons * SHARE
+        if lons == 8:
+            x, pair = full[pl.ds(g, n)], free[pl.ds(g, n)]
+        else:
+            x, pair = full[g, pl.ds(0, lons)], free[g, pl.ds(0, lons)]
+        return x.reshape(rows, MEMBERS), pair.reshape(rows, 2 * MEMBERS)
 
     def put(f, lon, x, n):
         made[f, pl.ds(lon, n)] = x.reshape(n, SHARE, MEMBERS)
 
+    def store(f):
+        return pltpu.make_async_copy(made.at[f], out.at[f], stores.at[f])
+
+    tail = [float(RIGHT + 8 + j % 2) for j in range(8)]
+
     @pl.when(counts[0] == 0)
     def _():
-        def field(f, _):
-            for q, lo, n in ((0, 0, 5), (1, 5, 4)):
-                groups = [(f * INNER + lo + i, 8.0 * (lo + i + 1)) for i in range(n)]
-                x, lons = block(groups, q)
-                put(f, 8 * (lo + 1), short(x, lons, q), 8 * n)
-            for q, lon in ((0, 0), (1, RIGHT)):
-                x, lons = block([(INSIDE + 2 * f + q, float(lon))], q)
-                put(f, lon, short(x, lons, q), 8)
-            return 0
-
-        lax.fori_loop(0, FIELDS, field, 0)
-        tail = [float(RIGHT + 8 + j % 2) for j in range(8)]
-        x = short(jnp.concatenate(fetch(GROUPS - 2), axis=0), tail, 1)
+        x = short(*block(GROUPS - 2, 1), tail, 1)
         for f in range(4):
             put(f, RIGHT + 8, x[f * 2 * SHARE : (f + 1) * 2 * SHARE], 2)
-        x = short(jnp.concatenate(fetch(GROUPS - 1)[:2], axis=0), tail[:2], 1)
-        put(4, RIGHT + 8, x, 2)
+        put(4, RIGHT + 8, short(*block(GROUPS - 1, 1, 2), tail[:2], 1), 2)
+
+        def field(f, _):
+            for c in inside(f):
+                c.wait()
+            for q, lo, n in ((0, 0, 5), (1, 5, 4)):
+                lons = [8.0 * (lo + 1) + i for i in range(8 * n)]
+                put(f, 8 * (lo + 1), short(*block(f * INNER + lo, n), lons, q), 8 * n)
+            for q, lon in ((0, 0), (1, RIGHT)):
+                lons = [float(lon + i) for i in range(8)]
+                put(f, lon, short(*block(INSIDE + 2 * f + q, 1), lons, q), 8)
+            store(f).start()
+            return 0
+
+        lax.fori_loop(0, FIELDS, field, 0)
 
     @pl.when(counts[0] != 0)
     def _():
-        lons_of = [
-            (f * INNER + i, f, 8 * (i + 1)) for f in range(FIELDS) for i in range(INNER)
-        ]
-
-        def long(x, lons):
+        for f in range(FIELDS):
+            for c in inside(f):
+                c.wait()
+        pltpu.sync_copy(many_lead, long_lead)
+        pltpu.sync_copy(many_gain, long_gain)
+        pltpu.sync_copy(many_where, long_where)
+
+        def long(x, _, lons):
             for b in range(2):
-                mean, anomaly = centre(x)
+                mean = jnp.sum(x, axis=1, keepdims=True) * (1.0 / MEMBERS)
+                anomaly = x - mean
+                big[pl.ds(0, x.shape[0]), :] = x + (roots[b] - 1.0) * anomaly
                 anomaly = roots[b] * anomaly
-                big[pl.ds(0, x.shape[0]), :] = mean + anomaly
 
                 def chunk(c, _):
-                    t = taper(many_where[b, c], lons)
-                    w = t * product(anomaly, many_lead[b, c])
-                    big[pl.ds(0, x.shape[0]), :] += product(w, many_gain[b, c])
+                    t = taper(long_where[b, c], lons)
+                    w = t * product(anomaly, long_lead[b, c])
+                    big[pl.ds(0, x.shape[0]), :] += product(w, long_gain[b, c])
                     return 0
 
                 lax.fori_loop(0, counts[1 + b], chunk, 0)
@@ -583,44 +671,48 @@
             return x
 
         def each(g, _):
-            inside = g < INSIDE
+            inner = g < INSIDE
             h = g - INSIDE
-            f = jnp.where(inside, g // INNER, h // 2)
-            lon = jnp.where(inside, 8 * (g % INNER + 1), RIGHT * (h % 2))
+            f = jnp.where(inner, g // INNER, h // 2)
+            lon = jnp.where(inner, 8 * (g % INNER + 1), RIGHT * (h % 2))
             at = lon.astype(F32)
-            x = jnp.concatenate(fetch(g), axis=0)
-            put(f, lon, long(x, [at + j for j in range(8)]), 8)
+            put(f, lon, long(*block(g, 1), [at + j for j in range(8)]), 8)
             return 0
 
         lax.fori_loop(0, GROUPS - 2, each, 0)
-        tail = [float(RIGHT + 8 + j % 2) for j in range(8)]
-        x = long(jnp.concatenate(fetch(GROUPS - 2), axis=0), tail)
+        x = long(*block(GROUPS - 2, 1), tail)
         for f in range(4):
             put(f, RIGHT + 8, x[f * 2 * SHARE : (f + 1) * 2 * SHARE], 2)
-        x = long(jnp.concatenate(fetch(GROUPS - 1)[:2], axis=0), tail[:2])
-        put(4, RIGHT + 8, x, 2)
-
-    store = pltpu.make_async_copy(made, out, sems.at[0])
-    store.start()
-    store.wait()
-
-
-def regress(tables, parts):
+        put(4, RIGHT + 8, long(*block(GROUPS - 1, 1, 2), tail[:2]), 2)
+        for f in range(FIELDS):
+            store(f).start()
+
+    for f in range(FIELDS):
+        store(f).wait()
+
+
+def regress(tables, state):
     *tables, counts, roots = tables
+    square = (2, CHUNKS, 2 * SLOTS, 2 * MEMBERS)
     return pl.pallas_call(
         regress_kernel,
         out_shape=jax.ShapeDtypeStruct((FIELDS, WIDTH, SHARE, MEMBERS), F32),
-        in_specs=[SMEM] * 2 + [VMEM] * 7 + [ANY],
+        in_specs=[SMEM] * 2 + [VMEM] * 4 + [ANY] * 5,
         out_specs=ANY,
         scratch_shapes=[
-            pltpu.VMEM((BANDS, GROUPS, SHARE, LAT), F32),
+            pltpu.VMEM((GROUPS, 8, SHARE, MEMBERS), F32),
+            pltpu.VMEM((GROUPS, 8, SHARE, 2 * MEMBERS), BF16),
             pltpu.VMEM((FIELDS, WIDTH, SHARE, MEMBERS), F32),
             pltpu.VMEM((8 * SHARE, MEMBERS), F32),
-            pltpu.SemaphoreType.DMA((1,)),
+            pltpu.VMEM(square, BF16),
+            pltpu.VMEM(square, BF16),
+            pltpu.VMEM((2, CHUNKS, SHARE + 8, SLOTS), F32),
+            pltpu.SemaphoreType.DMA((FIELDS + 1, 2)),
+            pltpu.SemaphoreType.DMA((FIELDS,)),
         ],
         compiler_params=PARAMS,
         name="regress_state",
-    )(counts, roots, *tables, parts)
+    )(counts, roots, *tables, *state)
 
 
 def across(x, axis, bits):
@@ -655,7 +747,8 @@
     west = sector * WIDTH
     here = obs_lon - west
     cell = ((obs_field - 2) * WIDTH + here) * LAT + obs_lat
-    own, count = own_list(obs_order, jnp.where((here >= 0) & (here < WIDTH), cell, -1))
+    cell = jnp.where((here >= 0) & (here < WIDTH), cell, -1)
+    place = jnp.stack([west, member * SHARE, member])
 
     messages, seen = forecast_inner(ens, ocean_depth, land_mask, vort)
     messages, seen = forecast_outer(
@@ -663,14 +756,18 @@
     )
     parts = lax.all_to_all(messages, "member", split_axis=0, concat_axis=0, tiled=True)
 
-    priors = pick(own, count, seen.reshape(3 * WIDTH, SHARE, LAT))
-    for k in range(4):
-        priors = priors + across(priors, "sector", 1 << k)
-    priors = priors[None]
-    for k in range(3):
-        priors = jnp.concatenate([priors, across(priors, "member", 1 << k)])
-    place = jnp.stack([west, member * SHARE, member])
-    analysis = regress(filter_obs(place, priors, facts), parts)
+    priors = pick(obs_order, cell, seen.reshape(3 * WIDTH, SHARE, LAT), [facts, place])
+    for bit in (2, 4, 1):
+        priors = priors + across(priors, "sector", bit)
+    both = ("member", "sector")
+    count = lax.axis_size("member") * sectors
+    crossed = lax.ppermute(priors, both, [(i, i ^ (4 * sectors + 8)) for i in range(count)])
+    priors = jnp.stack(
+        [priors + across(priors, "sector", 8), across(priors, "member", 4) + crossed]
+    )
+    priors = [priors] + [across(priors, "member", x) for x in (1, 2, 3)]
+    state = arrange(parts)
+    analysis = regress(filter_obs(place, priors, facts, state[0]), state)
     return jnp.transpose(analysis, (0, 2, 1, 3))
 
 

time: 134 us -> 105 us (0.78)
  Pallas kernels: 66.2 us -> 47 us
  waiting for transfers between devices: 32.9 us -> 26.6 us
  starting transfers between devices: 29.6 us -> 25.7 us
    pallas_call x1, Pallas kernels: 21.8 us -> 9.92 us  [regress(): pl.pallas_call(regress_kernel, out_shape=jax.ShapeDtypeStruct((FIELDS, WI...]
    ppermute x7 -> x8, waiting for transfers between devices: 32.9 us -> 24.8 us  [across(): return lax.ppermute(x, axis, [(i, i ^ bits) for i in range(count)])]
    ppermute x7 -> x8, starting transfers between devices: 20.1 us -> 13 us  [across(): return lax.ppermute(x, axis, [(i, i ^ bits) for i in range(count)])]
    pallas_call x1, Pallas kernels: 12.7 us -> 8.76 us  [forecast_inner(): pl.pallas_call(inner_kernel, out_shape=[jax.ShapeDtypeStruct((BANDS, GROU...]
    ppermute x0 -> x1, starting transfers between devices: none -> 3.16 us  [shards(): lax.ppermute(priors, both, [(i, i ^ 4 * sectors + 8) for i in range(count)])]
    pallas_call x1, Pallas kernels: 6.22 us -> 4.18 us  [forecast_outer(): pl.pallas_call(outer_kernel, out_shape=[jax.ShapeDtypeStruct(messages.sha...]
    ppermute x0 -> x1, waiting for transfers between devices: none -> 1.87 us  [shards(): lax.ppermute(priors, both, [(i, i ^ 4 * sectors + 8) for i in range(count)])]
    pallas_call x1, Pallas kernels: 8.1 us -> 6.41 us  [pick(): pl.pallas_call(pick_kernel, out_shape=jax.ShapeDtypeStruct((BLOCKS, SHARE...]
  transfers between devices with their start and end apart: 10 -> 12, of which waited for: 7 -> 7; matrix products, arithmetic and copies ran while one was open for 3% -> 3% of each run, Pallas kernels for 27% -> 23%
where the time goes in v1:
time: 105 us; the launch traced here: 104 us
  Pallas kernels  47 us (45%)
  waiting for transfers between devices  26.6 us (25%)
  starting transfers between devices  25.7 us (24%)
  other arithmetic  2.17 us (2%)
  local copies, waits for them, and re-layouts  2.08 us (2%)
    ppermute x8, waiting for transfers between devices, across(): return lax.ppermute(x, axis, [(i, i ^ bits) for i in range(count)])  24.8 us
    ppermute x8, starting transfers between devices, across(): return lax.ppermute(x, axis, [(i, i ^ bits) for i in range(count)])  13 us
    pallas_call x1, Pallas kernels, regress(): pl.pallas_call(regress_kernel, out_shape=jax.ShapeDtypeStruct((FIELDS, WI...  9.92 us
    pallas_call x1, Pallas kernels, forecast_inner(): pl.pallas_call(inner_kernel, out_shape=[jax.ShapeDtypeStruct((BANDS, GROU...  8.76 us
    all_to_all x1, starting transfers between devices, shards(): lax.all_to_all(messages, 'member', split_axis=0, concat_axis=0, tiled=True)  7.75 us
    pallas_call x1, Pallas kernels, pick(): pl.pallas_call(pick_kernel, out_shape=jax.ShapeDtypeStruct((BLOCKS, SHARE...  6.41 us
    pallas_call x1, Pallas kernels, filter_obs(): pl.pallas_call(filter_kernel, out_shape=[jax.ShapeDtypeStruct((2,) + squa...  6.35 us
    pallas_call x1, Pallas kernels, arrange(): pl.pallas_call(arrange_kernel, out_shape=shapes, in_specs=[ANY], out_spec...  6.02 us
  transfers between devices with their start and end apart: 12, of which 7 were waited for; matrix products, arithmetic and copies ran while one was open for 3% of the time, Pallas kernels for 23%

profile of v1, /device:TPU:8, one launch (start us, length us, event | category | flops | bytes accessed | tf_op | source)
XLA Modules:
  0.0 103.9 jit_solution(11666879589682913489)
XLA Ops:
  0.0 2.6 %pack_edges.1 = (f32[6,4,16,128]{3,2,1,0:T(8,128)}, f32[6,4,16,128]{3,2,1,0:T(8,128)}) custom-call(f32[5,90,16,128]{3,2,1,0:T(8,128)} %bitcast.16, f32[90,128]{1,0:T(8,128)} %depth.5, s32[90,128]{1,0:T(8,128)} %mask.5), custom_call_target="tpu_custom_call" | custom-call | tf_op jit(solution)/shard_map/pack_edges/pallas_call | solution.py:56
  2.7 1.7 %collective-permute-start.1 = (f32[6,4,16,128]{3,2,1,0:T(8,128)}, f32[6,4,16,128]{3,2,1,0:T(8,128)S(1)}, u32[]{:S(2)}, u32[]{:S(2)}) collective-permute-start(f32[6,4,16,128]{3,2,1,0:T(8,128)} %get-tuple-element.23), channel_id=1, source_target_pairs={{1,0},{2,1},{3,2},{4,3},{5,4},{6,5},{7,6},{8,7},{9,8},{10,9},{11,1... | collective-permute-start | bytes 589832 | tf_op jit(solution)/shard_map/ppermute | solution.py:741
  4.4 8.8 %forecast_inner.1 = (f32[8,57,16,128]{3,2,1,0:T(8,128)}, f32[3,90,16,128]{3,2,1,0:T(8,128)}) custom-call(f32[5,90,16,128]{3,2,1,0:T(8,128)} %bitcast.17, f32[90,128]{1,0:T(8,128)} %depth.5, s32[90,128]{1,0:T(8,128)} %mask.5, f32[1,128]{1,0:T(1,128)} %bitcast.25), custom_call_target="tpu_custom_call" | custom-call | tf_op jit(solution)/shard_map/forecast_inner/pallas_call | solution.py:168
  13.2 0.6 copy-done.1
  13.8 0.1 copy-done.2
  13.9 4.2 %forecast_outer.1 = (f32[8,57,16,128]{3,2,1,0:T(8,128)}, f32[3,90,16,128]{3,2,1,0:T(8,128)}) custom-call(f32[5,90,16,128]{3,2,1,0:T(8,128)} %bitcast.18, f32[6,4,16,128]{3,2,1,0:T(8,128)} %copy-done.1, f32[6,4,16,128]{3,2,1,0:T(8,128)} %copy-done.2, f32[90,128]{1,0:T(8,128)} %depth.5, s32[90,128]{1,0:T(8,128)} %mask.5, ...), custom_call_target="tpu_custom_call", output_to_operand_aliasing={{0}: (6, {}), {1}: (7, {})} | custom-call | tf_op jit(solution)/shard_map/forecast_outer/pallas_call | solution.py:252
  18.2 7.8 %all-to-all-start = ((f32[8,57,16,128]{3,2,1,0:T(8,128)}), f32[8,57,16,128]{3,2,1,0:T(8,128)}, u32[]{:S(2)}, u32[]{:S(2)}) async-start(f32[8,57,16,128]{3,2,1,0:T(8,128)} %get-tuple-element.27), calls=%async_computation | async-start | bytes 7471104 | tf_op jit(solution)/shard_map/all_to_all | solution.py:757
  25.9 0.6 fusion
  26.6 0.7 stack.48.facts
  27.2 2.8 %obs_in_batch_order.1._.facts = f32[8,8,128]{2,1,0:T(8,128)} custom-call(s32[8,1,128]{2,1,0:T(1,128)} %bitcast.20, f32[8,1024]{1,0:T(8,128)} %stack.48.facts), custom_call_target="tpu_custom_call" | custom-call | tf_op jit(solution)/shard_map/obs_in_batch_order/pallas_call | solution.py:334
  30.0 0.7 pad_add_fusion._2.place
  30.6 6.4 %pick_priors.1 = f32[8,16,128]{2,1,0:T(8,128)} custom-call(s32[1024]{0:T(1024)} %order.1, s32[1024]{0:T(1024)} %get-tuple-element.40.cell, f32[270,16,128]{2,1,0:T(8,128)} %bitcast.19, f32[8,8,128]{2,1,0:T(8,128)} %obs_in_batch_order.1._.facts, s32[3]{0:T(128)} %pad_add_fusion._2.place), custom_call_target="tpu_custom_call" | custom-call | tf_op jit(solution)/shard_map/pick_priors/pallas_call | solution.py:305
  37.1 2.7 %collective-permute-start.2 = (f32[8,16,128]{2,1,0:T(8,128)}, f32[8,16,128]{2,1,0:T(8,128)S(1)}, u32[]{:S(2)}, u32[]{:S(2)}) collective-permute-start(f32[8,16,128]{2,1,0:T(8,128)} %pick_priors.1), channel_id=1, source_target_pairs={{0,2},{1,3},{2,0},{3,1},{4,6},{5,7},{6,4},{7,5},{8,10},{9,11},{10,... | collective-permute-start | bytes 196616 | tf_op jit(solution)/shard_map/ppermute | solution.py:720
  39.7 2.5 %collective-permute-done.2 = f32[8,16,128]{2,1,0:T(8,128)S(1)} collective-permute-done((f32[8,16,128]{2,1,0:T(8,128)}, f32[8,16,128]{2,1,0:T(8,128)S(1)}, u32[]{:S(2)}, u32[]{:S(2)}) %collective-permute-start.2) | collective-permute-done | bytes 65568 | tf_op jit(solution)/shard_map/ppermute | solution.py:720
  42.2 0.9 add.24
  43.0 1.5 %collective-permute-start.3 = (f32[8,16,128]{2,1,0:T(8,128)S(1)}, f32[8,16,128]{2,1,0:T(8,128)S(1)}, u32[]{:S(2)}, u32[]{:S(2)}) collective-permute-start(f32[8,16,128]{2,1,0:T(8,128)S(1)} %add.24), channel_id=1, source_target_pairs={{0,4},{1,5},{2,6},{3,7},{4,0},{5,1},{6,2},{7,3},{8,12},{9,13},{10,... | collective-permute-start | bytes 196616 | tf_op jit(solution)/shard_map/ppermute | solution.py:720
  44.5 4.3 %collective-permute-done.3 = f32[8,16,128]{2,1,0:T(8,128)S(1)} collective-permute-done((f32[8,16,128]{2,1,0:T(8,128)S(1)}, f32[8,16,128]{2,1,0:T(8,128)S(1)}, u32[]{:S(2)}, u32[]{:S(2)}) %collective-permute-start.3) | collective-permute-done | bytes 65568 | tf_op jit(solution)/shard_map/ppermute | solution.py:720
  48.9 0.1 collective-permute-start.4
  49.0 1.2 %collective-permute-done.4 = f32[8,16,128]{2,1,0:T(8,128)S(1)} collective-permute-done((f32[8,16,128]{2,1,0:T(8,128)S(1)}, f32[8,16,128]{2,1,0:T(8,128)S(1)}, u32[]{:S(2)}, u32[]{:S(2)}) %collective-permute-start.4) | collective-permute-done | bytes 65568 | tf_op jit(solution)/shard_map/ppermute | solution.py:720
  50.2 1.0 collective-permute-start.5
  51.2 3.2 %collective-permute-start.7 = (f32[8,16,128]{2,1,0:T(8,128)S(1)}, f32[8,16,128]{2,1,0:T(8,128)S(1)}, u32[]{:S(2)}, u32[]{:S(2)}) collective-permute-start(f32[8,16,128]{2,1,0:T(8,128)S(1)} %add.26), channel_id=1, source_target_pairs={{0,72},{1,73},{2,74},{3,75},{4,76},{5,77},{6,78},{7,79},{8,64},{9,... | collective-permute-start | bytes 196616 | tf_op jit(solution)/shard_map/ppermute | solution.py:764
  54.4 1.0 collective-permute-start.6
  55.3 4.7 %collective-permute-done.5 = f32[8,16,128]{2,1,0:T(8,128)S(1)} collective-permute-done((f32[8,16,128]{2,1,0:T(8,128)S(1)}, f32[8,16,128]{2,1,0:T(8,128)S(1)}, u32[]{:S(2)}, u32[]{:S(2)}) %collective-permute-start.5) | collective-permute-done | bytes 65568 | tf_op jit(solution)/shard_map/ppermute | solution.py:720
  60.0 1.9 %collective-permute-done.7 = f32[8,16,128]{2,1,0:T(8,128)S(1)} collective-permute-done((f32[8,16,128]{2,1,0:T(8,128)S(1)}, f32[8,16,128]{2,1,0:T(8,128)S(1)}, u32[]{:S(2)}, u32[]{:S(2)}) %collective-permute-start.7) | collective-permute-done | bytes 65568 | tf_op jit(solution)/shard_map/ppermute | solution.py:764
  61.9 11.2 %collective-permute-done.6 = f32[8,16,128]{2,1,0:T(8,128)S(1)} collective-permute-done((f32[8,16,128]{2,1,0:T(8,128)S(1)}, f32[8,16,128]{2,1,0:T(8,128)S(1)}, u32[]{:S(2)}, u32[]{:S(2)}) %collective-permute-start.6) | collective-permute-done | bytes 65568 | tf_op jit(solution)/shard_map/ppermute | solution.py:720
  73.1 5.8 %collective-permute-start.10 = (f32[2,8,16,128]{3,2,1,0:T(8,128)S(1)}, f32[2,8,16,128]{3,2,1,0:T(8,128)S(1)}, u32[]{:S(2)}, u32[]{:S(2)}) collective-permute-start(f32[2,8,16,128]{3,2,1,0:T(8,128)S(1)} %pad_maximum_fusion.p0), channel_id=1, source_target_pairs={{0,48},{16,32},{32,16},{48,0},{64,112},{80,96},{96,80},{112,64},{1... | collective-permute-start | bytes 393224 | tf_op jit(solution)/shard_map/ppermute | solution.py:720
  78.9 0.9 collective-permute-start.8
  79.9 6.0 %arrange_members.1 = (f32[57,8,16,128]{3,2,1,0:T(8,128)}, bf16[57,8,16,256]{3,2,1,0:T(8,128)(2,1)}) custom-call(f32[8,57,16,128]{3,2,1,0:T(8,128)} %all-to-all-done.parts), custom_call_target="tpu_custom_call" | custom-call | tf_op jit(solution)/shard_map/arrange_members/pallas_call | solution.py:544
  85.9 0.9 collective-permute-done.9.p2
  86.8 0.6 copy-done.4
  87.5 6.3 %filter_observations.1 = (bf16[2,256,256]{2,1,0:T(8,128)(2,1)}, bf16[2,256,256]{2,1,0:T(8,128)(2,1)}, bf16[2,256,256]{2,1,0:T(8,128)(2,1)}, f32[2,24,128]{2,1,0:...) custom-call(s32[3]{0:T(128)} %pad_add_fusion._2.place, ...), custom_call_target="tpu_custom_call" | custom-call | tf_op jit(solution)/shard_map/filter_observations/pallas_call | solution.py:487
  93.9 9.9 %regress_state.1 = f32[5,90,16,128]{3,2,1,0:T(8,128)} custom-call(s32[3]{0:T(128)} %get-tuple-element.29.counts, f32[2]{0:T(128)} %get-tuple-element.30.roots, bf16[2,256,256]{2,1,0:T(8,128)(2,1)} %get-tuple-element.31.lead, bf16[2,256,256]{2,1,0:T(8,128)(2,1)} %get-tuple-element.32.link, bf16[2,256,256]{2,1,0:T(8,128)(2,1)} %get-tuple-element.33.gain, ...), custom_call_target="tpu_custom_call" | custom-call | tf_op jit(solution)/shard_map/regress_state/pallas_call | solution.py:697
  (32 shorter events, 0.2 us)
Async XLA Ops:
  2.6 10.6 %collective-permute-start = (f32[6,4,16,128]{3,2,1,0:T(8,128)}, f32[6,4,16,128]{3,2,1,0:T(8,128)S(1)}, u32[]{:S(2)}, u32[]{:S(2)}) collective-permute-start(f32[6,4,16,128]{3,2,1,0:T(8,128)} %get-tuple-element.22), channel_id=1, source_target_pairs={{0,1},{1,2},{2,3},{3,4},{4,5},{5,6},{6,7},{7,8},{8,9},{9,10},{10,1... | collective-permute-start | bytes 589832 | tf_op jit(solution)/shard_map/ppermute | solution.py:740
  2.7 10.5 %collective-permute-start.1 = (f32[6,4,16,128]{3,2,1,0:T(8,128)}, f32[6,4,16,128]{3,2,1,0:T(8,128)S(1)}, u32[]{:S(2)}, u32[]{:S(2)}) collective-permute-start(f32[6,4,16,128]{3,2,1,0:T(8,128)} %get-tuple-element.23), channel_id=1, source_target_pairs={{1,0},{2,1},{3,2},{4,3},{5,4},{6,5},{7,6},{8,7},{9,8},{10,9},{11,1... | collective-permute-start | bytes 589832 | tf_op jit(solution)/shard_map/ppermute | solution.py:741
  13.2 0.7 copy-start.1
  13.2 0.7 copy-start.2
  18.1 7.8 %copy-start.6 = (s32[1024]{0:T(1024)S(1)}, s32[1024]{0:T(1024)}, u32[]{:S(2)}) copy-start(s32[1024]{0:T(1024)} %param.17) | copy-start | bytes 12292
  18.1 7.8 %copy-start.7 = (s32[1024]{0:T(1024)S(1)}, s32[1024]{0:T(1024)}, u32[]{:S(2)}) copy-start(s32[1024]{0:T(1024)} %param.18) | copy-start | bytes 12292
  18.1 7.8 %copy-start.8 = (s32[1024]{0:T(1024)S(1)}, s32[1024]{0:T(1024)}, u32[]{:S(2)}) copy-start(s32[1024]{0:T(1024)} %param.16) | copy-start | bytes 12292
  18.1 8.4 %copy-start.9 = (f32[1024]{0:T(1024)S(1)}, f32[1024]{0:T(1024)}, u32[]{:S(2)}) copy-start(f32[1024]{0:T(1024)} %param.14) | copy-start | bytes 12292
  18.2 8.4 %copy-start.10 = (f32[1024]{0:T(1024)S(1)}, f32[1024]{0:T(1024)}, u32[]{:S(2)}) copy-start(f32[1024]{0:T(1024)} %param.15) | copy-start | bytes 12292
  18.2 61.7 %all-to-all-start = ((f32[8,57,16,128]{3,2,1,0:T(8,128)}), f32[8,57,16,128]{3,2,1,0:T(8,128)}, u32[]{:S(2)}, u32[]{:S(2)}) async-start(f32[8,57,16,128]{3,2,1,0:T(8,128)} %get-tuple-element.27), calls=%async_computation | async-start | bytes 7471104 | tf_op jit(solution)/shard_map/all_to_all | solution.py:757
  37.1 5.1 %collective-permute-start.2 = (f32[8,16,128]{2,1,0:T(8,128)}, f32[8,16,128]{2,1,0:T(8,128)S(1)}, u32[]{:S(2)}, u32[]{:S(2)}) collective-permute-start(f32[8,16,128]{2,1,0:T(8,128)} %pick_priors.1), channel_id=1, source_target_pairs={{0,2},{1,3},{2,0},{3,1},{4,6},{5,7},{6,4},{7,5},{8,10},{9,11},{10,... | collective-permute-start | bytes 196616 | tf_op jit(solution)/shard_map/ppermute | solution.py:720
  43.0 5.8 %collective-permute-start.3 = (f32[8,16,128]{2,1,0:T(8,128)S(1)}, f32[8,16,128]{2,1,0:T(8,128)S(1)}, u32[]{:S(2)}, u32[]{:S(2)}) collective-permute-start(f32[8,16,128]{2,1,0:T(8,128)S(1)} %add.24), channel_id=1, source_target_pairs={{0,4},{1,5},{2,6},{3,7},{4,0},{5,1},{6,2},{7,3},{8,12},{9,13},{10,... | collective-permute-start | bytes 196616 | tf_op jit(solution)/shard_map/ppermute | solution.py:720
  48.9 1.3 %collective-permute-start.4 = (f32[8,16,128]{2,1,0:T(8,128)S(1)}, f32[8,16,128]{2,1,0:T(8,128)S(1)}, u32[]{:S(2)}, u32[]{:S(2)}) collective-permute-start(f32[8,16,128]{2,1,0:T(8,128)S(1)} %add.25), channel_id=1, source_target_pairs={{0,1},{1,0},{2,3},{3,2},{4,5},{5,4},{6,7},{7,6},{8,9},{9,8},{10,11... | collective-permute-start | bytes 196616 | tf_op jit(solution)/shard_map/ppermute | solution.py:720
  50.2 9.8 %collective-permute-start.5 = (f32[8,16,128]{2,1,0:T(8,128)S(1)}, f32[8,16,128]{2,1,0:T(8,128)S(1)}, u32[]{:S(2)}, u32[]{:S(2)}) collective-permute-start(f32[8,16,128]{2,1,0:T(8,128)S(1)} %add.26), channel_id=1, source_target_pairs={{0,8},{1,9},{2,10},{3,11},{4,12},{5,13},{6,14},{7,15},{8,0},{9,1},... | collective-permute-start | bytes 196616 | tf_op jit(solution)/shard_map/ppermute | solution.py:720
  51.2 10.7 %collective-permute-start.7 = (f32[8,16,128]{2,1,0:T(8,128)S(1)}, f32[8,16,128]{2,1,0:T(8,128)S(1)}, u32[]{:S(2)}, u32[]{:S(2)}) collective-permute-start(f32[8,16,128]{2,1,0:T(8,128)S(1)} %add.26), channel_id=1, source_target_pairs={{0,72},{1,73},{2,74},{3,75},{4,76},{5,77},{6,78},{7,79},{8,64},{9,... | collective-permute-start | bytes 196616 | tf_op jit(solution)/shard_map/ppermute | solution.py:764
  54.4 18.7 %collective-permute-start.6 = (f32[8,16,128]{2,1,0:T(8,128)S(1)}, f32[8,16,128]{2,1,0:T(8,128)S(1)}, u32[]{:S(2)}, u32[]{:S(2)}) collective-permute-start(f32[8,16,128]{2,1,0:T(8,128)S(1)} %add.26), channel_id=1, source_target_pairs={{0,64},{16,80},{32,96},{48,112},{64,0},{80,16},{96,32},{112,48},{1... | collective-permute-start | bytes 196616 | tf_op jit(solution)/shard_map/ppermute | solution.py:720
  73.1 13.7 %copy-start = (f32[2,8,16,128]{3,2,1,0:T(8,128)}, f32[2,8,16,128]{3,2,1,0:T(8,128)S(1)}, u32[]{:S(2)}) copy-start(f32[2,8,16,128]{3,2,1,0:T(8,128)S(1)} %pad_maximum_fusion.p0) | copy-start | bytes 393220
  73.1 12.8 %collective-permute-start.10 = (f32[2,8,16,128]{3,2,1,0:T(8,128)S(1)}, f32[2,8,16,128]{3,2,1,0:T(8,128)S(1)}, u32[]{:S(2)}, u32[]{:S(2)}) collective-permute-start(f32[2,8,16,128]{3,2,1,0:T(8,128)S(1)} %pad_maximum_fusion.p0), channel_id=1, source_target_pairs={{0,48},{16,32},{32,16},{48,0},{64,112},{80,96},{96,80},{112,64},{1... | collective-permute-start | bytes 393224 | tf_op jit(solution)/shard_map/ppermute | solution.py:720
  78.9 7.9 %collective-permute-start.9 = (f32[2,8,16,128]{3,2,1,0:T(8,128)S(1)}, f32[2,8,16,128]{3,2,1,0:T(8,128)S(1)}, u32[]{:S(2)}, u32[]{:S(2)}) collective-permute-start(f32[2,8,16,128]{3,2,1,0:T(8,128)S(1)} %pad_maximum_fusion.p0), channel_id=1, source_target_pairs={{0,32},{16,48},{32,0},{48,16},{64,96},{80,112},{96,64},{112,80},{1... | collective-permute-start | bytes 393224 | tf_op jit(solution)/shard_map/ppermute | solution.py:720
  78.9 7.9 %collective-permute-start.8 = (f32[2,8,16,128]{3,2,1,0:T(8,128)S(1)}, f32[2,8,16,128]{3,2,1,0:T(8,128)S(1)}, u32[]{:S(2)}, u32[]{:S(2)}) collective-permute-start(f32[2,8,16,128]{3,2,1,0:T(8,128)S(1)} %pad_maximum_fusion.p0), channel_id=1, source_target_pairs={{0,16},{16,0},{32,48},{48,32},{64,80},{80,64},{96,112},{112,96},{1... | collective-permute-start | bytes 393224 | tf_op jit(solution)/shard_map/ppermute | solution.py:720
  85.9 0.9 copy-start.3
  86.8 0.6 copy-start.4
  86.8 0.7 copy-start.5

commit v2 on v1

v2 whole, which is shorter than its diff:
```python
import jax
import jax.numpy as jnp
from jax import lax
from jax.experimental import pallas as pl
from jax.experimental.pallas import tpu as pltpu
from jax.sharding import PartitionSpec as P

NLON = 1440
LAT = 128
FIELDS = 5
MEMBERS = 128
NOBS = 1024
BATCH = 512
BLOCKS = NOBS // LAT
RADIUS = 48
SHARE = 16
BANDS = 8
WIDTH = 90
EDGE = 4
INNER = 9
RIGHT = 80
INSIDE = FIELDS * INNER
OUTSIDE = 2 * FIELDS + 2
GROUPS = INSIDE + OUTSIDE
SETS = (GROUPS + 7) // 8
CUT = 48
SLOTS = 128
CHUNKS = BATCH // SLOTS
MEAN = SLOTS - 1
FLOW, REST = 39, 38
SCALE = 1.0 / (RADIUS * RADIUS)
F32 = jnp.float32
BF16 = jnp.bfloat16
SMEM = pl.BlockSpec(memory_space=pltpu.SMEM)
VMEM = pl.BlockSpec(memory_space=pltpu.VMEM)
ANY = pl.BlockSpec(memory_space=pl.ANY)
PARAMS = pltpu.CompilerParams(vmem_limit_bytes=56 * 1024 * 1024)


def edges_kernel(ens, depth, mask, west, east, deep, sea, sems):
    sides = ((west, 0), (east, WIDTH - EDGE))
    grids = ((0, 0, 8), (RIGHT, 8, WIDTH - RIGHT))
    copies = [
        pltpu.make_async_copy(ens.at[:, pl.ds(lon, EDGE)], out.at[pl.ds(0, FIELDS)], sems.at[i])
        for i, (out, lon) in enumerate(sides)
    ]
    for i, (lon, at, n) in enumerate(grids):
        for j, (grid, to) in enumerate(((depth, deep), (mask, sea))):
            copies.append(
                pltpu.make_async_copy(
                    grid.at[pl.ds(lon, n)], to.at[pl.ds(at, n)], sems.at[2 + 2 * i + j]
                )
            )
    for c in copies:
        c.start()
    for c in copies:
        c.wait()
    for (out, lon), (start, at, _) in zip(sides, grids):
        rows = pl.ds(at + lon - start, EDGE)
        out[FIELDS, 0, pl.ds(0, 8), :] = jnp.concatenate([deep[rows, :], sea[rows, :].astype(F32)], axis=0)


def edges(ens, depth, mask):
    side = jax.ShapeDtypeStruct((FIELDS + 1, EDGE, SHARE, LAT), F32)
    return pl.pallas_call(
        edges_kernel,
        out_shape=[side, side],
        in_specs=[ANY, ANY, ANY],
        out_specs=[VMEM, VMEM],
        scratch_shapes=[
            pltpu.VMEM((24, LAT), F32),
            pltpu.VMEM((24, LAT), jnp.int32),
            pltpu.SemaphoreType.DMA((6,)),
        ],
        compiler_params=PARAMS,
        name="pack_edges",
    )(ens, depth, mask)


def split(a):
    high = a.astype(BF16)
    return high, (a - high.astype(F32)).astype(BF16)


def bands(out):
    row = lax.broadcasted_iota(jnp.int32, (2 * LAT, 2 * LAT), 0) % LAT
    col = lax.broadcasted_iota(jnp.int32, (2 * LAT, 2 * LAT), 1)
    gap = row - col % LAT
    value = jnp.where(jnp.abs(gap) == 1, jnp.where(col < LAT, gap, 1), 0)
    out[...] = value.astype(F32).astype(BF16)


def stepper(dep, sea, vort, flux, band):
    spin = jnp.broadcast_to(vort[...], (SHARE, LAT))

    def halves(tiles):
        return jnp.concatenate(split(jnp.concatenate(tiles, axis=0)), axis=1)

    def difference(tiles):
        got = jnp.dot(halves(tiles), band[:, 0:LAT], preferred_element_type=F32)
        return [got[i * SHARE : (i + 1) * SHARE] for i in range(len(tiles))]

    def both(tiles):
        got = jnp.dot(halves(tiles), band[...], preferred_element_type=F32)
        rows = [got[i * SHARE : (i + 1) * SHARE] for i in range(len(tiles))]
        return [r[:, 0:LAT] for r in rows], [r[:, LAT:] for r in rows]

    def flow(src, dst, places):
        slope = difference([src[2, e] for e, _ in places])
        for (e, row), dh in zip(places, slope):
            u, v = src[0, e], src[1, e]
            m = sea[pl.ds(row, 1), :]
            un = m * (u + spin * v - 0.15 * (src[2, e + 1] - src[2, e - 1]))
            dst[0, e] = un
            dst[1, e] = m * (v - spin * u - 0.15 * dh)
            flux[e] = dep[pl.ds(row, 1), :] * un

    def others(src, dst, places):
        slope = difference([dep[pl.ds(row, 1), :] * dst[1, e] for e, row in places])
        for (e, _), dv in zip(places, slope):
            dst[2, e] = src[2, e] - 0.15 * (flux[e + 1] - flux[e - 1] + dv)
        for c in (3, 4):
            slope, total = both([src[c, e] for e, _ in places])
            for (e, _), dc, around in zip(places, slope, total):
                a, ae, aw = src[c, e], src[c, e + 1], src[c, e - 1]
                dst[c, e] = (
                    a
                    - 0.15 * (dst[0, e] * (ae - aw) + dst[1, e] * dc)
                    + 0.1 * (((ae + aw) + around) - 4.0 * a)
                )

    return flow, others


def in_blocks(stage, src, dst, lo, hi, row, n):
    def block(i, _):
        e = jnp.minimum(lo + i * n, hi - n)
        stage(src, dst, [(e + k, e + k + row) for k in range(n)])
        return 0

    lax.fori_loop(0, (hi - lo + n - 1) // n, block, 0)


def turn(tiles, out, g):
    tile = jnp.transpose(tiles.reshape(8 * SHARE, LAT))
    for b in range(BANDS):
        out[b, g] = tile[b * SHARE : (b + 1) * SHARE]


def inner_kernel(ens, depth, mask, vort, out, seen, now, nxt, flux, sea, band, made, sems):
    span = INNER * 8
    first = FLOW + 2
    loads = [
        pltpu.make_async_copy(
            ens.at[:, pl.ds(EDGE + at, n)], now.at[:, pl.ds(at, n)], sems.at[2 + i]
        )
        for i, (at, n) in enumerate(((0, first), (first, span + 2 * EDGE - first)))
    ]
    for c in loads:
        c.start()
    sea[...] = mask[...].astype(F32)
    bands(band)
    flow, others = stepper(depth, sea, vort, flux, band)
    for at, c in zip((1, 1 + FLOW), loads):
        c.wait()
        flow(now, nxt, [(at + k, at + k + EDGE) for k in range(FLOW)])
    in_blocks(others, now, nxt, 2, span + 6, EDGE, REST)
    in_blocks(flow, nxt, now, 3, span + 5, EDGE, FLOW)
    in_blocks(others, nxt, now, 4, span + 4, EDGE, REST)
    keep = pltpu.make_async_copy(
        now.at[pl.ds(2, 3), pl.ds(EDGE, span)], seen.at[:, pl.ds(8, span)], sems.at[1]
    )
    keep.start()

    def send(f):
        at = pl.ds(f * INNER, INNER)
        return pltpu.make_async_copy(made.at[:, at], out.at[:, at], sems.at[2 + f])

    def field(f, _):
        for i in range(INNER):
            turn(now[f, pl.ds(EDGE + i * 8, 8)], made, f * INNER + i)
        send(f).start()
        return 0

    lax.fori_loop(0, FIELDS, field, 0)
    for f in range(FIELDS):
        send(f).wait()
    keep.wait()


def forecast_inner(ens, depth, mask, vort):
    window = INNER * 8 + 2 * EDGE
    return pl.pallas_call(
        inner_kernel,
        out_shape=[
            jax.ShapeDtypeStruct((BANDS, GROUPS, SHARE, LAT), F32),
            jax.ShapeDtypeStruct((3, WIDTH, SHARE, LAT), F32),
        ],
        in_specs=[ANY, VMEM, VMEM, VMEM],
        out_specs=[ANY, ANY],
        scratch_shapes=[
            pltpu.VMEM((FIELDS, window, SHARE, LAT), F32),
            pltpu.VMEM((FIELDS, window, SHARE, LAT), F32),
            pltpu.VMEM((window, SHARE, LAT), F32),
            pltpu.VMEM((WIDTH, LAT), F32),
            pltpu.VMEM((2 * LAT, 2 * LAT), BF16),
            pltpu.VMEM((BANDS, INSIDE, SHARE, LAT), F32),
            pltpu.SemaphoreType.DMA((2 + FIELDS,)),
        ],
        compiler_params=PARAMS,
        name="forecast_inner",
    )(ens, depth, mask, vort)


def outer_kernel(
    ens, left, right, depth, mask, vort, _, _2, out, seen, now, nxt, flux, dep, sea, band, made, sems
):
    near, far = 3 * EDGE, 3 * EDGE + 2
    second = near + EDGE
    loads = [
        pltpu.make_async_copy(ens.at[:, pl.ds(0, near)], now.at[:, pl.ds(EDGE, near)], sems.at[0]),
        pltpu.make_async_copy(
            ens.at[:, pl.ds(WIDTH - far, far)], now.at[:, pl.ds(second, far)], sems.at[1]
        ),
        pltpu.make_async_copy(left.at[pl.ds(0, FIELDS)], now.at[:, pl.ds(0, EDGE)], sems.at[2]),
        pltpu.make_async_copy(
            right.at[pl.ds(0, FIELDS)], now.at[:, pl.ds(second + far, EDGE)], sems.at[3]
        ),
    ]
    for c in loads:
        c.start()
    for grid, own, at in ((dep, depth, 0), (sea, mask, EDGE)):
        grid[pl.ds(8, WIDTH), :] = own[...].astype(F32)
        grid[pl.ds(4, EDGE), :] = left[FIELDS, 0, pl.ds(at, EDGE), :]
        grid[pl.ds(8 + WIDTH, EDGE), :] = right[FIELDS, 0, pl.ds(at, EDGE), :]
    bands(band)
    flow, others = stepper(dep, sea, vort, flux, band)
    for c in loads:
        c.wait()
    end = second + far + EDGE
    skip = 8 + WIDTH - far - second
    for d, stage, src, dst in (
        (1, flow, now, nxt),
        (2, others, now, nxt),
        (3, flow, nxt, now),
        (4, others, nxt, now),
    ):
        places = [(e, e + 4) for e in range(d, second - d)]
        stage(src, dst, places + [(e, e + skip) for e in range(second + d, end - d)])
    right_at = second + EDGE
    keeps = [
        pltpu.make_async_copy(
            now.at[pl.ds(2, 3), pl.ds(EDGE, 8)], seen.at[:, pl.ds(0, 8)], sems.at[1]
        ),
        pltpu.make_async_copy(
            now.at[pl.ds(2, 3), pl.ds(right_at, WIDTH - RIGHT)],
            seen.at[:, pl.ds(RIGHT, WIDTH - RIGHT)],
            sems.at[2],
        ),
    ]
    for c in keeps:
        c.start()
    for f in range(FIELDS):
        turn(now[f, pl.ds(EDGE, 8)], made, 2 * f)
        turn(now[f, pl.ds(right_at, 8)], made, 2 * f + 1)
    turn(now[pl.ds(0, 4), pl.ds(right_at + 8, 2)], made, 2 * FIELDS)
    last = now[4, pl.ds(right_at + 8, 2)]
    turn(jnp.concatenate([last] * 4, axis=0), made, 2 * FIELDS + 1)
    send = pltpu.make_async_copy(made, out.at[:, pl.ds(INSIDE, OUTSIDE)], sems.at[0])
    send.start()
    for c in [send] + keeps:
        c.wait()


def forecast_outer(ens, left, right, depth, mask, vort, messages, seen):
    window = 6 * EDGE + 2 + 2 * EDGE
    return pl.pallas_call(
        outer_kernel,
        out_shape=[
            jax.ShapeDtypeStruct(messages.shape, F32),
            jax.ShapeDtypeStruct(seen.shape, F32),
        ],
        in_specs=[ANY] + [VMEM] * 5 + [ANY] * 2,
        out_specs=[ANY, ANY],
        scratch_shapes=[
            pltpu.VMEM((FIELDS, window, SHARE, LAT), F32),
            pltpu.VMEM((FIELDS, window, SHARE, LAT), F32),
            pltpu.VMEM((window, SHARE, LAT), F32),
            pltpu.VMEM((112, LAT), F32),
            pltpu.VMEM((112, LAT), F32),
            pltpu.VMEM((2 * LAT, 2 * LAT), BF16),
            pltpu.VMEM((BANDS, OUTSIDE, SHARE, LAT), F32),
            pltpu.SemaphoreType.DMA((4,)),
        ],
        input_output_aliases={6: 0, 7: 1},
        compiler_params=PARAMS,
        name="forecast_outer",
    )(ens, left, right, depth, mask, vort, messages, seen)


def pick_kernel(order, cell, seen, _, out, own):
    lane = lax.broadcasted_iota(jnp.int32, (SHARE, LAT), 1)

    def listed(i, n):
        codes = [cell[order[i * 16 + k]] for k in range(16)]
        for k, at in enumerate(codes):
            own[n] = at + (i * 16 + k) * (1 << 16)
            n = n + jnp.where(at >= 0, 1, 0)
        return n

    total = lax.fori_loop(0, NOBS // 16, listed, 0)
    out[...] = jnp.zeros_like(out)

    def some(i, _):
        found = []
        for k in range(8):
            valid = i * 8 + k < total
            code = jnp.where(valid, own[i * 8 + k], 0)
            j, at, lat = code >> 16, (code >> 7) & 511, code & 127
            tile = pltpu.roll(seen[at], (j - lat) & (LAT - 1), 1)
            found.append((j >> 7, jnp.where(valid, j & 127, -1), tile))
        for b, r, tile in found:
            out[b] = jnp.where(lane == r, tile, out[b])
        return 0

    lax.fori_loop(0, (total + 7) // 8, some, 0)


def pick(order, cell, seen, before):
    return pl.pallas_call(
        pick_kernel,
        out_shape=jax.ShapeDtypeStruct((BLOCKS, SHARE, LAT), F32),
        in_specs=[SMEM, SMEM, VMEM, ANY],
        out_specs=VMEM,
        scratch_shapes=[pltpu.SMEM((NOBS + 16,), jnp.int32)],
        compiler_params=PARAMS,
        name="pick_priors",
    )(order, cell, seen, before)


def sort_kernel(order, facts, out):
    data = facts[...]
    high, rest = split(data)
    left = data - high.astype(F32)
    mid, low = split(left)
    parts = jnp.concatenate([high, mid, low, jnp.zeros_like(rest)], axis=0)
    row = lax.broadcasted_iota(jnp.int32, (NOBS, LAT), 0)

    def block(b, _):
        hot = jnp.where(row == order[b], 1.0, 0.0).astype(BF16)
        got = jnp.dot(parts, hot, preferred_element_type=F32)
        out[b] = got[0:8] + got[8:16] + got[16:24]
        return 0

    lax.fori_loop(0, BLOCKS, block, 0)


def in_order(order, facts):
    return pl.pallas_call(
        sort_kernel,
        out_shape=jax.ShapeDtypeStruct((BLOCKS, 8, LAT), F32),
        in_specs=[VMEM, VMEM],
        out_specs=VMEM,
        compiler_params=PARAMS,
        name="obs_in_batch_order",
    )(order.reshape(BLOCKS, 1, LAT), facts)


def dot_nt(a, b):
    return lax.dot_general(a, b, (((1,), (1,)), ((), ())), preferred_element_type=F32)


def exact(a, b, dims):
    (ah, al), (bh, bl) = split(a), split(b)

    def dot(x, y):
        return lax.dot_general(x, y, (dims, ((), ())), preferred_element_type=F32)

    return dot(ah, bh) + (dot(ah, bl) + dot(al, bh))


def paired(high, low):
    top = jnp.concatenate([high, low], axis=1)
    bottom = jnp.concatenate([high, jnp.zeros_like(low)], axis=1)
    return jnp.concatenate([top, bottom], axis=0).astype(BF16)


def batch_facts(facts):
    return [jnp.concatenate([facts[b * 4 + i] for i in range(4)], axis=1) for b in range(2)]


def finder(place, fact):
    west, south = place[0].astype(F32), place[1].astype(F32)
    later_than = lax.broadcasted_iota(jnp.int32, (BATCH, BATCH), 0)
    later_than = later_than <= lax.broadcasted_iota(jnp.int32, (BATCH, BATCH), 1)
    upper = jnp.where(later_than, 1.0, 0.0).astype(BF16)
    number = lax.broadcasted_iota(jnp.int32, (SLOTS, BATCH), 0).astype(F32)
    lane = lax.broadcasted_iota(jnp.int32, (1, SLOTS), 1).astype(F32)
    row = lax.broadcasted_iota(jnp.int32, (SHARE, SLOTS), 0).astype(F32)
    rel, lat = [], []
    for b in range(2):
        r = fact[b][0:1] - west
        r = jnp.where(r < -float(NLON // 2 - WIDTH // 2), r + NLON, r)
        r = jnp.where(r >= float(NLON // 2 + WIDTH // 2), r - NLON, r)
        rel.append(r)
        lat.append(fact[b][1:2] - south)

    def near(b, lo, hi):
        dl = jnp.maximum(jnp.maximum(lo - rel[b], rel[b] - hi), 0.0)
        dr = jnp.maximum(jnp.maximum(-lat[b], lat[b] - (SHARE - 1.0)), 0.0)
        flag = jnp.where(dl * dl + dr * dr < float(RADIUS * RADIUS), 1.0, 0.0)
        upto = jnp.dot(
            jnp.broadcast_to(flag, (16, BATCH)).astype(BF16), upper, preferred_element_type=F32
        )[0:1]
        return jnp.where(flag > 0.0, upto - 1.0, -float(NOBS)), jnp.sum(flag)

    def hot(slot, shift):
        return jnp.where(slot == number + shift, 1.0, 0.0).astype(BF16)

    def spot(b, h):
        both = jnp.concatenate(
            [jnp.broadcast_to(rel[b], (8, BATCH)), jnp.broadcast_to(lat[b], (8, BATCH))], axis=0
        )
        high, low = split(both)
        got = dot_nt(high, h) + dot_nt(low, h)
        return got[0:1], got[8:9]

    def placed(lon, up, used, mean):
        gap = row - up
        base = jnp.where(lane < used, 1.0 - gap * gap * SCALE, -1.0)
        base = jnp.where(lane == mean, 1.0, base)
        scale = jnp.where(lane == mean, 0.0, SCALE)
        rows = [jnp.broadcast_to(a, (8, SLOTS)) for a in (lon, scale)]
        return jnp.concatenate([base] + rows, axis=0)

    return near, hot, spot, placed


def prepare_kernel(place, facts, hots, taper, where, count):
    fact = batch_facts(facts)
    near, hot, spot, placed = finder(place, fact)

    def column(a):
        tall = jnp.transpose(jnp.broadcast_to(a, (LAT, BATCH)))
        return jnp.concatenate([tall] * (BATCH // LAT), axis=1)

    east = jnp.abs(column(fact[0][0:1]) - fact[1][0:1])
    east = jnp.minimum(east, NLON - east)
    up = column(fact[0][1:2]) - fact[1][1:2]
    t = jnp.maximum(1.0 - (east * east + up * up) * SCALE, 0.0)
    taper[...] = t * t
    full = jnp.float32(0.0)
    for q, (lo, hi) in enumerate(((0.0, CUT - 1.0), (float(CUT), WIDTH - 1.0))):
        slot1, n1 = near(0, lo, hi)
        slot2, n2 = near(1, lo, hi)
        full = jnp.maximum(full, n1 + n2)
        h1, h2 = hot(slot1, 0.0), hot(slot2, -n1)
        hots[q, 0], hots[q, 1] = h1, h2
        (lon1, lat1), (lon2, lat2) = spot(0, h1), spot(1, h2)
        where[q] = placed(lon1 + lon2, lat1 + lat2, n1 + n2, MEAN)
    count[0] = jnp.where(full > MEAN, 1, 0)


def prepare(place, facts):
    return pl.pallas_call(
        prepare_kernel,
        out_shape=[
            jax.ShapeDtypeStruct((2, 2, SLOTS, BATCH), BF16),
            jax.ShapeDtypeStruct((BATCH, BATCH), F32),
            jax.ShapeDtypeStruct((2, SHARE + 16, SLOTS), F32),
            jax.ShapeDtypeStruct((1,), jnp.int32),
        ],
        in_specs=[SMEM, VMEM],
        out_specs=[VMEM] * 3 + [SMEM],
        compiler_params=PARAMS,
        name="list_observations",
    )(place, facts)


def arrange_kernel(parts, out, state, mid, halves, sems, stores):
    sets = [(g, min(8, GROUPS - g)) for g in range(0, GROUPS, 8)]
    loads = [
        pltpu.make_async_copy(parts.at[:, pl.ds(g, n)], state.at[:, pl.ds(g, n)], sems.at[t])
        for t, (g, n) in enumerate(sets)
    ]
    for c in loads:
        c.start()
    saves = []
    for t, (g, n) in enumerate(sets):
        loads[t].wait()
        for s in range(8):
            tile = jnp.transpose(state[s, pl.ds(g, 8)].reshape(8 * SHARE, LAT))
            for j in range(8):
                mid[j, pl.ds(s * SHARE, SHARE), :] = tile[j * SHARE : (j + 1) * SHARE]
        for j in range(8):
            pair = jnp.concatenate(split(jnp.transpose(mid[j])), axis=1)
            for i in range(n):
                halves[g + i, j] = pair[i * SHARE : (i + 1) * SHARE]
        saves.append(
            pltpu.make_async_copy(halves.at[pl.ds(g, n)], out.at[pl.ds(g, n)], stores.at[t])
        )
        saves[-1].start()
    for c in saves:
        c.wait()


def arrange(parts):
    shape = jax.ShapeDtypeStruct((GROUPS, 8, SHARE, 2 * MEMBERS), BF16)
    return pl.pallas_call(
        arrange_kernel,
        out_shape=shape,
        in_specs=[ANY],
        out_specs=ANY,
        scratch_shapes=[
            pltpu.VMEM((BANDS, SETS * 8, SHARE, LAT), F32),
            pltpu.VMEM((8, MEMBERS, LAT), F32),
            pltpu.VMEM(shape.shape, BF16),
            pltpu.SemaphoreType.DMA((SETS,)),
            pltpu.SemaphoreType.DMA((SETS,)),
        ],
        compiler_params=PARAMS,
        name="arrange_members",
    )(parts)


def analyse_kernel(
    place, many, p0, p1, p2, p3, facts, where, hots_in, taper_in, given, out,
    hots, taper, state, table, lead, link, gain, shapes, made, big, long_lead, long_gain, long_where, sems, stores,
):
    loads = [
        pltpu.make_async_copy(taper_in, taper, sems.at[FIELDS + 1]),
        pltpu.make_async_copy(hots_in, hots, sems.at[FIELDS + 2]),
    ]

    def inside(f):
        at = pl.ds(f * INNER, INNER)
        return pltpu.make_async_copy(given.at[at], state.at[at], sems.at[f])

    at = pl.ds(INSIDE, OUTSIDE)
    outside = pltpu.make_async_copy(given.at[at], state.at[at], sems.at[FIELDS])
    for c in loads + [outside] + [inside(f) for f in range(FIELDS)]:
        c.start()

    me = place[2]
    for x, got in enumerate((p0, p1, p2, p3)):
        for z in range(2):
            at = pl.multiple_of((me ^ (4 * z + x)) * SHARE, SHARE)
            for b in range(BLOCKS):
                table[pl.ds(at, SHARE), pl.ds(b * LAT, LAT)] = got[z, b]
    fact = batch_facts(facts)

    def adjust(picked, b):
        values, errors = fact[b][2:3], fact[b][3:4]
        mean = jnp.sum(picked, axis=0, keepdims=True) * (1.0 / MEMBERS)
        anomalies = picked - mean
        variance = jnp.sum(anomalies * anomalies, axis=0, keepdims=True) / (MEMBERS - 1) + 1e-6
        innovation = values - mean
        ratio = jnp.sum(innovation * innovation, axis=1, keepdims=True) / jnp.sum(
            variance + errors, axis=1, keepdims=True
        )
        root = jnp.sqrt(ratio)
        inflated = ratio * variance
        spread = root * anomalies
        post_var = 1.0 / (1.0 / inflated + 1.0 / errors)
        post_mean = post_var * (mean / inflated + values / errors)
        increments = post_mean - mean + (jnp.sqrt(post_var / inflated) - 1.0) * spread
        return root, spread * (1.0 / ((MEMBERS - 1) * inflated)), increments

    root1, scaled1, inc1 = adjust(table[:, pl.ds(0, BATCH)], 0)

    later = table[:, pl.ds(BATCH, BATCH)]
    mean = jnp.sum(later, axis=0, keepdims=True) * (1.0 / MEMBERS)
    spread = root1 * (later - mean)
    cov = exact(jnp.transpose(scaled1), spread, ((1,), (0,)))
    for c in loads:
        c.wait()
    later = (mean + spread) + exact(inc1, taper[...] * cov, ((1,), (0,)))
    root2, scaled2, inc2 = adjust(later, 1)
    both_roots = jnp.sum(root1 * root2)

    sp1, sp2 = split(root1 * scaled1), split(root1 * root2 * scaled2)
    shift1 = jnp.sum(inc1, axis=0, keepdims=True) * (1.0 / MEMBERS)
    free1 = inc1 - shift1
    g1, g2 = split(root2 * free1 + shift1), split(inc2)
    f1, s2 = split(free1), split(root2 * scaled2)
    lane = lax.broadcasted_iota(jnp.int32, (1, SLOTS), 1)
    tall = lax.broadcasted_iota(jnp.int32, (SLOTS, 1), 0)
    rest = [a.astype(F32) for a in split(1.0 - root1 * root2)]
    for q in range(2):
        h1, h2 = hots[q, 0], hots[q, 1]
        lead_h, lead_l = [dot_nt(a, h1) + dot_nt(b, h2) for a, b in zip(sp1, sp2)]
        lead[q] = paired(jnp.where(lane == MEAN, 1.0 / MEMBERS, lead_h), lead_l)
        gain_h, gain_l = [dot_nt(h1, a) + dot_nt(h2, b) for a, b in zip(g1, g2)]
        gain[q] = paired(
            jnp.where(tall == MEAN, rest[0], gain_h), jnp.where(tall == MEAN, rest[1], gain_l)
        )
        one = dot_nt(h1, f1[0]) + dot_nt(h1, f1[1])
        two = dot_nt(h2, s2[0]) + dot_nt(h2, s2[1])
        link[q] = paired(*split(exact(one, two, ((1,), (1,)))))

    outside.wait()

    def times(pair, m):
        got = jnp.dot(pair, m, preferred_element_type=F32)
        return got[:, :MEMBERS] + got[:, MEMBERS:]

    def product(a, m):
        return times(jnp.concatenate(split(a), axis=1), m)

    def taper_of(spots, lon):
        base, at, scale = spots[0:SHARE], spots[SHARE : SHARE + 1], spots[SHARE + 8 : SHARE + 9]
        gap = at - lon
        t = jnp.maximum(base - gap * gap * scale, 0.0)
        return t * t

    def whole(pair):
        return pair[:, :MEMBERS].astype(F32) + pair[:, MEMBERS:].astype(F32)

    def short(pair, t, q):
        cov = times(pair, lead[q])
        cov = cov + product(t * cov, link[q])
        return both_roots * whole(pair) + product(t * cov, gain[q])

    def block(g, n, lons=8):
        pair = state[pl.ds(g, n)] if lons == 8 else state[g, pl.ds(0, lons)]
        return pair.reshape(n * lons * SHARE, 2 * MEMBERS)

    def put(f, lon, x, n):
        made[f, pl.ds(lon, n)] = x.reshape(n, SHARE, MEMBERS)

    def store(f):
        return pltpu.make_async_copy(made.at[f], out.at[f], stores.at[f])

    @pl.when(many[0] == 0)
    def _():
        for q, (lo, hi) in enumerate(((0, CUT), (CUT, WIDTH))):
            for lon in range(lo, hi):
                shapes[lon] = taper_of(where[q], float(lon))

        def shape(lon, n):
            return shapes[pl.ds(lon, n)].reshape(n * SHARE, SLOTS)

        x = short(block(GROUPS - 2, 1), jnp.concatenate([shape(RIGHT + 8, 2)] * 4, axis=0), 1)
        for f in range(4):
            put(f, RIGHT + 8, x[f * 2 * SHARE : (f + 1) * 2 * SHARE], 2)
        put(4, RIGHT + 8, short(block(GROUPS - 1, 1, 2), shape(RIGHT + 8, 2), 1), 2)

        def some(fs):
            for f in fs:
                inside(f).wait()
            for q, lo, n, edge in ((0, 0, 5, 0), (1, 5, 4, RIGHT)):
                lon = 8 * (lo + 1)
                pair = jnp.concatenate(
                    [a for f in fs for a in (block(f * INNER + lo, n), block(INSIDE + 2 * f + q, 1))],
                    axis=0,
                )
                t = jnp.concatenate([shape(lon, 8 * n), shape(edge, 8)] * len(fs), axis=0)
                x = short(pair, t, q)
                r = 8 * (n + 1) * SHARE
                for i, f in enumerate(fs):
                    put(f, lon, x[i * r : i * r + 8 * n * SHARE], 8 * n)
                    put(f, edge, x[i * r + 8 * n * SHARE : (i + 1) * r], 8)
            for f in fs:
                store(f).start()

        some([0, 1])
        some([2, 3])
        some([4])

    @pl.when(many[0] != 0)
    def _():
        near, hot, spot, placed = finder(place, fact)
        roots = [jnp.sum(root1), jnp.sum(root2)]
        chunks = []
        for b, (sp, g) in enumerate(((split(scaled1), split(inc1)), (split(scaled2), g2))):
            slot, n = near(b, 0.0, WIDTH - 1.0)
            chunks.append((n.astype(jnp.int32) + SLOTS - 1) // SLOTS)
            for c in range(CHUNKS):
                h = hot(slot, float(c * SLOTS))
                long_lead[b, c] = paired(dot_nt(sp[0], h), dot_nt(sp[1], h))
                long_gain[b, c] = paired(dot_nt(h, g[0]), dot_nt(h, g[1]))
                lon, up = spot(b, h)
                long_where[b, c] = placed(lon, up, n - float(c * SLOTS), -1)
        for f in range(FIELDS):
            inside(f).wait()

        def long(pair, lons):
            x = whole(pair)
            for b in range(2):
                mean = jnp.sum(x, axis=1, keepdims=True) * (1.0 / MEMBERS)
                anomaly = x - mean
                big[pl.ds(0, x.shape[0]), :] = x + (roots[b] - 1.0) * anomaly
                anomaly = roots[b] * anomaly

                def chunk(c, _):
                    t = jnp.concatenate([taper_of(long_where[b, c], lon) for lon in lons], axis=0)
                    w = t * product(anomaly, long_lead[b, c])
                    big[pl.ds(0, x.shape[0]), :] += product(w, long_gain[b, c])
                    return 0

                lax.fori_loop(0, chunks[b], chunk, 0)
                x = big[pl.ds(0, x.shape[0]), :]
            return x

        def each(g, _):
            inner = g < INSIDE
            h = g - INSIDE
            f = jnp.where(inner, g // INNER, h // 2)
            lon = jnp.where(inner, 8 * (g % INNER + 1), RIGHT * (h % 2))
            at = lon.astype(F32)
            put(f, lon, long(block(g, 1), [at + j for j in range(8)]), 8)
            return 0

        lax.fori_loop(0, GROUPS - 2, each, 0)
        tail = [float(RIGHT + 8 + j % 2) for j in range(8)]
        x = long(block(GROUPS - 2, 1), tail)
        for f in range(4):
            put(f, RIGHT + 8, x[f * 2 * SHARE : (f + 1) * 2 * SHARE], 2)
        put(4, RIGHT + 8, long(block(GROUPS - 1, 1, 2), tail[:2]), 2)
        for f in range(FIELDS):
            store(f).start()

    for f in range(FIELDS):
        store(f).wait()


def analyse(place, many, priors, facts, where, hots, taper, state):
    square = (2 * SLOTS, 2 * MEMBERS)
    return pl.pallas_call(
        analyse_kernel,
        out_shape=jax.ShapeDtypeStruct((FIELDS, WIDTH, SHARE, MEMBERS), F32),
        in_specs=[SMEM] * 2 + [VMEM] * 6 + [ANY] * 3,
        out_specs=ANY,
        scratch_shapes=[
            pltpu.VMEM(hots.shape, BF16),
            pltpu.VMEM(taper.shape, F32),
            pltpu.VMEM(state.shape, BF16),
            pltpu.VMEM((MEMBERS, NOBS), F32),
            pltpu.VMEM((2,) + square, BF16),
            pltpu.VMEM((2,) + square, BF16),
            pltpu.VMEM((2,) + square, BF16),
            pltpu.VMEM((WIDTH, SHARE, SLOTS), F32),
            pltpu.VMEM((FIELDS, WIDTH, SHARE, MEMBERS), F32),
            pltpu.VMEM((8 * SHARE, MEMBERS), F32),
            pltpu.VMEM((2, CHUNKS) + square, BF16),
            pltpu.VMEM((2, CHUNKS) + square, BF16),
            pltpu.VMEM((2, CHUNKS, SHARE + 16, SLOTS), F32),
            pltpu.SemaphoreType.DMA((FIELDS + 3,)),
            pltpu.SemaphoreType.DMA((FIELDS,)),
        ],
        compiler_params=PARAMS,
        name="analyse",
    )(place, many, *priors, facts, where, hots, taper, state)


def across(x, axis, bits):
    count = lax.axis_size(axis)
    return lax.ppermute(x, axis, [(i, i ^ bits) for i in range(count)])


def shards(
    ensemble,
    ocean_depth,
    planetary_vorticity,
    land_mask,
    obs_values,
    obs_error,
    obs_lon,
    obs_lat,
    obs_field,
    obs_order,
):
    member, sector = lax.axis_index("member"), lax.axis_index("sector")
    sectors = lax.axis_size("sector")
    vort = planetary_vorticity.reshape(1, LAT)
    ens = jnp.transpose(ensemble, (1, 2, 0, 3))
    west_side, east_side = edges(ens, ocean_depth, land_mask)
    left = lax.ppermute(east_side, "sector", [(i, (i + 1) % sectors) for i in range(sectors)])
    right = lax.ppermute(west_side, "sector", [((i + 1) % sectors, i) for i in range(sectors)])

    lon_f, lat_f = obs_lon.astype(F32), obs_lat.astype(F32)
    facts = in_order(
        obs_order, jnp.stack([lon_f, lat_f, obs_values, obs_error] + [jnp.zeros_like(lon_f)] * 4)
    )
    west = sector * WIDTH
    here = obs_lon - west
    cell = ((obs_field - 2) * WIDTH + here) * LAT + obs_lat
    cell = jnp.where((here >= 0) & (here < WIDTH), cell, -1)
    place = jnp.stack([west, member * SHARE, member])
    hots, taper, where, many = prepare(place, facts)

    messages, seen = forecast_inner(ens, ocean_depth, land_mask, vort)
    messages, seen = forecast_outer(
        ens, left, right, ocean_depth, land_mask, vort, messages, seen
    )
    parts = lax.all_to_all(messages, "member", split_axis=0, concat_axis=0, tiled=True)

    priors = pick(obs_order, cell, seen.reshape(3 * WIDTH, SHARE, LAT), where)
    for bit in (2, 4, 1):
        priors = priors + across(priors, "sector", bit)
    both = ("member", "sector")
    count = lax.axis_size("member") * sectors
    crossed = lax.ppermute(priors, both, [(i, i ^ (4 * sectors + 8)) for i in range(count)])
    priors = jnp.stack(
        [priors + across(priors, "sector", 8), across(priors, "member", 4) + crossed]
    )
    priors = [priors] + [across(priors, "member", x) for x in (1, 2, 3)]
    analysis = analyse(place, many, priors, facts, where, hots, taper, arrange(parts))
    return jnp.transpose(analysis, (0, 2, 1, 3))


def solution(mesh):
    placed = (
        P("member", None, "sector", None),
        P("sector", None),
        P(),
        P("sector", None),
        P(),
        P(),
        P(),
        P(),
        P(),
        P(),
    )
    return jax.shard_map(
        shards,
        mesh=mesh,
        in_specs=placed,
        out_specs=P(None, "member", "sector", None),
        check_vma=False,
    )
```

time: 105 us -> 97.6 us (0.930)
  Pallas kernels: 47 us -> 41.2 us
    ppermute x8, waiting for transfers between devices: 24.8 us -> 14.9 us  [across(): return lax.ppermute(x, axis, [(i, i ^ bits) for i in range(count)])]
    ppermute x1, waiting for transfers between devices: 1.87 us -> 10.8 us  [shards(): lax.ppermute(priors, both, [(i, i ^ 4 * sectors + 8) for i in range(count)])]
    pallas_call x4, Pallas kernels: 24.9 us -> 19.8 us  [the longest x1 10.7 us: analyse(): pl.pallas_call(analyse_kernel, out_shape=jax.ShapeDtypeStruct((FIELDS, WI...]
  transfers between devices with their start and end apart: 12 -> 12, of which waited for: 7 -> 8; matrix products, arithmetic and copies ran while one was open for 3% -> 3% of each run, Pallas kernels for 23% -> 25%
where the time goes in v2:
time: 97.6 us; the launch traced here: 97 us
  Pallas kernels  41.2 us (42%)
  starting transfers between devices  25.6 us (26%)
  waiting for transfers between devices  25.6 us (26%)
  other arithmetic  2.15 us (2%)
  local copies, waits for them, and re-layouts  2.11 us (2%)
    ppermute x8, waiting for transfers between devices, across(): return lax.ppermute(x, axis, [(i, i ^ bits) for i in range(count)])  14.9 us
    ppermute x8, starting transfers between devices, across(): return lax.ppermute(x, axis, [(i, i ^ bits) for i in range(count)])  12.5 us
    ppermute x1, waiting for transfers between devices, shards(): lax.ppermute(priors, both, [(i, i ^ 4 * sectors + 8) for i in range(count)])  10.8 us
    pallas_call x1, Pallas kernels, analyse(): pl.pallas_call(analyse_kernel, out_shape=jax.ShapeDtypeStruct((FIELDS, WI...  10.7 us
    pallas_call x1, Pallas kernels, forecast_inner(): pl.pallas_call(inner_kernel, out_shape=[jax.ShapeDtypeStruct((BANDS, GROU...  7.97 us
    all_to_all x1, starting transfers between devices, shards(): lax.all_to_all(messages, 'member', split_axis=0, concat_axis=0, tiled=True)  7.75 us
    pallas_call x1, Pallas kernels, pick(): pl.pallas_call(pick_kernel, out_shape=jax.ShapeDtypeStruct((BLOCKS, SHARE...  6.4 us
    pallas_call x1, Pallas kernels, arrange(): pl.pallas_call(arrange_kernel, out_shape=shape, in_specs=[ANY], out_specs...  4.61 us
  transfers between devices with their start and end apart: 12, of which 8 were waited for; matrix products, arithmetic and copies ran while one was open for 3% of the time, Pallas kernels for 25%

profile of v2, /device:TPU:8, one launch (start us, length us, event | category | flops | bytes accessed | tf_op | source)
XLA Modules:
  0.0 97.0 jit_solution(230607809864844607)
XLA Ops:
  0.0 1.8 %pack_edges.1 = (f32[6,4,16,128]{3,2,1,0:T(8,128)}, f32[6,4,16,128]{3,2,1,0:T(8,128)}) custom-call(f32[5,90,16,128]{3,2,1,0:T(8,128)} %bitcast.16, f32[90,128]{1,0:T(8,128)} %depth.5, s32[90,128]{1,0:T(8,128)} %mask.5), custom_call_target="tpu_custom_call" | custom-call | tf_op jit(solution)/shard_map/pack_edges/pallas_call | solution.py:65
  1.9 1.7 %collective-permute-start.1 = (f32[6,4,16,128]{3,2,1,0:T(8,128)}, f32[6,4,16,128]{3,2,1,0:T(8,128)S(1)}, u32[]{:S(2)}, u32[]{:S(2)}) collective-permute-start(f32[6,4,16,128]{3,2,1,0:T(8,128)} %get-tuple-element.17), channel_id=1, source_target_pairs={{1,0},{2,1},{3,2},{4,3},{5,4},{6,5},{7,6},{8,7},{9,8},{10,9},{11,1... | collective-permute-start | bytes 589832 | tf_op jit(solution)/shard_map/ppermute | solution.py:779
  3.6 8.0 %forecast_inner.1 = (f32[8,57,16,128]{3,2,1,0:T(8,128)}, f32[3,90,16,128]{3,2,1,0:T(8,128)}) custom-call(f32[5,90,16,128]{3,2,1,0:T(8,128)} %bitcast.17, f32[90,128]{1,0:T(8,128)} %depth.5, s32[90,128]{1,0:T(8,128)} %mask.5, f32[1,128]{1,0:T(1,128)} %bitcast.25), custom_call_target="tpu_custom_call" | custom-call | tf_op jit(solution)/shard_map/forecast_inner/pallas_call | solution.py:193
  11.7 0.7 copy-done.1
  12.4 4.2 %forecast_outer.1 = (f32[8,57,16,128]{3,2,1,0:T(8,128)}, f32[3,90,16,128]{3,2,1,0:T(8,128)}) custom-call(f32[5,90,16,128]{3,2,1,0:T(8,128)} %bitcast.18, f32[6,4,16,128]{3,2,1,0:T(8,128)} %copy-done.1, f32[6,4,16,128]{3,2,1,0:T(8,128)} %copy-done.2, f32[90,128]{1,0:T(8,128)} %depth.5, s32[90,128]{1,0:T(8,128)} %mask.5, ...), custom_call_target="tpu_custom_call", output_to_operand_aliasing={{0}: (6, {}), {1}: (7, {})} | custom-call | tf_op jit(solution)/shard_map/forecast_outer/pallas_call | solution.py:277
  16.7 7.8 %all-to-all-start = ((f32[8,57,16,128]{3,2,1,0:T(8,128)}), f32[8,57,16,128]{3,2,1,0:T(8,128)}, u32[]{:S(2)}, u32[]{:S(2)}) async-start(f32[8,57,16,128]{3,2,1,0:T(8,128)} %get-tuple-element.24), calls=%async_computation | async-start | bytes 7471104 | tf_op jit(solution)/shard_map/all_to_all | solution.py:796
  24.4 0.6 add_select_fusion
  25.1 0.6 stack.48.facts
  25.7 2.8 %obs_in_batch_order.1.facts = f32[8,8,128]{2,1,0:T(8,128)} custom-call(s32[8,1,128]{2,1,0:T(1,128)} %bitcast.20, f32[8,1024]{1,0:T(8,128)} %stack.48.facts), custom_call_target="tpu_custom_call" | custom-call | tf_op jit(solution)/shard_map/obs_in_batch_order/pallas_call | solution.py:359
  28.5 0.6 pad_add_fusion.place
  29.1 2.7 %list_observations.1 = (bf16[2,2,128,512]{3,2,1,0:T(8,128)(2,1)}, f32[512,512]{1,0:T(8,128)}, f32[2,32,128]{2,1,0:T(8,128)}, s32[1]{0:T(128)}) custom-call(s32[3]{0:T(128)} %pad_add_fusion.place, f32[8,8,128]{2,1,0:T(8,128)} %obs_in_batch_order.1.facts), custom_call_target="tpu_custom_call" | custom-call | tf_op jit(solution)/shard_map/list_observations/pallas_call | solution.py:465
  31.8 6.4 %pick_priors.1 = f32[8,16,128]{2,1,0:T(8,128)} custom-call(s32[1024]{0:T(1024)} %order.1, s32[1024]{0:T(1024)} %get-tuple-element.25.cell, f32[270,16,128]{2,1,0:T(8,128)} %bitcast.19, f32[2,32,128]{2,1,0:T(8,128)} %get-tuple-element.21._.where), custom_call_target="tpu_custom_call" | custom-call | tf_op jit(solution)/shard_map/pick_priors/pallas_call | solution.py:330
  38.2 3.0 %collective-permute-start.2 = (f32[8,16,128]{2,1,0:T(8,128)}, f32[8,16,128]{2,1,0:T(8,128)S(1)}, u32[]{:S(2)}, u32[]{:S(2)}) collective-permute-start(f32[8,16,128]{2,1,0:T(8,128)} %pick_priors.1), channel_id=1, source_target_pairs={{0,2},{1,3},{2,0},{3,1},{4,6},{5,7},{6,4},{7,5},{8,10},{9,11},{10,... | collective-permute-start | bytes 196616 | tf_op jit(solution)/shard_map/ppermute | solution.py:758
  41.3 2.5 %collective-permute-done.2 = f32[8,16,128]{2,1,0:T(8,128)S(1)} collective-permute-done((f32[8,16,128]{2,1,0:T(8,128)}, f32[8,16,128]{2,1,0:T(8,128)S(1)}, u32[]{:S(2)}, u32[]{:S(2)}) %collective-permute-start.2) | collective-permute-done | bytes 65568 | tf_op jit(solution)/shard_map/ppermute | solution.py:758
  43.7 0.9 add.24
  44.6 1.4 %collective-permute-start.3 = (f32[8,16,128]{2,1,0:T(8,128)S(1)}, f32[8,16,128]{2,1,0:T(8,128)S(1)}, u32[]{:S(2)}, u32[]{:S(2)}) collective-permute-start(f32[8,16,128]{2,1,0:T(8,128)S(1)} %add.24), channel_id=1, source_target_pairs={{0,4},{1,5},{2,6},{3,7},{4,0},{5,1},{6,2},{7,3},{8,12},{9,13},{10,... | collective-permute-start | bytes 196616 | tf_op jit(solution)/shard_map/ppermute | solution.py:758
  45.9 4.5 %collective-permute-done.3 = f32[8,16,128]{2,1,0:T(8,128)S(1)} collective-permute-done((f32[8,16,128]{2,1,0:T(8,128)S(1)}, f32[8,16,128]{2,1,0:T(8,128)S(1)}, u32[]{:S(2)}, u32[]{:S(2)}) %collective-permute-start.3) | collective-permute-done | bytes 65568 | tf_op jit(solution)/shard_map/ppermute | solution.py:758
  50.4 0.1 collective-permute-start.4
  50.5 1.2 %collective-permute-done.4 = f32[8,16,128]{2,1,0:T(8,128)S(1)} collective-permute-done((f32[8,16,128]{2,1,0:T(8,128)S(1)}, f32[8,16,128]{2,1,0:T(8,128)S(1)}, u32[]{:S(2)}, u32[]{:S(2)}) %collective-permute-start.4) | collective-permute-done | bytes 65568 | tf_op jit(solution)/shard_map/ppermute | solution.py:758
  51.8 0.6 collective-permute-start.5
  52.4 3.5 %collective-permute-start.7 = (f32[8,16,128]{2,1,0:T(8,128)S(1)}, f32[8,16,128]{2,1,0:T(8,128)S(1)}, u32[]{:S(2)}, u32[]{:S(2)}) collective-permute-start(f32[8,16,128]{2,1,0:T(8,128)S(1)} %add.26), channel_id=1, source_target_pairs={{0,72},{1,73},{2,74},{3,75},{4,76},{5,77},{6,78},{7,79},{8,64},{9,... | collective-permute-start | bytes 196616 | tf_op jit(solution)/shard_map/ppermute | solution.py:803
  55.9 0.6 collective-permute-start.6
  56.5 1.9 %collective-permute-done.5 = f32[8,16,128]{2,1,0:T(8,128)S(1)} collective-permute-done((f32[8,16,128]{2,1,0:T(8,128)S(1)}, f32[8,16,128]{2,1,0:T(8,128)S(1)}, u32[]{:S(2)}, u32[]{:S(2)}) %collective-permute-start.5) | collective-permute-done | bytes 65568 | tf_op jit(solution)/shard_map/ppermute | solution.py:758
  58.5 10.8 %collective-permute-done.7 = f32[8,16,128]{2,1,0:T(8,128)S(1)} collective-permute-done((f32[8,16,128]{2,1,0:T(8,128)S(1)}, f32[8,16,128]{2,1,0:T(8,128)S(1)}, u32[]{:S(2)}, u32[]{:S(2)}) %collective-permute-start.7) | collective-permute-done | bytes 65568 | tf_op jit(solution)/shard_map/ppermute | solution.py:803
  69.2 2.5 %collective-permute-done.6 = f32[8,16,128]{2,1,0:T(8,128)S(1)} collective-permute-done((f32[8,16,128]{2,1,0:T(8,128)S(1)}, f32[8,16,128]{2,1,0:T(8,128)S(1)}, u32[]{:S(2)}, u32[]{:S(2)}) %collective-permute-start.6) | collective-permute-done | bytes 65568 | tf_op jit(solution)/shard_map/ppermute | solution.py:758
  71.7 5.8 %collective-permute-start.10 = (f32[2,8,16,128]{3,2,1,0:T(8,128)S(1)}, f32[2,8,16,128]{3,2,1,0:T(8,128)S(1)}, u32[]{:S(2)}, u32[]{:S(2)}) collective-permute-start(f32[2,8,16,128]{3,2,1,0:T(8,128)S(1)} %pad_maximum_fusion.p0), channel_id=1, source_target_pairs={{0,48},{16,32},{32,16},{48,0},{64,112},{80,96},{96,80},{112,64},{1... | collective-permute-start | bytes 393224 | tf_op jit(solution)/shard_map/ppermute | solution.py:758
  77.5 0.9 collective-permute-start.8
  78.5 4.6 %arrange_members.1.given = bf16[57,8,16,256]{3,2,1,0:T(8,128)(2,1)} custom-call(f32[8,57,16,128]{3,2,1,0:T(8,128)} %all-to-all-done.parts), custom_call_target="tpu_custom_call" | custom-call | tf_op jit(solution)/shard_map/arrange_members/pallas_call | solution.py:509
  83.1 1.1 %collective-permute-done.10.p3 = f32[2,8,16,128]{3,2,1,0:T(8,128)S(1)} collective-permute-done((f32[2,8,16,128]{3,2,1,0:T(8,128)S(1)}, f32[2,8,16,128]{3,2,1,0:T(8,128)S(1)}, u32[]{:S(2)}, u32[]{:S(2)}) %collective-permute-start.10) | collective-permute-done | bytes 131104 | tf_op jit(solution)/shard_map/ppermute | solution.py:758
  84.2 1.2 %collective-permute-done.9.p2 = f32[2,8,16,128]{3,2,1,0:T(8,128)S(1)} collective-permute-done((f32[2,8,16,128]{3,2,1,0:T(8,128)S(1)}, f32[2,8,16,128]{3,2,1,0:T(8,128)S(1)}, u32[]{:S(2)}, u32[]{:S(2)}) %collective-permute-start.9) | collective-permute-done | bytes 131104 | tf_op jit(solution)/shard_map/ppermute | solution.py:758
  85.4 0.6 copy-done.4
  86.1 10.7 %analyse.1 = f32[5,90,16,128]{3,2,1,0:T(8,128)} custom-call(s32[3]{0:T(128)} %pad_add_fusion.place, s32[1]{0:T(128)} %get-tuple-element.15.many, f32[2,8,16,128]{3,2,1,0:T(8,128)} %copy-done, f32[2,8,16,128]{3,2,1,0:T(8,128)} %copy-done.5, f32[2,8,16,128]{3,2,1,0:T(8,128)} %copy-done.4, f32[2,8,16,128]{3,2,1,0:T(8,128)} %copy-done.3, ...), custom_call_target="tpu_custom_call" | custom-call | tf_op jit(solution)/shard_map/analyse/pallas_call | solution.py:729
  (32 shorter events, 0.3 us)
Async XLA Ops:
  1.8 9.8 %collective-permute-start = (f32[6,4,16,128]{3,2,1,0:T(8,128)}, f32[6,4,16,128]{3,2,1,0:T(8,128)S(1)}, u32[]{:S(2)}, u32[]{:S(2)}) collective-permute-start(f32[6,4,16,128]{3,2,1,0:T(8,128)} %get-tuple-element.16), channel_id=1, source_target_pairs={{0,1},{1,2},{2,3},{3,4},{4,5},{5,6},{6,7},{7,8},{8,9},{9,10},{10,1... | collective-permute-start | bytes 589832 | tf_op jit(solution)/shard_map/ppermute | solution.py:778
  1.9 9.7 %collective-permute-start.1 = (f32[6,4,16,128]{3,2,1,0:T(8,128)}, f32[6,4,16,128]{3,2,1,0:T(8,128)S(1)}, u32[]{:S(2)}, u32[]{:S(2)}) collective-permute-start(f32[6,4,16,128]{3,2,1,0:T(8,128)} %get-tuple-element.17), channel_id=1, source_target_pairs={{1,0},{2,1},{3,2},{4,3},{5,4},{6,5},{7,6},{8,7},{9,8},{10,9},{11,1... | collective-permute-start | bytes 589832 | tf_op jit(solution)/shard_map/ppermute | solution.py:779
  11.6 0.7 copy-start.1
  11.6 0.7 copy-start.2
  16.6 7.8 %copy-start.6 = (s32[1024]{0:T(1024)S(1)}, s32[1024]{0:T(1024)}, u32[]{:S(2)}) copy-start(s32[1024]{0:T(1024)} %param.17) | copy-start | bytes 12292
  16.6 7.8 %copy-start.7 = (s32[1024]{0:T(1024)S(1)}, s32[1024]{0:T(1024)}, u32[]{:S(2)}) copy-start(s32[1024]{0:T(1024)} %param.18) | copy-start | bytes 12292
  16.6 7.8 %copy-start.8 = (s32[1024]{0:T(1024)S(1)}, s32[1024]{0:T(1024)}, u32[]{:S(2)}) copy-start(s32[1024]{0:T(1024)} %param.16) | copy-start | bytes 12292
  16.6 8.4 %copy-start.9 = (f32[1024]{0:T(1024)S(1)}, f32[1024]{0:T(1024)}, u32[]{:S(2)}) copy-start(f32[1024]{0:T(1024)} %param.14) | copy-start | bytes 12292
  16.6 8.4 %copy-start.10 = (f32[1024]{0:T(1024)S(1)}, f32[1024]{0:T(1024)}, u32[]{:S(2)}) copy-start(f32[1024]{0:T(1024)} %param.15) | copy-start | bytes 12292
  16.7 61.8 %all-to-all-start = ((f32[8,57,16,128]{3,2,1,0:T(8,128)}), f32[8,57,16,128]{3,2,1,0:T(8,128)}, u32[]{:S(2)}, u32[]{:S(2)}) async-start(f32[8,57,16,128]{3,2,1,0:T(8,128)} %get-tuple-element.24), calls=%async_computation | async-start | bytes 7471104 | tf_op jit(solution)/shard_map/all_to_all | solution.py:796
  38.2 5.5 %collective-permute-start.2 = (f32[8,16,128]{2,1,0:T(8,128)}, f32[8,16,128]{2,1,0:T(8,128)S(1)}, u32[]{:S(2)}, u32[]{:S(2)}) collective-permute-start(f32[8,16,128]{2,1,0:T(8,128)} %pick_priors.1), channel_id=1, source_target_pairs={{0,2},{1,3},{2,0},{3,1},{4,6},{5,7},{6,4},{7,5},{8,10},{9,11},{10,... | collective-permute-start | bytes 196616 | tf_op jit(solution)/shard_map/ppermute | solution.py:758
  44.6 5.8 %collective-permute-start.3 = (f32[8,16,128]{2,1,0:T(8,128)S(1)}, f32[8,16,128]{2,1,0:T(8,128)S(1)}, u32[]{:S(2)}, u32[]{:S(2)}) collective-permute-start(f32[8,16,128]{2,1,0:T(8,128)S(1)} %add.24), channel_id=1, source_target_pairs={{0,4},{1,5},{2,6},{3,7},{4,0},{5,1},{6,2},{7,3},{8,12},{9,13},{10,... | collective-permute-start | bytes 196616 | tf_op jit(solution)/shard_map/ppermute | solution.py:758
  50.4 1.3 %collective-permute-start.4 = (f32[8,16,128]{2,1,0:T(8,128)S(1)}, f32[8,16,128]{2,1,0:T(8,128)S(1)}, u32[]{:S(2)}, u32[]{:S(2)}) collective-permute-start(f32[8,16,128]{2,1,0:T(8,128)S(1)} %add.25), channel_id=1, source_target_pairs={{0,1},{1,0},{2,3},{3,2},{4,5},{5,4},{6,7},{7,6},{8,9},{9,8},{10,11... | collective-permute-start | bytes 196616 | tf_op jit(solution)/shard_map/ppermute | solution.py:758
  51.8 6.7 %collective-permute-start.5 = (f32[8,16,128]{2,1,0:T(8,128)S(1)}, f32[8,16,128]{2,1,0:T(8,128)S(1)}, u32[]{:S(2)}, u32[]{:S(2)}) collective-permute-start(f32[8,16,128]{2,1,0:T(8,128)S(1)} %add.26), channel_id=1, source_target_pairs={{0,8},{1,9},{2,10},{3,11},{4,12},{5,13},{6,14},{7,15},{8,0},{9,1},... | collective-permute-start | bytes 196616 | tf_op jit(solution)/shard_map/ppermute | solution.py:758
  52.4 16.8 %collective-permute-start.7 = (f32[8,16,128]{2,1,0:T(8,128)S(1)}, f32[8,16,128]{2,1,0:T(8,128)S(1)}, u32[]{:S(2)}, u32[]{:S(2)}) collective-permute-start(f32[8,16,128]{2,1,0:T(8,128)S(1)} %add.26), channel_id=1, source_target_pairs={{0,72},{1,73},{2,74},{3,75},{4,76},{5,77},{6,78},{7,79},{8,64},{9,... | collective-permute-start | bytes 196616 | tf_op jit(solution)/shard_map/ppermute | solution.py:803
  55.9 15.7 %collective-permute-start.6 = (f32[8,16,128]{2,1,0:T(8,128)S(1)}, f32[8,16,128]{2,1,0:T(8,128)S(1)}, u32[]{:S(2)}, u32[]{:S(2)}) collective-permute-start(f32[8,16,128]{2,1,0:T(8,128)S(1)} %add.26), channel_id=1, source_target_pairs={{0,64},{16,80},{32,96},{48,112},{64,0},{80,16},{96,32},{112,48},{1... | collective-permute-start | bytes 196616 | tf_op jit(solution)/shard_map/ppermute | solution.py:758
  71.7 13.7 %copy-start = (f32[2,8,16,128]{3,2,1,0:T(8,128)}, f32[2,8,16,128]{3,2,1,0:T(8,128)S(1)}, u32[]{:S(2)}) copy-start(f32[2,8,16,128]{3,2,1,0:T(8,128)S(1)} %pad_maximum_fusion.p0) | copy-start | bytes 393220
  71.7 12.5 %collective-permute-start.10 = (f32[2,8,16,128]{3,2,1,0:T(8,128)S(1)}, f32[2,8,16,128]{3,2,1,0:T(8,128)S(1)}, u32[]{:S(2)}, u32[]{:S(2)}) collective-permute-start(f32[2,8,16,128]{3,2,1,0:T(8,128)S(1)} %pad_maximum_fusion.p0), channel_id=1, source_target_pairs={{0,48},{16,32},{32,16},{48,0},{64,112},{80,96},{96,80},{112,64},{1... | collective-permute-start | bytes 393224 | tf_op jit(solution)/shard_map/ppermute | solution.py:758
  77.5 7.9 %collective-permute-start.9 = (f32[2,8,16,128]{3,2,1,0:T(8,128)S(1)}, f32[2,8,16,128]{3,2,1,0:T(8,128)S(1)}, u32[]{:S(2)}, u32[]{:S(2)}) collective-permute-start(f32[2,8,16,128]{3,2,1,0:T(8,128)S(1)} %pad_maximum_fusion.p0), channel_id=1, source_target_pairs={{0,32},{16,48},{32,0},{48,16},{64,96},{80,112},{96,64},{112,80},{1... | collective-permute-start | bytes 393224 | tf_op jit(solution)/shard_map/ppermute | solution.py:758
  77.5 7.9 %collective-permute-start.8 = (f32[2,8,16,128]{3,2,1,0:T(8,128)S(1)}, f32[2,8,16,128]{3,2,1,0:T(8,128)S(1)}, u32[]{:S(2)}, u32[]{:S(2)}) collective-permute-start(f32[2,8,16,128]{3,2,1,0:T(8,128)S(1)} %pad_maximum_fusion.p0), channel_id=1, source_target_pairs={{0,16},{16,0},{32,48},{48,32},{64,80},{80,64},{96,112},{112,96},{1... | collective-permute-start | bytes 393224 | tf_op jit(solution)/shard_map/ppermute | solution.py:758
  84.2 1.2 %copy-start.3 = (f32[2,8,16,128]{3,2,1,0:T(8,128)}, f32[2,8,16,128]{3,2,1,0:T(8,128)S(1)}, u32[]{:S(2)}) copy-start(f32[2,8,16,128]{3,2,1,0:T(8,128)S(1)} %collective-permute-done.10.p3) | copy-start | bytes 393220
  85.4 0.6 copy-start.4
  85.4 0.7 copy-start.5

commit v3 on v2

--- a/solution.py
+++ b/solution.py
@@ -17,17 +17,16 @@
 BANDS = 8
 WIDTH = 90
 EDGE = 4
-INNER = 9
+INNER = 10
+REST_AT = EDGE + 8 * INNER
+INSIDE = FIELDS * INNER + 2
+GROUPS = INSIDE + FIELDS
 RIGHT = 80
-INSIDE = FIELDS * INNER
-OUTSIDE = 2 * FIELDS + 2
-GROUPS = INSIDE + OUTSIDE
-SETS = (GROUPS + 7) // 8
-CUT = 48
+SETS = (INSIDE + 7) // 8
+CUT = 44
 SLOTS = 128
 CHUNKS = BATCH // SLOTS
 MEAN = SLOTS - 1
-FLOW, REST = 39, 38
 SCALE = 1.0 / (RADIUS * RADIUS)
 F32 = jnp.float32
 BF16 = jnp.bfloat16
@@ -148,33 +147,35 @@
 
 
 def inner_kernel(ens, depth, mask, vort, out, seen, now, nxt, flux, sea, band, made, sems):
-    span = INNER * 8
-    first = FLOW + 2
+    half = WIDTH // 2
     loads = [
-        pltpu.make_async_copy(
-            ens.at[:, pl.ds(EDGE + at, n)], now.at[:, pl.ds(at, n)], sems.at[2 + i]
-        )
-        for i, (at, n) in enumerate(((0, first), (first, span + 2 * EDGE - first)))
+        pltpu.make_async_copy(ens.at[:, pl.ds(at, n)], now.at[:, pl.ds(at, n)], sems.at[2 + i])
+        for i, (at, n) in enumerate(((0, half + 1), (half + 1, half - 1)))
     ]
     for c in loads:
         c.start()
     sea[...] = mask[...].astype(F32)
     bands(band)
     flow, others = stepper(depth, sea, vort, flux, band)
-    for at, c in zip((1, 1 + FLOW), loads):
+    for at, c in zip((1, half), loads):
         c.wait()
-        flow(now, nxt, [(at + k, at + k + EDGE) for k in range(FLOW)])
-    in_blocks(others, now, nxt, 2, span + 6, EDGE, REST)
-    in_blocks(flow, nxt, now, 3, span + 5, EDGE, FLOW)
-    in_blocks(others, nxt, now, 4, span + 4, EDGE, REST)
+        flow(now, nxt, [(at + k, at + k) for k in range(half - 1)])
+    for d, stage, src, dst in ((2, others, now, nxt), (3, flow, nxt, now), (4, others, nxt, now)):
+        in_blocks(stage, src, dst, d, WIDTH - d, 0, half - d)
     keep = pltpu.make_async_copy(
-        now.at[pl.ds(2, 3), pl.ds(EDGE, span)], seen.at[:, pl.ds(8, span)], sems.at[1]
+        now.at[pl.ds(2, 3), pl.ds(EDGE, WIDTH - 2 * EDGE)],
+        seen.at[:, pl.ds(EDGE, WIDTH - 2 * EDGE)],
+        sems.at[1],
     )
     keep.start()
 
     def send(f):
-        at = pl.ds(f * INNER, INNER)
+        at = pl.ds(f * INNER, INNER if isinstance(f, jax.Array) or f < FIELDS else 2)
         return pltpu.make_async_copy(made.at[:, at], out.at[:, at], sems.at[2 + f])
+
+    turn(now[pl.ds(0, 4), pl.ds(REST_AT, 2)], made, INSIDE - 2)
+    turn(jnp.concatenate([now[4, pl.ds(REST_AT, 2)]] * 4, axis=0), made, INSIDE - 1)
+    send(FIELDS).start()
 
     def field(f, _):
         for i in range(INNER):
@@ -183,29 +184,28 @@
         return 0
 
     lax.fori_loop(0, FIELDS, field, 0)
-    for f in range(FIELDS):
+    for f in range(FIELDS + 1):
         send(f).wait()
     keep.wait()
 
 
 def forecast_inner(ens, depth, mask, vort):
-    window = INNER * 8 + 2 * EDGE
     return pl.pallas_call(
         inner_kernel,
         out_shape=[
-            jax.ShapeDtypeStruct((BANDS, GROUPS, SHARE, LAT), F32),
+            jax.ShapeDtypeStruct((BANDS, INSIDE, SHARE, LAT), F32),
             jax.ShapeDtypeStruct((3, WIDTH, SHARE, LAT), F32),
         ],
         in_specs=[ANY, VMEM, VMEM, VMEM],
         out_specs=[ANY, ANY],
         scratch_shapes=[
-            pltpu.VMEM((FIELDS, window, SHARE, LAT), F32),
-            pltpu.VMEM((FIELDS, window, SHARE, LAT), F32),
-            pltpu.VMEM((window, SHARE, LAT), F32),
+            pltpu.VMEM((FIELDS, WIDTH, SHARE, LAT), F32),
+            pltpu.VMEM((FIELDS, WIDTH, SHARE, LAT), F32),
+            pltpu.VMEM((WIDTH, SHARE, LAT), F32),
             pltpu.VMEM((WIDTH, LAT), F32),
             pltpu.VMEM((2 * LAT, 2 * LAT), BF16),
             pltpu.VMEM((BANDS, INSIDE, SHARE, LAT), F32),
-            pltpu.SemaphoreType.DMA((2 + FIELDS,)),
+            pltpu.SemaphoreType.DMA((3 + FIELDS,)),
         ],
         compiler_params=PARAMS,
         name="forecast_inner",
@@ -213,32 +213,32 @@
 
 
 def outer_kernel(
-    ens, left, right, depth, mask, vort, _, _2, out, seen, now, nxt, flux, dep, sea, band, made, sems
+    ens, left, right, depth, mask, vort, _, out, seen, now, nxt, flux, dep, sea, band, made, sems
 ):
-    near, far = 3 * EDGE, 3 * EDGE + 2
-    second = near + EDGE
+    own = 2 * EDGE
+    second = own + EDGE
     loads = [
-        pltpu.make_async_copy(ens.at[:, pl.ds(0, near)], now.at[:, pl.ds(EDGE, near)], sems.at[0]),
+        pltpu.make_async_copy(ens.at[:, pl.ds(0, own)], now.at[:, pl.ds(EDGE, own)], sems.at[0]),
         pltpu.make_async_copy(
-            ens.at[:, pl.ds(WIDTH - far, far)], now.at[:, pl.ds(second, far)], sems.at[1]
+            ens.at[:, pl.ds(WIDTH - own, own)], now.at[:, pl.ds(second, own)], sems.at[1]
         ),
         pltpu.make_async_copy(left.at[pl.ds(0, FIELDS)], now.at[:, pl.ds(0, EDGE)], sems.at[2]),
         pltpu.make_async_copy(
-            right.at[pl.ds(0, FIELDS)], now.at[:, pl.ds(second + far, EDGE)], sems.at[3]
+            right.at[pl.ds(0, FIELDS)], now.at[:, pl.ds(second + own, EDGE)], sems.at[3]
         ),
     ]
     for c in loads:
         c.start()
-    for grid, own, at in ((dep, depth, 0), (sea, mask, EDGE)):
-        grid[pl.ds(8, WIDTH), :] = own[...].astype(F32)
+    for grid, whole, at in ((dep, depth, 0), (sea, mask, EDGE)):
+        grid[pl.ds(8, WIDTH), :] = whole[...].astype(F32)
         grid[pl.ds(4, EDGE), :] = left[FIELDS, 0, pl.ds(at, EDGE), :]
         grid[pl.ds(8 + WIDTH, EDGE), :] = right[FIELDS, 0, pl.ds(at, EDGE), :]
     bands(band)
     flow, others = stepper(dep, sea, vort, flux, band)
     for c in loads:
         c.wait()
-    end = second + far + EDGE
-    skip = 8 + WIDTH - far - second
+    end = second + own + EDGE
+    skip = 8 + WIDTH - own - second
     for d, stage, src, dst in (
         (1, flow, now, nxt),
         (2, others, now, nxt),
@@ -247,41 +247,31 @@
     ):
         places = [(e, e + 4) for e in range(d, second - d)]
         stage(src, dst, places + [(e, e + skip) for e in range(second + d, end - d)])
-    right_at = second + EDGE
     keeps = [
         pltpu.make_async_copy(
-            now.at[pl.ds(2, 3), pl.ds(EDGE, 8)], seen.at[:, pl.ds(0, 8)], sems.at[1]
-        ),
-        pltpu.make_async_copy(
-            now.at[pl.ds(2, 3), pl.ds(right_at, WIDTH - RIGHT)],
-            seen.at[:, pl.ds(RIGHT, WIDTH - RIGHT)],
-            sems.at[2],
-        ),
+            now.at[pl.ds(2, 3), pl.ds(at, EDGE)], seen.at[:, pl.ds(lon, EDGE)], sems.at[i]
+        )
+        for i, (at, lon) in enumerate(((EDGE, 0), (second + EDGE, WIDTH - EDGE)))
     ]
     for c in keeps:
         c.start()
     for f in range(FIELDS):
-        turn(now[f, pl.ds(EDGE, 8)], made, 2 * f)
-        turn(now[f, pl.ds(right_at, 8)], made, 2 * f + 1)
-    turn(now[pl.ds(0, 4), pl.ds(right_at + 8, 2)], made, 2 * FIELDS)
-    last = now[4, pl.ds(right_at + 8, 2)]
-    turn(jnp.concatenate([last] * 4, axis=0), made, 2 * FIELDS + 1)
-    send = pltpu.make_async_copy(made, out.at[:, pl.ds(INSIDE, OUTSIDE)], sems.at[0])
+        sides = [now[f, pl.ds(EDGE, EDGE)], now[f, pl.ds(second + EDGE, EDGE)]]
+        turn(jnp.concatenate(sides, axis=0), made, f)
+    send = pltpu.make_async_copy(made, out, sems.at[2])
     send.start()
     for c in [send] + keeps:
         c.wait()
 
 
-def forecast_outer(ens, left, right, depth, mask, vort, messages, seen):
-    window = 6 * EDGE + 2 + 2 * EDGE
+def forecast_outer(ens, left, right, depth, mask, vort, seen):
+    window = 6 * EDGE
+    messages = jax.ShapeDtypeStruct((BANDS, FIELDS, SHARE, LAT), F32)
     return pl.pallas_call(
         outer_kernel,
-        out_shape=[
-            jax.ShapeDtypeStruct(messages.shape, F32),
-            jax.ShapeDtypeStruct(seen.shape, F32),
-        ],
-        in_specs=[ANY] + [VMEM] * 5 + [ANY] * 2,
-        out_specs=[ANY, ANY],
+        out_shape=[messages, jax.ShapeDtypeStruct(seen.shape, F32)],
+        in_specs=[ANY] + [VMEM] * 5 + [ANY],
+        out_specs=[ANY] * 2,
         scratch_shapes=[
             pltpu.VMEM((FIELDS, window, SHARE, LAT), F32),
             pltpu.VMEM((FIELDS, window, SHARE, LAT), F32),
@@ -289,13 +279,13 @@
             pltpu.VMEM((112, LAT), F32),
             pltpu.VMEM((112, LAT), F32),
             pltpu.VMEM((2 * LAT, 2 * LAT), BF16),
-            pltpu.VMEM((BANDS, OUTSIDE, SHARE, LAT), F32),
+            pltpu.VMEM((BANDS, FIELDS, SHARE, LAT), F32),
             pltpu.SemaphoreType.DMA((4,)),
         ],
-        input_output_aliases={6: 0, 7: 1},
+        input_output_aliases={6: 1},
         compiler_params=PARAMS,
         name="forecast_outer",
-    )(ens, left, right, depth, mask, vort, messages, seen)
+    )(ens, left, right, depth, mask, vort, seen)
 
 
 def pick_kernel(order, cell, seen, _, out, own):
@@ -477,8 +467,19 @@
     )(place, facts)
 
 
+def members_to_lanes(state, g, n, mid, halves):
+    for s in range(8):
+        tile = jnp.transpose(state[s, pl.ds(g, 8)].reshape(8 * SHARE, LAT))
+        for j in range(8):
+            mid[j, pl.ds(s * SHARE, SHARE), :] = tile[j * SHARE : (j + 1) * SHARE]
+    for j in range(8):
+        pair = jnp.concatenate(split(jnp.transpose(mid[j])), axis=1)
+        for i in range(n):
+            halves(i, j, pair[i * SHARE : (i + 1) * SHARE])
+
+
 def arrange_kernel(parts, out, state, mid, halves, sems, stores):
-    sets = [(g, min(8, GROUPS - g)) for g in range(0, GROUPS, 8)]
+    sets = [(g, min(8, INSIDE - g)) for g in range(0, INSIDE, 8)]
     loads = [
         pltpu.make_async_copy(parts.at[:, pl.ds(g, n)], state.at[:, pl.ds(g, n)], sems.at[t])
         for t, (g, n) in enumerate(sets)
@@ -488,14 +489,11 @@
     saves = []
     for t, (g, n) in enumerate(sets):
         loads[t].wait()
-        for s in range(8):
-            tile = jnp.transpose(state[s, pl.ds(g, 8)].reshape(8 * SHARE, LAT))
-            for j in range(8):
-                mid[j, pl.ds(s * SHARE, SHARE), :] = tile[j * SHARE : (j + 1) * SHARE]
-        for j in range(8):
-            pair = jnp.concatenate(split(jnp.transpose(mid[j])), axis=1)
-            for i in range(n):
-                halves[g + i, j] = pair[i * SHARE : (i + 1) * SHARE]
+
+        def put(i, j, pair):
+            halves[g + i, j] = pair
+
+        members_to_lanes(state, g, n, mid, put)
         saves.append(
             pltpu.make_async_copy(halves.at[pl.ds(g, n)], out.at[pl.ds(g, n)], stores.at[t])
         )
@@ -505,7 +503,7 @@
 
 
 def arrange(parts):
-    shape = jax.ShapeDtypeStruct((GROUPS, 8, SHARE, 2 * MEMBERS), BF16)
+    shape = jax.ShapeDtypeStruct((INSIDE, 8, SHARE, 2 * MEMBERS), BF16)
     return pl.pallas_call(
         arrange_kernel,
         out_shape=shape,
@@ -524,8 +522,8 @@
 
 
 def analyse_kernel(
-    place, many, p0, p1, p2, p3, facts, where, hots_in, taper_in, given, out,
-    hots, taper, state, table, lead, link, gain, shapes, made, big, long_lead, long_gain, long_where, sems, stores,
+    place, many, p0, p1, p2, p3, facts, where, hots_in, taper_in, given, given_edges, out,
+    hots, taper, state, edges, mid, table, lead, link, gain, shapes, made, big, long_lead, long_gain, long_where, sems, stores,
 ):
     loads = [
         pltpu.make_async_copy(taper_in, taper, sems.at[FIELDS + 1]),
@@ -536,9 +534,10 @@
         at = pl.ds(f * INNER, INNER)
         return pltpu.make_async_copy(given.at[at], state.at[at], sems.at[f])
 
-    at = pl.ds(INSIDE, OUTSIDE)
-    outside = pltpu.make_async_copy(given.at[at], state.at[at], sems.at[FIELDS])
-    for c in loads + [outside] + [inside(f) for f in range(FIELDS)]:
+    at = pl.ds(FIELDS * INNER, 2)
+    tail = pltpu.make_async_copy(given.at[at], state.at[at], sems.at[FIELDS])
+    sides = pltpu.make_async_copy(given_edges, edges.at[:, pl.ds(0, FIELDS)], sems.at[FIELDS + 3])
+    for c in loads + [sides, tail] + [inside(f) for f in range(FIELDS)]:
         c.start()
 
     me = place[2]
@@ -598,7 +597,12 @@
         two = dot_nt(h2, s2[0]) + dot_nt(h2, s2[1])
         link[q] = paired(*split(exact(one, two, ((1,), (1,)))))
 
-    outside.wait()
+    def put_edge(i, j, pair):
+        state[INSIDE + i, j] = pair
+
+    sides.wait()
+    members_to_lanes(edges, 0, FIELDS, mid, put_edge)
+    tail.wait()
 
     def times(pair, m):
         got = jnp.dot(pair, m, preferred_element_type=F32)
@@ -621,9 +625,15 @@
         cov = cov + product(t * cov, link[q])
         return both_roots * whole(pair) + product(t * cov, gain[q])
 
-    def block(g, n, lons=8):
-        pair = state[pl.ds(g, n)] if lons == 8 else state[g, pl.ds(0, lons)]
-        return pair.reshape(n * lons * SHARE, 2 * MEMBERS)
+    def block(g, n):
+        return state[pl.ds(g, n)].reshape(n * 8 * SHARE, 2 * MEMBERS)
+
+    def part(g, at, n):
+        return state[g, pl.ds(at, n)].reshape(n * SHARE, 2 * MEMBERS)
+
+    def put_rest(x):
+        for f in range(FIELDS):
+            put(f, REST_AT, x[f * 2 * SHARE : (f + 1) * 2 * SHARE], 2)
 
     def put(f, lon, x, n):
         made[f, pl.ds(lon, n)] = x.reshape(n, SHARE, MEMBERS)
@@ -640,26 +650,28 @@
         def shape(lon, n):
             return shapes[pl.ds(lon, n)].reshape(n * SHARE, SLOTS)
 
-        x = short(block(GROUPS - 2, 1), jnp.concatenate([shape(RIGHT + 8, 2)] * 4, axis=0), 1)
-        for f in range(4):
-            put(f, RIGHT + 8, x[f * 2 * SHARE : (f + 1) * 2 * SHARE], 2)
-        put(4, RIGHT + 8, short(block(GROUPS - 1, 1, 2), shape(RIGHT + 8, 2), 1), 2)
+        pair = jnp.concatenate([block(INSIDE - 2, 1), part(INSIDE - 1, 0, 2)], axis=0)
+        put_rest(short(pair, jnp.concatenate([shape(REST_AT, 2)] * FIELDS, axis=0), 1))
 
         def some(fs):
             for f in fs:
                 inside(f).wait()
-            for q, lo, n, edge in ((0, 0, 5, 0), (1, 5, 4, RIGHT)):
-                lon = 8 * (lo + 1)
+            n = INNER // 2
+            for q, lon, edge in ((0, EDGE, 0), (1, CUT, WIDTH - EDGE)):
                 pair = jnp.concatenate(
-                    [a for f in fs for a in (block(f * INNER + lo, n), block(INSIDE + 2 * f + q, 1))],
+                    [
+                        a
+                        for f in fs
+                        for a in (block(f * INNER + q * n, n), part(INSIDE + f, q * EDGE, EDGE))
+                    ],
                     axis=0,
                 )
-                t = jnp.concatenate([shape(lon, 8 * n), shape(edge, 8)] * len(fs), axis=0)
+                t = jnp.concatenate([shape(lon, 8 * n), shape(edge, EDGE)] * len(fs), axis=0)
                 x = short(pair, t, q)
-                r = 8 * (n + 1) * SHARE
+                r, m = (8 * n + EDGE) * SHARE, 8 * n * SHARE
                 for i, f in enumerate(fs):
-                    put(f, lon, x[i * r : i * r + 8 * n * SHARE], 8 * n)
-                    put(f, edge, x[i * r + 8 * n * SHARE : (i + 1) * r], 8)
+                    put(f, lon, x[i * r : i * r + m], 8 * n)
+                    put(f, edge, x[i * r + m : (i + 1) * r], EDGE)
             for f in fs:
                 store(f).start()
 
@@ -703,20 +715,19 @@
             return x
 
         def each(g, _):
-            inner = g < INSIDE
-            h = g - INSIDE
-            f = jnp.where(inner, g // INNER, h // 2)
-            lon = jnp.where(inner, 8 * (g % INNER + 1), RIGHT * (h % 2))
+            f, lon = g // INNER, 8 * (g % INNER) + EDGE
             at = lon.astype(F32)
             put(f, lon, long(block(g, 1), [at + j for j in range(8)]), 8)
             return 0
 
-        lax.fori_loop(0, GROUPS - 2, each, 0)
-        tail = [float(RIGHT + 8 + j % 2) for j in range(8)]
-        x = long(block(GROUPS - 2, 1), tail)
-        for f in range(4):
-            put(f, RIGHT + 8, x[f * 2 * SHARE : (f + 1) * 2 * SHARE], 2)
-        put(4, RIGHT + 8, long(block(GROUPS - 1, 1, 2), tail[:2]), 2)
+        lax.fori_loop(0, FIELDS * INNER, each, 0)
+        last = long(part(INSIDE - 1, 0, 2), [float(REST_AT + j) for j in range(2)])
+        first = long(block(INSIDE - 2, 1), [float(REST_AT + j % 2) for j in range(8)])
+        put_rest(jnp.concatenate([first, last], axis=0))
+        for f in range(FIELDS):
+            for at, lon in ((0, 0), (EDGE, WIDTH - EDGE)):
+                lons = [float(lon + j) for j in range(EDGE)]
+                put(f, lon, long(part(INSIDE + f, at, EDGE), lons), EDGE)
         for f in range(FIELDS):
             store(f).start()
 
@@ -724,17 +735,19 @@
         store(f).wait()
 
 
-def analyse(place, many, priors, facts, where, hots, taper, state):
+def analyse(place, many, priors, facts, where, hots, taper, state, sides):
     square = (2 * SLOTS, 2 * MEMBERS)
     return pl.pallas_call(
         analyse_kernel,
         out_shape=jax.ShapeDtypeStruct((FIELDS, WIDTH, SHARE, MEMBERS), F32),
-        in_specs=[SMEM] * 2 + [VMEM] * 6 + [ANY] * 3,
+        in_specs=[SMEM] * 2 + [VMEM] * 6 + [ANY] * 4,
         out_specs=ANY,
         scratch_shapes=[
             pltpu.VMEM(hots.shape, BF16),
             pltpu.VMEM(taper.shape, F32),
-            pltpu.VMEM(state.shape, BF16),
+            pltpu.VMEM((GROUPS,) + state.shape[1:], BF16),
+            pltpu.VMEM((BANDS, 8, SHARE, LAT), F32),
+            pltpu.VMEM((8, MEMBERS, LAT), F32),
             pltpu.VMEM((MEMBERS, NOBS), F32),
             pltpu.VMEM((2,) + square, BF16),
             pltpu.VMEM((2,) + square, BF16),
@@ -745,12 +758,12 @@
             pltpu.VMEM((2, CHUNKS) + square, BF16),
             pltpu.VMEM((2, CHUNKS) + square, BF16),
             pltpu.VMEM((2, CHUNKS, SHARE + 16, SLOTS), F32),
-            pltpu.SemaphoreType.DMA((FIELDS + 3,)),
+            pltpu.SemaphoreType.DMA((FIELDS + 4,)),
             pltpu.SemaphoreType.DMA((FIELDS,)),
         ],
         compiler_params=PARAMS,
         name="analyse",
-    )(place, many, *priors, facts, where, hots, taper, state)
+    )(place, many, *priors, facts, where, hots, taper, state, sides)
 
 
 def across(x, axis, bits):
@@ -790,22 +803,19 @@
     hots, taper, where, many = prepare(place, facts)
 
     messages, seen = forecast_inner(ens, ocean_depth, land_mask, vort)
-    messages, seen = forecast_outer(
-        ens, left, right, ocean_depth, land_mask, vort, messages, seen
-    )
     parts = lax.all_to_all(messages, "member", split_axis=0, concat_axis=0, tiled=True)
-
-    priors = pick(obs_order, cell, seen.reshape(3 * WIDTH, SHARE, LAT), where)
-    for bit in (2, 4, 1):
-        priors = priors + across(priors, "sector", bit)
-    both = ("member", "sector")
+    sides, seen = forecast_outer(ens, left, right, ocean_depth, land_mask, vort, seen)
+    sides = lax.all_to_all(sides, "member", split_axis=0, concat_axis=0, tiled=True)
+
+    own = pick(obs_order, cell, seen.reshape(3 * WIDTH, SHARE, LAT), where)
+    own = (own + across(own, "sector", 2)) + (across(own, "sector", 4) + across(own, "sector", 6))
+    own = own + across(own, "sector", 1)
+    axes = ("member", "sector")
     count = lax.axis_size("member") * sectors
-    crossed = lax.ppermute(priors, both, [(i, i ^ (4 * sectors + 8)) for i in range(count)])
-    priors = jnp.stack(
-        [priors + across(priors, "sector", 8), across(priors, "member", 4) + crossed]
-    )
-    priors = [priors] + [across(priors, "member", x) for x in (1, 2, 3)]
-    analysis = analyse(place, many, priors, facts, where, hots, taper, arrange(parts))
+    both = lax.ppermute(own, axes, [(i, i ^ (4 * sectors + 8)) for i in range(count)])
+    own = jnp.stack([own + across(own, "sector", 8), across(own, "member", 4) + both])
+    priors = [own] + [across(own, "member", x) for x in (1, 2, 3)]
+    analysis = analyse(place, many, priors, facts, where, hots, taper, arrange(parts), sides)
     return jnp.transpose(analysis, (0, 2, 1, 3))
 
 

time: 97.6 us -> 95.5 us (0.978)
  waiting for transfers between devices: 25.6 us -> 11.3 us
  starting transfers between devices: 25.6 us -> 36.8 us
  other arithmetic: 2.15 us -> 4.47 us
  local copies, waits for them, and re-layouts: 2.11 us -> 0.69 us
    all_to_all x0 -> x1, starting transfers between devices: none -> 13.3 us  [shards(): lax.all_to_all(sides, 'member', split_axis=0, concat_axis=0, tiled=True)]
    ppermute x1, waiting for transfers between devices: 10.8 us -> 0.01 us  [shards(): lax.ppermute(own, axes, [(i, i ^ 4 * sectors + 8) for i in range(count)])]
    ppermute x8 -> x9, waiting for transfers between devices: 14.9 us -> 10.4 us  [across(): return lax.ppermute(x, axis, [(i, i ^ bits) for i in range(count)])]
    another operation x3, other arithmetic: 0.03 us -> 2.33 us  [shards(): jnp.stack([own + across(own, 'sector', 8), across(own, 'member', 4) + both])]
    ppermute x8 -> x9, starting transfers between devices: 12.5 us -> 11 us  [across(): return lax.ppermute(x, axis, [(i, i ^ bits) for i in range(count)])]
    unnamed x22 -> x14, local copies, waits for them, and re-layouts: 1.46 us -> 0.04 us
  transfers between devices with their start and end apart: 12 -> 14, of which waited for: 8 -> 6; matrix products, arithmetic and copies ran while one was open for 3% -> 5% of each run, Pallas kernels for 25% -> 23%
where the time goes in v3:
time: 95.5 us; the launch traced here: 94.7 us
  Pallas kernels  41.1 us (43%)
  starting transfers between devices  36.8 us (39%)
  waiting for transfers between devices  11.3 us (12%)
  other arithmetic  4.47 us (5%)
    all_to_all x1, starting transfers between devices, shards(): lax.all_to_all(sides, 'member', split_axis=0, concat_axis=0, tiled=True)  13.3 us
    ppermute x9, starting transfers between devices, across(): return lax.ppermute(x, axis, [(i, i ^ bits) for i in range(count)])  11 us
    pallas_call x1, Pallas kernels, analyse(): pl.pallas_call(analyse_kernel, out_shape=jax.ShapeDtypeStruct((FIELDS, WI...  10.7 us
    ppermute x9, waiting for transfers between devices, across(): return lax.ppermute(x, axis, [(i, i ^ bits) for i in range(count)])  10.4 us
    pallas_call x1, Pallas kernels, forecast_inner(): pl.pallas_call(inner_kernel, out_shape=[jax.ShapeDtypeStruct((BANDS, INSI...  8.69 us
    all_to_all x1, starting transfers between devices, shards(): lax.all_to_all(messages, 'member', split_axis=0, concat_axis=0, tiled=True)  7.62 us
    pallas_call x1, Pallas kernels, pick(): pl.pallas_call(pick_kernel, out_shape=jax.ShapeDtypeStruct((BLOCKS, SHARE...  6.53 us
    pallas_call x1, Pallas kernels, arrange(): pl.pallas_call(arrange_kernel, out_shape=shape, in_specs=[ANY], out_specs...  4.36 us
  transfers between devices with their start and end apart: 14, of which 6 were waited for; matrix products, arithmetic and copies ran while one was open for 5% of the time, Pallas kernels for 23%

profile of v3, /device:TPU:8, one launch (start us, length us, event | category | flops | bytes accessed | tf_op | source)
XLA Modules:
  0.0 94.7 jit_solution(5746502007426893471)
XLA Ops:
  0.0 8.7 %forecast_inner.1 = (f32[8,52,16,128]{3,2,1,0:T(8,128)}, f32[3,90,16,128]{3,2,1,0:T(8,128)}) custom-call(f32[5,90,16,128]{3,2,1,0:T(8,128)} %bitcast.16, f32[90,128]{1,0:T(8,128)} %depth.5, s32[90,128]{1,0:T(8,128)} %mask.5, f32[1,128]{1,0:T(1,128)} %bitcast.25), custom_call_target="tpu_custom_call" | custom-call | tf_op jit(solution)/shard_map/forecast_inner/pallas_call | solution.py:193
  8.7 7.6 %all-to-all-start = ((f32[8,52,16,128]{3,2,1,0:T(8,128)}), f32[8,52,16,128]{3,2,1,0:T(8,128)S(1)}, u32[]{:S(2)}, u32[]{:S(2)}) async-start(f32[8,52,16,128]{3,2,1,0:T(8,128)} %get-tuple-element.23), calls=%async_computation | async-start | bytes 6815744 | tf_op jit(solution)/shard_map/all_to_all | solution.py:806
  16.4 1.8 %pack_edges.1 = (f32[6,4,16,128]{3,2,1,0:T(8,128)}, f32[6,4,16,128]{3,2,1,0:T(8,128)}) custom-call(f32[5,90,16,128]{3,2,1,0:T(8,128)} %bitcast.17, f32[90,128]{1,0:T(8,128)} %depth.5, s32[90,128]{1,0:T(8,128)} %mask.5), custom_call_target="tpu_custom_call" | custom-call | tf_op jit(solution)/shard_map/pack_edges/pallas_call | solution.py:64
  18.3 1.7 %collective-permute-start.1 = (f32[6,4,16,128]{3,2,1,0:T(8,128)}, f32[6,4,16,128]{3,2,1,0:T(8,128)}, u32[]{:S(2)}, u32[]{:S(2)}) collective-permute-start(f32[6,4,16,128]{3,2,1,0:T(8,128)} %get-tuple-element.17), channel_id=1, source_target_pairs={{1,0},{2,1},{3,2},{4,3},{5,4},{6,5},{7,6},{8,7},{9,8},{10,9},{11,1... | collective-permute-start | bytes 589832 | tf_op jit(solution)/shard_map/ppermute | solution.py:792
  20.1 0.6 add_select_fusion
  20.7 0.6 stack.48.facts
  21.3 2.7 %obs_in_batch_order.1.facts = f32[8,8,128]{2,1,0:T(8,128)} custom-call(s32[8,1,128]{2,1,0:T(1,128)} %bitcast.20, f32[8,1024]{1,0:T(8,128)} %stack.48.facts), custom_call_target="tpu_custom_call" | custom-call | tf_op jit(solution)/shard_map/obs_in_batch_order/pallas_call | solution.py:349
  24.1 0.7 pad_add_fusion.place
  24.7 2.6 %list_observations.1 = (bf16[2,2,128,512]{3,2,1,0:T(8,128)(2,1)}, f32[512,512]{1,0:T(8,128)}, f32[2,32,128]{2,1,0:T(8,128)}, s32[1]{0:T(128)}) custom-call(s32[3]{0:T(128)} %pad_add_fusion.place, f32[8,8,128]{2,1,0:T(8,128)} %obs_in_batch_order.1.facts), custom_call_target="tpu_custom_call" | custom-call | tf_op jit(solution)/shard_map/list_observations/pallas_call | solution.py:455
  27.4 3.6 %forecast_outer.1 = (f32[8,5,16,128]{3,2,1,0:T(8,128)}, f32[3,90,16,128]{3,2,1,0:T(8,128)}) custom-call(f32[5,90,16,128]{3,2,1,0:T(8,128)} %bitcast.18, f32[6,4,16,128]{3,2,1,0:T(8,128)} %collective-permute-done.left, f32[6,4,16,128]{3,2,1,0:T(8,128)} %collective-permute-done.1.right, f32[90,128]{1,0:T(8,128)} %depth.5, ...), custom_call_target="tpu_custom_call", output_to_operand_aliasing={{1}: (6, {})} | custom-call | tf_op jit(solution)/shard_map/forecast_outer/pallas_call | solution.py:270
  31.0 6.5 %pick_priors.1 = f32[8,16,128]{2,1,0:T(8,128)} custom-call(s32[1024]{0:T(1024)} %order.1, s32[1024]{0:T(1024)} %get-tuple-element.25.cell, f32[270,16,128]{2,1,0:T(8,128)} %bitcast.19, f32[2,32,128]{2,1,0:T(8,128)} %get-tuple-element.20._.where), custom_call_target="tpu_custom_call" | custom-call | tf_op jit(solution)/shard_map/pick_priors/pallas_call | solution.py:320
  37.5 1.7 %collective-permute-start.4 = (f32[8,16,128]{2,1,0:T(8,128)}, f32[8,16,128]{2,1,0:T(8,128)S(1)}, u32[]{:S(2)}, u32[]{:S(2)}) collective-permute-start(f32[8,16,128]{2,1,0:T(8,128)} %pick_priors.1), channel_id=1, source_target_pairs={{0,6},{1,7},{2,4},{3,5},{4,2},{5,3},{6,0},{7,1},{8,14},{9,15},{10,... | collective-permute-start | bytes 196616 | tf_op jit(solution)/shard_map/ppermute | solution.py:771
  39.2 2.9 %collective-permute-start.3 = (f32[8,16,128]{2,1,0:T(8,128)}, f32[8,16,128]{2,1,0:T(8,128)S(1)}, u32[]{:S(2)}, u32[]{:S(2)}) collective-permute-start(f32[8,16,128]{2,1,0:T(8,128)} %pick_priors.1), channel_id=1, source_target_pairs={{0,4},{1,5},{2,6},{3,7},{4,0},{5,1},{6,2},{7,3},{8,12},{9,13},{10,... | collective-permute-start | bytes 196616 | tf_op jit(solution)/shard_map/ppermute | solution.py:771
  42.2 3.0 %collective-permute-done.3 = f32[8,16,128]{2,1,0:T(8,128)S(1)} collective-permute-done((f32[8,16,128]{2,1,0:T(8,128)}, f32[8,16,128]{2,1,0:T(8,128)S(1)}, u32[]{:S(2)}, u32[]{:S(2)}) %collective-permute-start.3) | collective-permute-done | bytes 65568 | tf_op jit(solution)/shard_map/ppermute | solution.py:771
  45.2 1.4 %collective-permute-done.2 = f32[8,16,128]{2,1,0:T(8,128)S(1)} collective-permute-done((f32[8,16,128]{2,1,0:T(8,128)}, f32[8,16,128]{2,1,0:T(8,128)S(1)}, u32[]{:S(2)}, u32[]{:S(2)}) %collective-permute-start.2) | collective-permute-done | bytes 65568 | tf_op jit(solution)/shard_map/ppermute | solution.py:771
  46.6 0.9 add_add_fusion
  47.6 1.2 %collective-permute-done.5 = f32[8,16,128]{2,1,0:T(8,128)S(1)} collective-permute-done((f32[8,16,128]{2,1,0:T(8,128)S(1)}, f32[8,16,128]{2,1,0:T(8,128)S(1)}, u32[]{:S(2)}, u32[]{:S(2)}) %collective-permute-start.5) | collective-permute-done | bytes 65568 | tf_op jit(solution)/shard_map/ppermute | solution.py:771
  48.8 1.0 %collective-permute-start.6 = (f32[8,16,128]{2,1,0:T(8,128)S(1)}, f32[8,16,128]{2,1,0:T(8,128)S(1)}, u32[]{:S(2)}, u32[]{:S(2)}) collective-permute-start(f32[8,16,128]{2,1,0:T(8,128)S(1)} %add.30), channel_id=1, source_target_pairs={{0,8},{1,9},{2,10},{3,11},{4,12},{5,13},{6,14},{7,15},{8,0},{9,1},... | collective-permute-start | bytes 196616 | tf_op jit(solution)/shard_map/ppermute | solution.py:771
  49.8 3.2 %collective-permute-start.8 = (f32[8,16,128]{2,1,0:T(8,128)S(1)}, f32[8,16,128]{2,1,0:T(8,128)S(1)}, u32[]{:S(2)}, u32[]{:S(2)}) collective-permute-start(f32[8,16,128]{2,1,0:T(8,128)S(1)} %add.30), channel_id=1, source_target_pairs={{0,72},{1,73},{2,74},{3,75},{4,76},{5,77},{6,78},{7,79},{8,64},{9,... | collective-permute-start | bytes 196616 | tf_op jit(solution)/shard_map/ppermute | solution.py:815
  53.0 1.0 %collective-permute-start.7 = (f32[8,16,128]{2,1,0:T(8,128)S(1)}, f32[8,16,128]{2,1,0:T(8,128)}, u32[]{:S(2)}, u32[]{:S(2)}) collective-permute-start(f32[8,16,128]{2,1,0:T(8,128)S(1)} %add.30), channel_id=1, source_target_pairs={{0,64},{16,80},{32,96},{48,112},{64,0},{80,16},{96,32},{112,48},{1... | collective-permute-start | bytes 196616 | tf_op jit(solution)/shard_map/ppermute | solution.py:771
  54.0 4.3 %collective-permute-done.6 = f32[8,16,128]{2,1,0:T(8,128)S(1)} collective-permute-done((f32[8,16,128]{2,1,0:T(8,128)S(1)}, f32[8,16,128]{2,1,0:T(8,128)S(1)}, u32[]{:S(2)}, u32[]{:S(2)}) %collective-permute-start.6) | collective-permute-done | bytes 65568 | tf_op jit(solution)/shard_map/ppermute | solution.py:771
  58.3 0.6 add_bitcast_fusion.1
  59.0 13.3 %all-to-all-start.1 = ((f32[8,5,16,128]{3,2,1,0:T(8,128)}), f32[8,5,16,128]{3,2,1,0:T(8,128)}, u32[]{:S(2)}, u32[]{:S(2)}) async-start(f32[8,5,16,128]{3,2,1,0:T(8,128)} %get-tuple-element.24), calls=%async_computation.1 | async-start | bytes 655360 | tf_op jit(solution)/shard_map/all_to_all | solution.py:808
  72.3 0.8 add_bitcast_fusion
  73.1 0.8 pad_maximum_fusion.p0
  74.0 3.3 %collective-permute-start.11 = (f32[2,8,16,128]{3,2,1,0:T(8,128)S(1)}, f32[2,8,16,128]{3,2,1,0:T(8,128)}, u32[]{:S(2)}, u32[]{:S(2)}) collective-permute-start(f32[2,8,16,128]{3,2,1,0:T(8,128)S(1)} %pad_maximum_fusion.p0), channel_id=1, source_target_pairs={{0,48},{16,32},{32,16},{48,0},{64,112},{80,96},{96,80},{112,64},{1... | collective-permute-start | bytes 393224 | tf_op jit(solution)/shard_map/ppermute | solution.py:771
  77.3 0.9 collective-permute-start.10
  78.2 0.1 collective-permute-start.9
  78.3 4.4 %arrange_members.1.given = bf16[52,8,16,256]{3,2,1,0:T(8,128)(2,1)} custom-call(f32[8,52,16,128]{3,2,1,0:T(8,128)} %copy-done), custom_call_target="tpu_custom_call" | custom-call | tf_op jit(solution)/shard_map/arrange_members/pallas_call | solution.py:507
  82.6 0.9 all-to-all-done.1.given_edges
  83.5 0.3 collective-permute-done.10.p2
  83.9 10.7 %analyse.1 = f32[5,90,16,128]{3,2,1,0:T(8,128)} custom-call(s32[3]{0:T(128)} %pad_add_fusion.place, s32[1]{0:T(128)} %get-tuple-element.15.many, f32[2,8,16,128]{3,2,1,0:T(8,128)} %copy-done.1, f32[2,8,16,128]{3,2,1,0:T(8,128)} %collective-permute-done.9.p1, f32[2,8,16,128]{3,2,1,0:T(8,128)} %collective-permute-done.10.p2, ...), custom_call_target="tpu_custom_call" | custom-call | tf_op jit(solution)/shard_map/analyse/pallas_call | solution.py:740
  (27 shorter events, 0.2 us)
Async XLA Ops:
  8.7 50.3 %all-to-all-start = ((f32[8,52,16,128]{3,2,1,0:T(8,128)}), f32[8,52,16,128]{3,2,1,0:T(8,128)S(1)}, u32[]{:S(2)}, u32[]{:S(2)}) async-start(f32[8,52,16,128]{3,2,1,0:T(8,128)} %get-tuple-element.23), calls=%async_computation | async-start | bytes 6815744 | tf_op jit(solution)/shard_map/all_to_all | solution.py:806
  16.3 3.7 %copy-start.2 = (s32[1024]{0:T(1024)S(1)}, s32[1024]{0:T(1024)}, u32[]{:S(2)}) copy-start(s32[1024]{0:T(1024)} %param.17) | copy-start | bytes 12292
  16.3 3.7 %copy-start.3 = (s32[1024]{0:T(1024)S(1)}, s32[1024]{0:T(1024)}, u32[]{:S(2)}) copy-start(s32[1024]{0:T(1024)} %param.18) | copy-start | bytes 12292
  16.3 3.7 %copy-start.4 = (s32[1024]{0:T(1024)S(1)}, s32[1024]{0:T(1024)}, u32[]{:S(2)}) copy-start(s32[1024]{0:T(1024)} %param.16) | copy-start | bytes 12292
  16.4 4.3 %copy-start.5 = (f32[1024]{0:T(1024)S(1)}, f32[1024]{0:T(1024)}, u32[]{:S(2)}) copy-start(f32[1024]{0:T(1024)} %param.14) | copy-start | bytes 12292
  16.4 4.3 %copy-start.6 = (f32[1024]{0:T(1024)S(1)}, f32[1024]{0:T(1024)}, u32[]{:S(2)}) copy-start(f32[1024]{0:T(1024)} %param.15) | copy-start | bytes 12292
  18.2 9.1 %collective-permute-start = (f32[6,4,16,128]{3,2,1,0:T(8,128)}, f32[6,4,16,128]{3,2,1,0:T(8,128)}, u32[]{:S(2)}, u32[]{:S(2)}) collective-permute-start(f32[6,4,16,128]{3,2,1,0:T(8,128)} %get-tuple-element.16), channel_id=1, source_target_pairs={{0,1},{1,2},{2,3},{3,4},{4,5},{5,6},{6,7},{7,8},{8,9},{9,10},{10,1... | collective-permute-start | bytes 589832 | tf_op jit(solution)/shard_map/ppermute | solution.py:791
  18.3 9.0 %collective-permute-start.1 = (f32[6,4,16,128]{3,2,1,0:T(8,128)}, f32[6,4,16,128]{3,2,1,0:T(8,128)}, u32[]{:S(2)}, u32[]{:S(2)}) collective-permute-start(f32[6,4,16,128]{3,2,1,0:T(8,128)} %get-tuple-element.17), channel_id=1, source_target_pairs={{1,0},{2,1},{3,2},{4,3},{5,4},{6,5},{7,6},{8,7},{9,8},{10,9},{11,1... | collective-permute-start | bytes 589832 | tf_op jit(solution)/shard_map/ppermute | solution.py:792
  37.5 4.6 %collective-permute-start.4 = (f32[8,16,128]{2,1,0:T(8,128)}, f32[8,16,128]{2,1,0:T(8,128)S(1)}, u32[]{:S(2)}, u32[]{:S(2)}) collective-permute-start(f32[8,16,128]{2,1,0:T(8,128)} %pick_priors.1), channel_id=1, source_target_pairs={{0,6},{1,7},{2,4},{3,5},{4,2},{5,3},{6,0},{7,1},{8,14},{9,15},{10,... | collective-permute-start | bytes 196616 | tf_op jit(solution)/shard_map/ppermute | solution.py:771
  39.2 6.0 %collective-permute-start.3 = (f32[8,16,128]{2,1,0:T(8,128)}, f32[8,16,128]{2,1,0:T(8,128)S(1)}, u32[]{:S(2)}, u32[]{:S(2)}) collective-permute-start(f32[8,16,128]{2,1,0:T(8,128)} %pick_priors.1), channel_id=1, source_target_pairs={{0,4},{1,5},{2,6},{3,7},{4,0},{5,1},{6,2},{7,3},{8,12},{9,13},{10,... | collective-permute-start | bytes 196616 | tf_op jit(solution)/shard_map/ppermute | solution.py:771
  42.2 4.5 %collective-permute-start.2 = (f32[8,16,128]{2,1,0:T(8,128)}, f32[8,16,128]{2,1,0:T(8,128)S(1)}, u32[]{:S(2)}, u32[]{:S(2)}) collective-permute-start(f32[8,16,128]{2,1,0:T(8,128)} %pick_priors.1), channel_id=1, source_target_pairs={{0,2},{1,3},{2,0},{3,1},{4,6},{5,7},{6,4},{7,5},{8,10},{9,11},{10,... | collective-permute-start | bytes 196616 | tf_op jit(solution)/shard_map/ppermute | solution.py:771
  47.5 1.3 %collective-permute-start.5 = (f32[8,16,128]{2,1,0:T(8,128)S(1)}, f32[8,16,128]{2,1,0:T(8,128)S(1)}, u32[]{:S(2)}, u32[]{:S(2)}) collective-permute-start(f32[8,16,128]{2,1,0:T(8,128)S(1)} %add_add_fusion), channel_id=1, source_target_pairs={{0,1},{1,0},{2,3},{3,2},{4,5},{5,4},{6,7},{7,6},{8,9},{9,8},{10,11... | collective-permute-start | bytes 196616 | tf_op jit(solution)/shard_map/ppermute | solution.py:771
  48.8 9.5 %collective-permute-start.6 = (f32[8,16,128]{2,1,0:T(8,128)S(1)}, f32[8,16,128]{2,1,0:T(8,128)S(1)}, u32[]{:S(2)}, u32[]{:S(2)}) collective-permute-start(f32[8,16,128]{2,1,0:T(8,128)S(1)} %add.30), channel_id=1, source_target_pairs={{0,8},{1,9},{2,10},{3,11},{4,12},{5,13},{6,14},{7,15},{8,0},{9,1},... | collective-permute-start | bytes 196616 | tf_op jit(solution)/shard_map/ppermute | solution.py:771
  49.8 22.4 %collective-permute-start.8 = (f32[8,16,128]{2,1,0:T(8,128)S(1)}, f32[8,16,128]{2,1,0:T(8,128)S(1)}, u32[]{:S(2)}, u32[]{:S(2)}) collective-permute-start(f32[8,16,128]{2,1,0:T(8,128)S(1)} %add.30), channel_id=1, source_target_pairs={{0,72},{1,73},{2,74},{3,75},{4,76},{5,77},{6,78},{7,79},{8,64},{9,... | collective-permute-start | bytes 196616 | tf_op jit(solution)/shard_map/ppermute | solution.py:815
  53.0 19.3 %collective-permute-start.7 = (f32[8,16,128]{2,1,0:T(8,128)S(1)}, f32[8,16,128]{2,1,0:T(8,128)}, u32[]{:S(2)}, u32[]{:S(2)}) collective-permute-start(f32[8,16,128]{2,1,0:T(8,128)S(1)} %add.30), channel_id=1, source_target_pairs={{0,64},{16,80},{32,96},{48,112},{64,0},{80,16},{96,32},{112,48},{1... | collective-permute-start | bytes 196616 | tf_op jit(solution)/shard_map/ppermute | solution.py:771
  59.0 19.3 %copy-start = (f32[8,52,16,128]{3,2,1,0:T(8,128)}, f32[8,52,16,128]{3,2,1,0:T(8,128)S(1)}, u32[]{:S(2)}) copy-start(f32[8,52,16,128]{3,2,1,0:T(8,128)S(1)} %all-to-all-done.parts) | copy-start | bytes 10223620
  59.0 24.6 %all-to-all-start.1 = ((f32[8,5,16,128]{3,2,1,0:T(8,128)}), f32[8,5,16,128]{3,2,1,0:T(8,128)}, u32[]{:S(2)}, u32[]{:S(2)}) async-start(f32[8,5,16,128]{3,2,1,0:T(8,128)} %get-tuple-element.24), calls=%async_computation.1 | async-start | bytes 655360 | tf_op jit(solution)/shard_map/all_to_all | solution.py:808
  74.0 9.9 %copy-start.1 = (f32[2,8,16,128]{3,2,1,0:T(8,128)}, f32[2,8,16,128]{3,2,1,0:T(8,128)S(1)}, u32[]{:S(2)}) copy-start(f32[2,8,16,128]{3,2,1,0:T(8,128)S(1)} %pad_maximum_fusion.p0) | copy-start | bytes 393220
  74.0 9.5 %collective-permute-start.11 = (f32[2,8,16,128]{3,2,1,0:T(8,128)S(1)}, f32[2,8,16,128]{3,2,1,0:T(8,128)}, u32[]{:S(2)}, u32[]{:S(2)}) collective-permute-start(f32[2,8,16,128]{3,2,1,0:T(8,128)S(1)} %pad_maximum_fusion.p0), channel_id=1, source_target_pairs={{0,48},{16,32},{32,16},{48,0},{64,112},{80,96},{96,80},{112,64},{1... | collective-permute-start | bytes 393224 | tf_op jit(solution)/shard_map/ppermute | solution.py:771
  77.3 6.6 %collective-permute-start.10 = (f32[2,8,16,128]{3,2,1,0:T(8,128)S(1)}, f32[2,8,16,128]{3,2,1,0:T(8,128)}, u32[]{:S(2)}, u32[]{:S(2)}) collective-permute-start(f32[2,8,16,128]{3,2,1,0:T(8,128)S(1)} %pad_maximum_fusion.p0), channel_id=1, source_target_pairs={{0,32},{16,48},{32,0},{48,16},{64,96},{80,112},{96,64},{112,80},{1... | collective-permute-start | bytes 393224 | tf_op jit(solution)/shard_map/ppermute | solution.py:771
  78.2 5.7 %collective-permute-start.9 = (f32[2,8,16,128]{3,2,1,0:T(8,128)S(1)}, f32[2,8,16,128]{3,2,1,0:T(8,128)}, u32[]{:S(2)}, u32[]{:S(2)}) collective-permute-start(f32[2,8,16,128]{3,2,1,0:T(8,128)S(1)} %pad_maximum_fusion.p0), channel_id=1, source_target_pairs={{0,16},{16,0},{32,48},{48,32},{64,80},{80,64},{96,112},{112,96},{1... | collective-permute-start | bytes 393224 | tf_op jit(solution)/shard_map/ppermute | solution.py:771

commit v4 on v3

--- a/solution.py
+++ b/solution.py
@@ -160,33 +160,37 @@
     for at, c in zip((1, half), loads):
         c.wait()
         flow(now, nxt, [(at + k, at + k) for k in range(half - 1)])
-    for d, stage, src, dst in ((2, others, now, nxt), (3, flow, nxt, now), (4, others, nxt, now)):
+    for d, stage, src, dst in ((2, others, now, nxt), (3, flow, nxt, now)):
         in_blocks(stage, src, dst, d, WIDTH - d, 0, half - d)
-    keep = pltpu.make_async_copy(
-        now.at[pl.ds(2, 3), pl.ds(EDGE, WIDTH - 2 * EDGE)],
-        seen.at[:, pl.ds(EDGE, WIDTH - 2 * EDGE)],
-        sems.at[1],
-    )
-    keep.start()
-
-    def send(f):
-        at = pl.ds(f * INNER, INNER if isinstance(f, jax.Array) or f < FIELDS else 2)
-        return pltpu.make_async_copy(made.at[:, at], out.at[:, at], sems.at[2 + f])
-
-    turn(now[pl.ds(0, 4), pl.ds(REST_AT, 2)], made, INSIDE - 2)
-    turn(jnp.concatenate([now[4, pl.ds(REST_AT, 2)]] * 4, axis=0), made, INSIDE - 1)
-    send(FIELDS).start()
-
-    def field(f, _):
-        for i in range(INNER):
-            turn(now[f, pl.ds(EDGE + i * 8, 8)], made, f * INNER + i)
-        send(f).start()
-        return 0
-
-    lax.fori_loop(0, FIELDS, field, 0)
-    for f in range(FIELDS + 1):
-        send(f).wait()
-    keep.wait()
+
+    def keep(i, at, n):
+        return pltpu.make_async_copy(
+            now.at[pl.ds(2, 3), pl.ds(at, n)], seen.at[:, pl.ds(at, n)], sems.at[i]
+        )
+
+    def send(i, g, n):
+        at = pl.ds(g, n)
+        return pltpu.make_async_copy(made.at[:, at], out.at[:, at], sems.at[4 + i])
+
+    groups, sends = INNER // 2, []
+    width = half - EDGE
+    for part in range(2):
+        at = EDGE + part * width
+        others(nxt, now, [(at + k, at + k) for k in range(width)])
+        sends.append(keep(part, at, width))
+        sends[-1].start()
+        if part == 1:
+            turn(now[pl.ds(0, 4), pl.ds(REST_AT, 2)], made, INSIDE - 2)
+            turn(jnp.concatenate([now[4, pl.ds(REST_AT, 2)]] * 4, axis=0), made, INSIDE - 1)
+            sends.append(send(2 * FIELDS, INSIDE - 2, 2))
+            sends[-1].start()
+        for f in range(FIELDS):
+            for i in range(part * groups, (part + 1) * groups):
+                turn(now[f, pl.ds(EDGE + i * 8, 8)], made, f * INNER + i)
+            sends.append(send(part * FIELDS + f, f * INNER + part * groups, groups))
+            sends[-1].start()
+    for c in sends:
+        c.wait()
 
 
 def forecast_inner(ens, depth, mask, vort):
@@ -205,7 +209,7 @@
             pltpu.VMEM((WIDTH, LAT), F32),
             pltpu.VMEM((2 * LAT, 2 * LAT), BF16),
             pltpu.VMEM((BANDS, INSIDE, SHARE, LAT), F32),
-            pltpu.SemaphoreType.DMA((3 + FIELDS,)),
+            pltpu.SemaphoreType.DMA((5 + 2 * FIELDS,)),
         ],
         compiler_params=PARAMS,
         name="forecast_inner",
@@ -813,7 +817,8 @@
     axes = ("member", "sector")
     count = lax.axis_size("member") * sectors
     both = lax.ppermute(own, axes, [(i, i ^ (4 * sectors + 8)) for i in range(count)])
-    own = jnp.stack([own + across(own, "sector", 8), across(own, "member", 4) + both])
+    low, high = across(own, "sector", 8), across(own, "member", 4)
+    own = jnp.stack([own, high]) + jnp.stack([low, both])
     priors = [own] + [across(own, "member", x) for x in (1, 2, 3)]
     analysis = analyse(place, many, priors, facts, where, hots, taper, arrange(parts), sides)
     return jnp.transpose(analysis, (0, 2, 1, 3))

time: 95.5 us -> 95.1 us (level)
  other arithmetic: 4.47 us -> 3.06 us
    all_to_all x1, waiting for transfers between devices: 0.01 us -> 4.85 us  [shards(): lax.all_to_all(messages, 'member', split_axis=0, concat_axis=0, tiled=True)]
    ppermute x9, waiting for transfers between devices: 10.4 us -> 6.12 us  [across(): return lax.ppermute(x, axis, [(i, i ^ bits) for i in range(count)])]
    another operation x3 -> x0, other arithmetic: 2.33 us -> none  [shards(): jnp.stack([own + across(own, 'sector', 8), across(own, 'member', 4) + both])]
  transfers between devices with their start and end apart: 14 -> 14, of which waited for: 6 -> 6; matrix products, arithmetic and copies ran while one was open for 5% -> 4% of each run, Pallas kernels for 23% -> 23%
where the time goes in v4:
time: 95.1 us; the launch traced here: 94.2 us
  Pallas kernels  40.6 us (43%)
  starting transfers between devices  37.1 us (39%)
  waiting for transfers between devices  11.9 us (13%)
  other arithmetic  3.06 us (3%)
  local copies, waits for them, and re-layouts  1.28 us (1%)
    all_to_all x1, starting transfers between devices, shards(): lax.all_to_all(sides, 'member', split_axis=0, concat_axis=0, tiled=True)  13.2 us
    pallas_call x1, Pallas kernels, analyse(): pl.pallas_call(analyse_kernel, out_shape=jax.ShapeDtypeStruct((FIELDS, WI...  10.8 us
    ppermute x9, starting transfers between devices, across(): return lax.ppermute(x, axis, [(i, i ^ bits) for i in range(count)])  10.5 us
    pallas_call x1, Pallas kernels, forecast_inner(): pl.pallas_call(inner_kernel, out_shape=[jax.ShapeDtypeStruct((BANDS, INSI...  8.26 us
    all_to_all x1, starting transfers between devices, shards(): lax.all_to_all(messages, 'member', split_axis=0, concat_axis=0, tiled=True)  7.63 us
    pallas_call x1, Pallas kernels, pick(): pl.pallas_call(pick_kernel, out_shape=jax.ShapeDtypeStruct((BLOCKS, SHARE...  6.41 us
    ppermute x9, waiting for transfers between devices, across(): return lax.ppermute(x, axis, [(i, i ^ bits) for i in range(count)])  6.12 us
    all_to_all x1, waiting for transfers between devices, shards(): lax.all_to_all(messages, 'member', split_axis=0, concat_axis=0, tiled=True)  4.85 us
  transfers between devices with their start and end apart: 14, of which 6 were waited for; matrix products, arithmetic and copies ran while one was open for 4% of the time, Pallas kernels for 23%

profile of v4, /device:TPU:8, one launch (start us, length us, event | category | flops | bytes accessed | tf_op | source)
XLA Modules:
  0.0 94.2 jit_solution(10833146559365270832)
XLA Ops:
  0.0 8.3 %forecast_inner.1 = (f32[8,52,16,128]{3,2,1,0:T(8,128)}, f32[3,90,16,128]{3,2,1,0:T(8,128)}) custom-call(f32[5,90,16,128]{3,2,1,0:T(8,128)} %bitcast.16, f32[90,128]{1,0:T(8,128)} %depth.5, s32[90,128]{1,0:T(8,128)} %mask.5, f32[1,128]{1,0:T(1,128)} %bitcast.27), custom_call_target="tpu_custom_call" | custom-call | tf_op jit(solution)/shard_map/forecast_inner/pallas_call | solution.py:197
  8.3 7.6 %all-to-all-start = ((f32[8,52,16,128]{3,2,1,0:T(8,128)}), f32[8,52,16,128]{3,2,1,0:T(8,128)S(1)}, u32[]{:S(2)}, u32[]{:S(2)}) async-start(f32[8,52,16,128]{3,2,1,0:T(8,128)} %get-tuple-element.23), calls=%async_computation | async-start | bytes 6815744 | tf_op jit(solution)/shard_map/all_to_all | solution.py:810
  16.0 1.8 %pack_edges.1 = (f32[6,4,16,128]{3,2,1,0:T(8,128)}, f32[6,4,16,128]{3,2,1,0:T(8,128)}) custom-call(f32[5,90,16,128]{3,2,1,0:T(8,128)} %bitcast.17, f32[90,128]{1,0:T(8,128)} %depth.5, s32[90,128]{1,0:T(8,128)} %mask.5), custom_call_target="tpu_custom_call" | custom-call | tf_op jit(solution)/shard_map/pack_edges/pallas_call | solution.py:64
  17.8 0.1 collective-permute-start
  17.9 1.7 %collective-permute-start.1 = (f32[6,4,16,128]{3,2,1,0:T(8,128)}, f32[6,4,16,128]{3,2,1,0:T(8,128)}, u32[]{:S(2)}, u32[]{:S(2)}) collective-permute-start(f32[6,4,16,128]{3,2,1,0:T(8,128)} %get-tuple-element.17), channel_id=1, source_target_pairs={{1,0},{2,1},{3,2},{4,3},{5,4},{6,5},{7,6},{8,7},{9,8},{10,9},{11,1... | collective-permute-start | bytes 589832 | tf_op jit(solution)/shard_map/ppermute | solution.py:796
  19.6 0.6 add_select_fusion
  20.2 0.6 stack.57.facts
  20.9 2.8 %obs_in_batch_order.1.facts = f32[8,8,128]{2,1,0:T(8,128)} custom-call(s32[8,1,128]{2,1,0:T(1,128)} %bitcast.22, f32[8,1024]{1,0:T(8,128)} %stack.57.facts), custom_call_target="tpu_custom_call" | custom-call | tf_op jit(solution)/shard_map/obs_in_batch_order/pallas_call | solution.py:353
  23.6 0.6 pad_add_fusion.place
  24.3 2.6 %list_observations.1 = (bf16[2,2,128,512]{3,2,1,0:T(8,128)(2,1)}, f32[512,512]{1,0:T(8,128)}, f32[2,32,128]{2,1,0:T(8,128)}, s32[1]{0:T(128)}) custom-call(s32[3]{0:T(128)} %pad_add_fusion.place, f32[8,8,128]{2,1,0:T(8,128)} %obs_in_batch_order.1.facts), custom_call_target="tpu_custom_call" | custom-call | tf_op jit(solution)/shard_map/list_observations/pallas_call | solution.py:459
  26.9 3.6 %forecast_outer.1 = (f32[8,5,16,128]{3,2,1,0:T(8,128)}, f32[3,90,16,128]{3,2,1,0:T(8,128)}) custom-call(f32[5,90,16,128]{3,2,1,0:T(8,128)} %bitcast.18, f32[6,4,16,128]{3,2,1,0:T(8,128)} %collective-permute-done.left, f32[6,4,16,128]{3,2,1,0:T(8,128)} %collective-permute-done.1.right, f32[90,128]{1,0:T(8,128)} %depth.5, ...), custom_call_target="tpu_custom_call", output_to_operand_aliasing={{1}: (6, {})} | custom-call | tf_op jit(solution)/shard_map/forecast_outer/pallas_call | solution.py:274
  30.5 6.4 %pick_priors.1 = f32[8,16,128]{2,1,0:T(8,128)} custom-call(s32[1024]{0:T(1024)} %order.1, s32[1024]{0:T(1024)} %get-tuple-element.25.cell, f32[270,16,128]{2,1,0:T(8,128)} %bitcast.19, f32[2,32,128]{2,1,0:T(8,128)} %get-tuple-element.20._.where), custom_call_target="tpu_custom_call" | custom-call | tf_op jit(solution)/shard_map/pick_priors/pallas_call | solution.py:324
  36.9 1.7 %collective-permute-start.4 = (f32[8,16,128]{2,1,0:T(8,128)}, f32[8,16,128]{2,1,0:T(8,128)S(1)}, u32[]{:S(2)}, u32[]{:S(2)}) collective-permute-start(f32[8,16,128]{2,1,0:T(8,128)} %pick_priors.1), channel_id=1, source_target_pairs={{0,6},{1,7},{2,4},{3,5},{4,2},{5,3},{6,0},{7,1},{8,14},{9,15},{10,... | collective-permute-start | bytes 196616 | tf_op jit(solution)/shard_map/ppermute | solution.py:775
  38.6 2.9 %collective-permute-start.3 = (f32[8,16,128]{2,1,0:T(8,128)}, f32[8,16,128]{2,1,0:T(8,128)S(1)}, u32[]{:S(2)}, u32[]{:S(2)}) collective-permute-start(f32[8,16,128]{2,1,0:T(8,128)} %pick_priors.1), channel_id=1, source_target_pairs={{0,4},{1,5},{2,6},{3,7},{4,0},{5,1},{6,2},{7,3},{8,12},{9,13},{10,... | collective-permute-start | bytes 196616 | tf_op jit(solution)/shard_map/ppermute | solution.py:775
  41.5 3.1 %collective-permute-done.3 = f32[8,16,128]{2,1,0:T(8,128)S(1)} collective-permute-done((f32[8,16,128]{2,1,0:T(8,128)}, f32[8,16,128]{2,1,0:T(8,128)S(1)}, u32[]{:S(2)}, u32[]{:S(2)}) %collective-permute-start.3) | collective-permute-done | bytes 65568 | tf_op jit(solution)/shard_map/ppermute | solution.py:775
  44.7 1.4 %collective-permute-done.2 = f32[8,16,128]{2,1,0:T(8,128)S(1)} collective-permute-done((f32[8,16,128]{2,1,0:T(8,128)}, f32[8,16,128]{2,1,0:T(8,128)S(1)}, u32[]{:S(2)}, u32[]{:S(2)}) %collective-permute-start.2) | collective-permute-done | bytes 65568 | tf_op jit(solution)/shard_map/ppermute | solution.py:775
  46.0 0.9 add_add_fusion
  46.9 0.1 collective-permute-start.5
  47.0 1.2 %collective-permute-done.5 = f32[8,16,128]{2,1,0:T(8,128)S(1)} collective-permute-done((f32[8,16,128]{2,1,0:T(8,128)S(1)}, f32[8,16,128]{2,1,0:T(8,128)S(1)}, u32[]{:S(2)}, u32[]{:S(2)}) %collective-permute-start.5) | collective-permute-done | bytes 65568 | tf_op jit(solution)/shard_map/ppermute | solution.py:775
  48.2 3.9 %collective-permute-start.8 = (f32[8,16,128]{2,1,0:T(8,128)S(1)}, f32[8,16,128]{2,1,0:T(8,128)S(1)}, u32[]{:S(2)}, u32[]{:S(2)}) collective-permute-start(f32[8,16,128]{2,1,0:T(8,128)S(1)} %add.27), channel_id=1, source_target_pairs={{0,72},{1,73},{2,74},{3,75},{4,76},{5,77},{6,78},{7,79},{8,64},{9,... | collective-permute-start | bytes 196616 | tf_op jit(solution)/shard_map/ppermute | solution.py:819
  52.1 1.6 %collective-permute-start.6 = (f32[8,16,128]{2,1,0:T(8,128)S(1)}, f32[8,16,128]{2,1,0:T(8,128)}, u32[]{:S(2)}, u32[]{:S(2)}) collective-permute-start(f32[8,16,128]{2,1,0:T(8,128)S(1)} %add.27), channel_id=1, source_target_pairs={{0,64},{16,80},{32,96},{48,112},{64,0},{80,16},{96,32},{112,48},{1... | collective-permute-start | bytes 196616 | tf_op jit(solution)/shard_map/ppermute | solution.py:775
  53.7 4.9 %all-to-all-done.parts = f32[8,52,16,128]{3,2,1,0:T(8,128)S(1)} async-done(((f32[8,52,16,128]{3,2,1,0:T(8,128)}), f32[8,52,16,128]{3,2,1,0:T(8,128)S(1)}, u32[]{:S(2)}, u32[]{:S(2)}) %all-to-all-start) | async-done | bytes 3407904 | tf_op jit(solution)/shard_map/all_to_all | solution.py:810
  58.5 13.2 %all-to-all-start.1 = ((f32[8,5,16,128]{3,2,1,0:T(8,128)}), f32[8,5,16,128]{3,2,1,0:T(8,128)}, u32[]{:S(2)}, u32[]{:S(2)}) async-start(f32[8,5,16,128]{3,2,1,0:T(8,128)} %get-tuple-element.24), calls=%async_computation.1 | async-start | bytes 655360 | tf_op jit(solution)/shard_map/all_to_all | solution.py:812
  71.8 0.6 copy-done.3
  72.4 1.0 %maximum_add_fusion.p0 = f32[2,8,16,128]{3,2,1,0:T(8,128)S(1)} fusion(f32[1,8,16,128]{3,2,1,0:T(8,128)} %bitcast.12, f32[1,8,16,128]{3,2,1,0:T(8,128)} %bitcast.20, f32[1,8,16,128]{3,2,1,0:T(8,128)} %bitcast.21, f32[1,8,16,128]{3,2,1,0:T(8,128)} %bitcast.13), kind=kLoop, calls=%fused_computation | loop fusion | flops 98304 | bytes 393216 | tf_op jit(solution)/shard_map/add | solution.py:821
  73.4 3.3 %collective-permute-start.11 = (f32[2,8,16,128]{3,2,1,0:T(8,128)S(1)}, f32[2,8,16,128]{3,2,1,0:T(8,128)}, u32[]{:S(2)}, u32[]{:S(2)}) collective-permute-start(f32[2,8,16,128]{3,2,1,0:T(8,128)S(1)} %maximum_add_fusion.p0), channel_id=1, source_target_pairs={{0,48},{16,32},{32,16},{48,0},{64,112},{80,96},{96,80},{112,64},{1... | collective-permute-start | bytes 393224 | tf_op jit(solution)/shard_map/ppermute | solution.py:775
  76.7 0.9 collective-permute-start.10
  77.5 0.1 collective-permute-start.9
  77.6 4.3 %arrange_members.1.given = bf16[52,8,16,256]{3,2,1,0:T(8,128)(2,1)} custom-call(f32[8,52,16,128]{3,2,1,0:T(8,128)} %copy-done), custom_call_target="tpu_custom_call" | custom-call | tf_op jit(solution)/shard_map/arrange_members/pallas_call | solution.py:511
  82.0 0.9 all-to-all-done.1.given_edges
  82.9 0.4 collective-permute-done.10.p2
  83.3 10.8 %analyse.1 = f32[5,90,16,128]{3,2,1,0:T(8,128)} custom-call(s32[3]{0:T(128)} %pad_add_fusion.place, s32[1]{0:T(128)} %get-tuple-element.15.many, f32[2,8,16,128]{3,2,1,0:T(8,128)} %copy-done.1, f32[2,8,16,128]{3,2,1,0:T(8,128)} %collective-permute-done.9.p1, f32[2,8,16,128]{3,2,1,0:T(8,128)} %collective-permute-done.10.p2, ...), custom_call_target="tpu_custom_call" | custom-call | tf_op jit(solution)/shard_map/analyse/pallas_call | solution.py:744
  (29 shorter events, 0.1 us)
Async XLA Ops:
  8.3 50.3 %all-to-all-start = ((f32[8,52,16,128]{3,2,1,0:T(8,128)}), f32[8,52,16,128]{3,2,1,0:T(8,128)S(1)}, u32[]{:S(2)}, u32[]{:S(2)}) async-start(f32[8,52,16,128]{3,2,1,0:T(8,128)} %get-tuple-element.23), calls=%async_computation | async-start | bytes 6815744 | tf_op jit(solution)/shard_map/all_to_all | solution.py:810
  15.9 3.7 %copy-start.4 = (s32[1024]{0:T(1024)S(1)}, s32[1024]{0:T(1024)}, u32[]{:S(2)}) copy-start(s32[1024]{0:T(1024)} %param.17) | copy-start | bytes 12292
  15.9 3.7 %copy-start.5 = (s32[1024]{0:T(1024)S(1)}, s32[1024]{0:T(1024)}, u32[]{:S(2)}) copy-start(s32[1024]{0:T(1024)} %param.18) | copy-start | bytes 12292
  15.9 3.7 %copy-start.6 = (s32[1024]{0:T(1024)S(1)}, s32[1024]{0:T(1024)}, u32[]{:S(2)}) copy-start(s32[1024]{0:T(1024)} %param.16) | copy-start | bytes 12292
  15.9 4.3 %copy-start.7 = (f32[1024]{0:T(1024)S(1)}, f32[1024]{0:T(1024)}, u32[]{:S(2)}) copy-start(f32[1024]{0:T(1024)} %param.14) | copy-start | bytes 12292
  15.9 4.3 %copy-start.8 = (f32[1024]{0:T(1024)S(1)}, f32[1024]{0:T(1024)}, u32[]{:S(2)}) copy-start(f32[1024]{0:T(1024)} %param.15) | copy-start | bytes 12292
  17.8 9.1 %collective-permute-start = (f32[6,4,16,128]{3,2,1,0:T(8,128)}, f32[6,4,16,128]{3,2,1,0:T(8,128)}, u32[]{:S(2)}, u32[]{:S(2)}) collective-permute-start(f32[6,4,16,128]{3,2,1,0:T(8,128)} %get-tuple-element.16), channel_id=1, source_target_pairs={{0,1},{1,2},{2,3},{3,4},{4,5},{5,6},{6,7},{7,8},{8,9},{9,10},{10,1... | collective-permute-start | bytes 589832 | tf_op jit(solution)/shard_map/ppermute | solution.py:795
  17.9 9.0 %collective-permute-start.1 = (f32[6,4,16,128]{3,2,1,0:T(8,128)}, f32[6,4,16,128]{3,2,1,0:T(8,128)}, u32[]{:S(2)}, u32[]{:S(2)}) collective-permute-start(f32[6,4,16,128]{3,2,1,0:T(8,128)} %get-tuple-element.17), channel_id=1, source_target_pairs={{1,0},{2,1},{3,2},{4,3},{5,4},{6,5},{7,6},{8,7},{9,8},{10,9},{11,1... | collective-permute-start | bytes 589832 | tf_op jit(solution)/shard_map/ppermute | solution.py:796
  36.9 4.6 %collective-permute-start.4 = (f32[8,16,128]{2,1,0:T(8,128)}, f32[8,16,128]{2,1,0:T(8,128)S(1)}, u32[]{:S(2)}, u32[]{:S(2)}) collective-permute-start(f32[8,16,128]{2,1,0:T(8,128)} %pick_priors.1), channel_id=1, source_target_pairs={{0,6},{1,7},{2,4},{3,5},{4,2},{5,3},{6,0},{7,1},{8,14},{9,15},{10,... | collective-permute-start | bytes 196616 | tf_op jit(solution)/shard_map/ppermute | solution.py:775
  38.6 6.1 %collective-permute-start.3 = (f32[8,16,128]{2,1,0:T(8,128)}, f32[8,16,128]{2,1,0:T(8,128)S(1)}, u32[]{:S(2)}, u32[]{:S(2)}) collective-permute-start(f32[8,16,128]{2,1,0:T(8,128)} %pick_priors.1), channel_id=1, source_target_pairs={{0,4},{1,5},{2,6},{3,7},{4,0},{5,1},{6,2},{7,3},{8,12},{9,13},{10,... | collective-permute-start | bytes 196616 | tf_op jit(solution)/shard_map/ppermute | solution.py:775
  41.5 4.5 %collective-permute-start.2 = (f32[8,16,128]{2,1,0:T(8,128)}, f32[8,16,128]{2,1,0:T(8,128)S(1)}, u32[]{:S(2)}, u32[]{:S(2)}) collective-permute-start(f32[8,16,128]{2,1,0:T(8,128)} %pick_priors.1), channel_id=1, source_target_pairs={{0,2},{1,3},{2,0},{3,1},{4,6},{5,7},{6,4},{7,5},{8,10},{9,11},{10,... | collective-permute-start | bytes 196616 | tf_op jit(solution)/shard_map/ppermute | solution.py:775
  46.9 1.3 %collective-permute-start.5 = (f32[8,16,128]{2,1,0:T(8,128)S(1)}, f32[8,16,128]{2,1,0:T(8,128)S(1)}, u32[]{:S(2)}, u32[]{:S(2)}) collective-permute-start(f32[8,16,128]{2,1,0:T(8,128)S(1)} %add_add_fusion), channel_id=1, source_target_pairs={{0,1},{1,0},{2,3},{3,2},{4,5},{5,4},{6,7},{7,6},{8,9},{9,8},{10,11... | collective-permute-start | bytes 196616 | tf_op jit(solution)/shard_map/ppermute | solution.py:775
  48.2 23.6 %copy-start.2 = (f32[8,16,128]{2,1,0:T(8,128)}, f32[8,16,128]{2,1,0:T(8,128)S(1)}, u32[]{:S(2)}) copy-start(f32[8,16,128]{2,1,0:T(8,128)S(1)} %add.27) | copy-start | bytes 196612
  48.2 23.6 %collective-permute-start.8 = (f32[8,16,128]{2,1,0:T(8,128)S(1)}, f32[8,16,128]{2,1,0:T(8,128)S(1)}, u32[]{:S(2)}, u32[]{:S(2)}) collective-permute-start(f32[8,16,128]{2,1,0:T(8,128)S(1)} %add.27), channel_id=1, source_target_pairs={{0,72},{1,73},{2,74},{3,75},{4,76},{5,77},{6,78},{7,79},{8,64},{9,... | collective-permute-start | bytes 196616 | tf_op jit(solution)/shard_map/ppermute | solution.py:819
  52.1 19.7 %collective-permute-start.7 = (f32[8,16,128]{2,1,0:T(8,128)S(1)}, f32[8,16,128]{2,1,0:T(8,128)}, u32[]{:S(2)}, u32[]{:S(2)}) collective-permute-start(f32[8,16,128]{2,1,0:T(8,128)S(1)} %add.27), channel_id=1, source_target_pairs={{0,8},{1,9},{2,10},{3,11},{4,12},{5,13},{6,14},{7,15},{8,0},{9,1},... | collective-permute-start | bytes 196616 | tf_op jit(solution)/shard_map/ppermute | solution.py:775
  52.1 19.7 %collective-permute-start.6 = (f32[8,16,128]{2,1,0:T(8,128)S(1)}, f32[8,16,128]{2,1,0:T(8,128)}, u32[]{:S(2)}, u32[]{:S(2)}) collective-permute-start(f32[8,16,128]{2,1,0:T(8,128)S(1)} %add.27), channel_id=1, source_target_pairs={{0,64},{16,80},{32,96},{48,112},{64,0},{80,16},{96,32},{112,48},{1... | collective-permute-start | bytes 196616 | tf_op jit(solution)/shard_map/ppermute | solution.py:775
  58.5 19.1 %copy-start = (f32[8,52,16,128]{3,2,1,0:T(8,128)}, f32[8,52,16,128]{3,2,1,0:T(8,128)S(1)}, u32[]{:S(2)}) copy-start(f32[8,52,16,128]{3,2,1,0:T(8,128)S(1)} %all-to-all-done.parts) | copy-start | bytes 10223620
  58.5 24.4 %all-to-all-start.1 = ((f32[8,5,16,128]{3,2,1,0:T(8,128)}), f32[8,5,16,128]{3,2,1,0:T(8,128)}, u32[]{:S(2)}, u32[]{:S(2)}) async-start(f32[8,5,16,128]{3,2,1,0:T(8,128)} %get-tuple-element.24), calls=%async_computation.1 | async-start | bytes 655360 | tf_op jit(solution)/shard_map/all_to_all | solution.py:812
  71.8 0.6 copy-start.3
  73.4 10.0 %copy-start.1 = (f32[2,8,16,128]{3,2,1,0:T(8,128)}, f32[2,8,16,128]{3,2,1,0:T(8,128)S(1)}, u32[]{:S(2)}) copy-start(f32[2,8,16,128]{3,2,1,0:T(8,128)S(1)} %maximum_add_fusion.p0) | copy-start | bytes 393220
  73.4 9.5 %collective-permute-start.11 = (f32[2,8,16,128]{3,2,1,0:T(8,128)S(1)}, f32[2,8,16,128]{3,2,1,0:T(8,128)}, u32[]{:S(2)}, u32[]{:S(2)}) collective-permute-start(f32[2,8,16,128]{3,2,1,0:T(8,128)S(1)} %maximum_add_fusion.p0), channel_id=1, source_target_pairs={{0,48},{16,32},{32,16},{48,0},{64,112},{80,96},{96,80},{112,64},{1... | collective-permute-start | bytes 393224 | tf_op jit(solution)/shard_map/ppermute | solution.py:775
  76.7 6.6 %collective-permute-start.10 = (f32[2,8,16,128]{3,2,1,0:T(8,128)S(1)}, f32[2,8,16,128]{3,2,1,0:T(8,128)}, u32[]{:S(2)}, u32[]{:S(2)}) collective-permute-start(f32[2,8,16,128]{3,2,1,0:T(8,128)S(1)} %maximum_add_fusion.p0), channel_id=1, source_target_pairs={{0,32},{16,48},{32,0},{48,16},{64,96},{80,112},{96,64},{112,80},{1... | collective-permute-start | bytes 393224 | tf_op jit(solution)/shard_map/ppermute | solution.py:775
  77.5 5.8 %collective-permute-start.9 = (f32[2,8,16,128]{3,2,1,0:T(8,128)S(1)}, f32[2,8,16,128]{3,2,1,0:T(8,128)}, u32[]{:S(2)}, u32[]{:S(2)}) collective-permute-start(f32[2,8,16,128]{3,2,1,0:T(8,128)S(1)} %maximum_add_fusion.p0), channel_id=1, source_target_pairs={{0,16},{16,0},{32,48},{48,32},{64,80},{80,64},{96,112},{112,96},{1... | collective-permute-start | bytes 393224 | tf_op jit(solution)/shard_map/ppermute | solution.py:775

commit v5 on v4

--- a/solution.py
+++ b/solution.py
@@ -569,6 +569,16 @@
         increments = post_mean - mean + (jnp.sqrt(post_var / inflated) - 1.0) * spread
         return root, spread * (1.0 / ((MEMBERS - 1) * inflated)), increments
 
+    def taper_of(spots, lon):
+        base, at, scale = spots[0:SHARE], spots[SHARE : SHARE + 1], spots[SHARE + 8 : SHARE + 9]
+        gap = at - lon
+        t = jnp.maximum(base - gap * gap * scale, 0.0)
+        return t * t
+
+    for q, (lo, hi) in enumerate(((0, CUT), (CUT, WIDTH))):
+        for lon in range(lo, hi):
+            shapes[lon] = taper_of(where[q], float(lon))
+
     root1, scaled1, inc1 = adjust(table[:, pl.ds(0, BATCH)], 0)
 
     later = table[:, pl.ds(BATCH, BATCH)]
@@ -615,12 +625,6 @@
     def product(a, m):
         return times(jnp.concatenate(split(a), axis=1), m)
 
-    def taper_of(spots, lon):
-        base, at, scale = spots[0:SHARE], spots[SHARE : SHARE + 1], spots[SHARE + 8 : SHARE + 9]
-        gap = at - lon
-        t = jnp.maximum(base - gap * gap * scale, 0.0)
-        return t * t
-
     def whole(pair):
         return pair[:, :MEMBERS].astype(F32) + pair[:, MEMBERS:].astype(F32)
 
@@ -647,10 +651,6 @@
 
     @pl.when(many[0] == 0)
     def _():
-        for q, (lo, hi) in enumerate(((0, CUT), (CUT, WIDTH))):
-            for lon in range(lo, hi):
-                shapes[lon] = taper_of(where[q], float(lon))
-
         def shape(lon, n):
             return shapes[pl.ds(lon, n)].reshape(n * SHARE, SLOTS)
 
@@ -679,9 +679,8 @@
             for f in fs:
                 store(f).start()
 
-        some([0, 1])
-        some([2, 3])
-        some([4])
+        some([0, 1, 2])
+        some([3, 4])
 
     @pl.when(many[0] != 0)
     def _():

time: 95.1 us -> 95 us (level)
  no operation moved by 1% of the time
where the time goes in v5:
time: 95 us; the launch traced here: 94.2 us
  Pallas kernels  40.4 us (43%)
  starting transfers between devices  37 us (39%)
  waiting for transfers between devices  12 us (13%)
  other arithmetic  3.06 us (3%)
  local copies, waits for them, and re-layouts  1.28 us (1%)
    all_to_all x1, starting transfers between devices, shards(): lax.all_to_all(sides, 'member', split_axis=0, concat_axis=0, tiled=True)  13.3 us
    pallas_call x1, Pallas kernels, analyse(): pl.pallas_call(analyse_kernel, out_shape=jax.ShapeDtypeStruct((FIELDS, WI...  10.6 us
    ppermute x9, starting transfers between devices, across(): return lax.ppermute(x, axis, [(i, i ^ bits) for i in range(count)])  10.5 us
    pallas_call x1, Pallas kernels, forecast_inner(): pl.pallas_call(inner_kernel, out_shape=[jax.ShapeDtypeStruct((BANDS, INSI...  8.26 us
    all_to_all x1, starting transfers between devices, shards(): lax.all_to_all(messages, 'member', split_axis=0, concat_axis=0, tiled=True)  7.63 us
    pallas_call x1, Pallas kernels, pick(): pl.pallas_call(pick_kernel, out_shape=jax.ShapeDtypeStruct((BLOCKS, SHARE...  6.4 us
    ppermute x9, waiting for transfers between devices, across(): return lax.ppermute(x, axis, [(i, i ^ bits) for i in range(count)])  6.12 us
    all_to_all x1, waiting for transfers between devices, shards(): lax.all_to_all(messages, 'member', split_axis=0, concat_axis=0, tiled=True)  4.97 us
  transfers between devices with their start and end apart: 14, of which 6 were waited for; matrix products, arithmetic and copies ran while one was open for 4% of the time, Pallas kernels for 23%

profile of v5, /device:TPU:8, one launch (start us, length us, event | category | flops | bytes accessed | tf_op | source)
XLA Modules:
  0.0 94.2 jit_solution(16080143457575530448)
XLA Ops:
  0.0 8.3 %forecast_inner.1 = (f32[8,52,16,128]{3,2,1,0:T(8,128)}, f32[3,90,16,128]{3,2,1,0:T(8,128)}) custom-call(f32[5,90,16,128]{3,2,1,0:T(8,128)} %bitcast.16, f32[90,128]{1,0:T(8,128)} %depth.5, s32[90,128]{1,0:T(8,128)} %mask.5, f32[1,128]{1,0:T(1,128)} %bitcast.27), custom_call_target="tpu_custom_call" | custom-call | tf_op jit(solution)/shard_map/forecast_inner/pallas_call | solution.py:197
  8.3 7.6 %all-to-all-start = ((f32[8,52,16,128]{3,2,1,0:T(8,128)}), f32[8,52,16,128]{3,2,1,0:T(8,128)S(1)}, u32[]{:S(2)}, u32[]{:S(2)}) async-start(f32[8,52,16,128]{3,2,1,0:T(8,128)} %get-tuple-element.23), calls=%async_computation | async-start | bytes 6815744 | tf_op jit(solution)/shard_map/all_to_all | solution.py:809
  16.0 1.8 %pack_edges.1 = (f32[6,4,16,128]{3,2,1,0:T(8,128)}, f32[6,4,16,128]{3,2,1,0:T(8,128)}) custom-call(f32[5,90,16,128]{3,2,1,0:T(8,128)} %bitcast.17, f32[90,128]{1,0:T(8,128)} %depth.5, s32[90,128]{1,0:T(8,128)} %mask.5), custom_call_target="tpu_custom_call" | custom-call | tf_op jit(solution)/shard_map/pack_edges/pallas_call | solution.py:64
  17.8 0.1 collective-permute-start
  17.9 1.7 %collective-permute-start.1 = (f32[6,4,16,128]{3,2,1,0:T(8,128)}, f32[6,4,16,128]{3,2,1,0:T(8,128)}, u32[]{:S(2)}, u32[]{:S(2)}) collective-permute-start(f32[6,4,16,128]{3,2,1,0:T(8,128)} %get-tuple-element.17), channel_id=1, source_target_pairs={{1,0},{2,1},{3,2},{4,3},{5,4},{6,5},{7,6},{8,7},{9,8},{10,9},{11,1... | collective-permute-start | bytes 589832 | tf_op jit(solution)/shard_map/ppermute | solution.py:795
  19.6 0.6 add_select_fusion
  20.2 0.6 stack.57.facts
  20.9 2.8 %obs_in_batch_order.1.facts = f32[8,8,128]{2,1,0:T(8,128)} custom-call(s32[8,1,128]{2,1,0:T(1,128)} %bitcast.22, f32[8,1024]{1,0:T(8,128)} %stack.57.facts), custom_call_target="tpu_custom_call" | custom-call | tf_op jit(solution)/shard_map/obs_in_batch_order/pallas_call | solution.py:353
  23.6 0.6 pad_add_fusion.place
  24.3 2.6 %list_observations.1 = (bf16[2,2,128,512]{3,2,1,0:T(8,128)(2,1)}, f32[512,512]{1,0:T(8,128)}, f32[2,32,128]{2,1,0:T(8,128)}, s32[1]{0:T(128)}) custom-call(s32[3]{0:T(128)} %pad_add_fusion.place, f32[8,8,128]{2,1,0:T(8,128)} %obs_in_batch_order.1.facts), custom_call_target="tpu_custom_call" | custom-call | tf_op jit(solution)/shard_map/list_observations/pallas_call | solution.py:459
  26.9 3.6 %forecast_outer.1 = (f32[8,5,16,128]{3,2,1,0:T(8,128)}, f32[3,90,16,128]{3,2,1,0:T(8,128)}) custom-call(f32[5,90,16,128]{3,2,1,0:T(8,128)} %bitcast.18, f32[6,4,16,128]{3,2,1,0:T(8,128)} %collective-permute-done.left, f32[6,4,16,128]{3,2,1,0:T(8,128)} %collective-permute-done.1.right, f32[90,128]{1,0:T(8,128)} %depth.5, ...), custom_call_target="tpu_custom_call", output_to_operand_aliasing={{1}: (6, {})} | custom-call | tf_op jit(solution)/shard_map/forecast_outer/pallas_call | solution.py:274
  30.5 6.4 %pick_priors.1 = f32[8,16,128]{2,1,0:T(8,128)} custom-call(s32[1024]{0:T(1024)} %order.1, s32[1024]{0:T(1024)} %get-tuple-element.25.cell, f32[270,16,128]{2,1,0:T(8,128)} %bitcast.19, f32[2,32,128]{2,1,0:T(8,128)} %get-tuple-element.20._.where), custom_call_target="tpu_custom_call" | custom-call | tf_op jit(solution)/shard_map/pick_priors/pallas_call | solution.py:324
  36.9 1.3 %collective-permute-start.4 = (f32[8,16,128]{2,1,0:T(8,128)}, f32[8,16,128]{2,1,0:T(8,128)S(1)}, u32[]{:S(2)}, u32[]{:S(2)}) collective-permute-start(f32[8,16,128]{2,1,0:T(8,128)} %pick_priors.1), channel_id=1, source_target_pairs={{0,6},{1,7},{2,4},{3,5},{4,2},{5,3},{6,0},{7,1},{8,14},{9,15},{10,... | collective-permute-start | bytes 196616 | tf_op jit(solution)/shard_map/ppermute | solution.py:774
  38.2 3.3 %collective-permute-start.3 = (f32[8,16,128]{2,1,0:T(8,128)}, f32[8,16,128]{2,1,0:T(8,128)S(1)}, u32[]{:S(2)}, u32[]{:S(2)}) collective-permute-start(f32[8,16,128]{2,1,0:T(8,128)} %pick_priors.1), channel_id=1, source_target_pairs={{0,4},{1,5},{2,6},{3,7},{4,0},{5,1},{6,2},{7,3},{8,12},{9,13},{10,... | collective-permute-start | bytes 196616 | tf_op jit(solution)/shard_map/ppermute | solution.py:774
  41.5 2.9 %collective-permute-done.3 = f32[8,16,128]{2,1,0:T(8,128)S(1)} collective-permute-done((f32[8,16,128]{2,1,0:T(8,128)}, f32[8,16,128]{2,1,0:T(8,128)S(1)}, u32[]{:S(2)}, u32[]{:S(2)}) %collective-permute-start.3) | collective-permute-done | bytes 65568 | tf_op jit(solution)/shard_map/ppermute | solution.py:774
  44.4 1.6 %collective-permute-done.2 = f32[8,16,128]{2,1,0:T(8,128)S(1)} collective-permute-done((f32[8,16,128]{2,1,0:T(8,128)}, f32[8,16,128]{2,1,0:T(8,128)S(1)}, u32[]{:S(2)}, u32[]{:S(2)}) %collective-permute-start.2) | collective-permute-done | bytes 65568 | tf_op jit(solution)/shard_map/ppermute | solution.py:774
  46.0 0.9 add_add_fusion
  46.9 0.1 collective-permute-start.5
  47.0 1.2 %collective-permute-done.5 = f32[8,16,128]{2,1,0:T(8,128)S(1)} collective-permute-done((f32[8,16,128]{2,1,0:T(8,128)S(1)}, f32[8,16,128]{2,1,0:T(8,128)S(1)}, u32[]{:S(2)}, u32[]{:S(2)}) %collective-permute-start.5) | collective-permute-done | bytes 65568 | tf_op jit(solution)/shard_map/ppermute | solution.py:774
  48.2 3.8 %collective-permute-start.8 = (f32[8,16,128]{2,1,0:T(8,128)S(1)}, f32[8,16,128]{2,1,0:T(8,128)S(1)}, u32[]{:S(2)}, u32[]{:S(2)}) collective-permute-start(f32[8,16,128]{2,1,0:T(8,128)S(1)} %add.27), channel_id=1, source_target_pairs={{0,72},{1,73},{2,74},{3,75},{4,76},{5,77},{6,78},{7,79},{8,64},{9,... | collective-permute-start | bytes 196616 | tf_op jit(solution)/shard_map/ppermute | solution.py:818
  52.0 1.6 %collective-permute-start.6 = (f32[8,16,128]{2,1,0:T(8,128)S(1)}, f32[8,16,128]{2,1,0:T(8,128)}, u32[]{:S(2)}, u32[]{:S(2)}) collective-permute-start(f32[8,16,128]{2,1,0:T(8,128)S(1)} %add.27), channel_id=1, source_target_pairs={{0,64},{16,80},{32,96},{48,112},{64,0},{80,16},{96,32},{112,48},{1... | collective-permute-start | bytes 196616 | tf_op jit(solution)/shard_map/ppermute | solution.py:774
  53.6 5.0 %all-to-all-done.parts = f32[8,52,16,128]{3,2,1,0:T(8,128)S(1)} async-done(((f32[8,52,16,128]{3,2,1,0:T(8,128)}), f32[8,52,16,128]{3,2,1,0:T(8,128)S(1)}, u32[]{:S(2)}, u32[]{:S(2)}) %all-to-all-start) | async-done | bytes 3407904 | tf_op jit(solution)/shard_map/all_to_all | solution.py:809
  58.5 13.3 %all-to-all-start.1 = ((f32[8,5,16,128]{3,2,1,0:T(8,128)}), f32[8,5,16,128]{3,2,1,0:T(8,128)}, u32[]{:S(2)}, u32[]{:S(2)}) async-start(f32[8,5,16,128]{3,2,1,0:T(8,128)} %get-tuple-element.24), calls=%async_computation.1 | async-start | bytes 655360 | tf_op jit(solution)/shard_map/all_to_all | solution.py:811
  71.8 0.6 copy-done.3
  72.4 1.0 %maximum_add_fusion.p0 = f32[2,8,16,128]{3,2,1,0:T(8,128)S(1)} fusion(f32[1,8,16,128]{3,2,1,0:T(8,128)} %bitcast.12, f32[1,8,16,128]{3,2,1,0:T(8,128)} %bitcast.20, f32[1,8,16,128]{3,2,1,0:T(8,128)} %bitcast.21, f32[1,8,16,128]{3,2,1,0:T(8,128)} %bitcast.13), kind=kLoop, calls=%fused_computation | loop fusion | flops 98304 | bytes 393216 | tf_op jit(solution)/shard_map/add | solution.py:820
  73.4 3.3 %collective-permute-start.11 = (f32[2,8,16,128]{3,2,1,0:T(8,128)S(1)}, f32[2,8,16,128]{3,2,1,0:T(8,128)}, u32[]{:S(2)}, u32[]{:S(2)}) collective-permute-start(f32[2,8,16,128]{3,2,1,0:T(8,128)S(1)} %maximum_add_fusion.p0), channel_id=1, source_target_pairs={{0,48},{16,32},{32,16},{48,0},{64,112},{80,96},{96,80},{112,64},{1... | collective-permute-start | bytes 393224 | tf_op jit(solution)/shard_map/ppermute | solution.py:774
  76.7 0.9 collective-permute-start.10
  77.6 0.1 collective-permute-start.9
  77.7 4.3 %arrange_members.1.given = bf16[52,8,16,256]{3,2,1,0:T(8,128)(2,1)} custom-call(f32[8,52,16,128]{3,2,1,0:T(8,128)} %copy-done), custom_call_target="tpu_custom_call" | custom-call | tf_op jit(solution)/shard_map/arrange_members/pallas_call | solution.py:511
  82.0 0.9 all-to-all-done.1.given_edges
  82.9 0.4 collective-permute-done.10.p2
  83.3 10.6 %analyse.1 = f32[5,90,16,128]{3,2,1,0:T(8,128)} custom-call(s32[3]{0:T(128)} %pad_add_fusion.place, s32[1]{0:T(128)} %get-tuple-element.15.many, f32[2,8,16,128]{3,2,1,0:T(8,128)} %copy-done.1, f32[2,8,16,128]{3,2,1,0:T(8,128)} %collective-permute-done.9.p1, f32[2,8,16,128]{3,2,1,0:T(8,128)} %collective-permute-done.10.p2, ...), custom_call_target="tpu_custom_call" | custom-call | tf_op jit(solution)/shard_map/analyse/pallas_call | solution.py:743
  (29 shorter events, 0.1 us)
Async XLA Ops:
  8.3 50.3 %all-to-all-start = ((f32[8,52,16,128]{3,2,1,0:T(8,128)}), f32[8,52,16,128]{3,2,1,0:T(8,128)S(1)}, u32[]{:S(2)}, u32[]{:S(2)}) async-start(f32[8,52,16,128]{3,2,1,0:T(8,128)} %get-tuple-element.23), calls=%async_computation | async-start | bytes 6815744 | tf_op jit(solution)/shard_map/all_to_all | solution.py:809
  15.9 3.7 %copy-start.4 = (s32[1024]{0:T(1024)S(1)}, s32[1024]{0:T(1024)}, u32[]{:S(2)}) copy-start(s32[1024]{0:T(1024)} %param.17) | copy-start | bytes 12292
  15.9 3.7 %copy-start.5 = (s32[1024]{0:T(1024)S(1)}, s32[1024]{0:T(1024)}, u32[]{:S(2)}) copy-start(s32[1024]{0:T(1024)} %param.18) | copy-start | bytes 12292
  15.9 3.7 %copy-start.6 = (s32[1024]{0:T(1024)S(1)}, s32[1024]{0:T(1024)}, u32[]{:S(2)}) copy-start(s32[1024]{0:T(1024)} %param.16) | copy-start | bytes 12292
  15.9 4.3 %copy-start.7 = (f32[1024]{0:T(1024)S(1)}, f32[1024]{0:T(1024)}, u32[]{:S(2)}) copy-start(f32[1024]{0:T(1024)} %param.14) | copy-start | bytes 12292
  15.9 4.3 %copy-start.8 = (f32[1024]{0:T(1024)S(1)}, f32[1024]{0:T(1024)}, u32[]{:S(2)}) copy-start(f32[1024]{0:T(1024)} %param.15) | copy-start | bytes 12292
  17.8 9.1 %collective-permute-start = (f32[6,4,16,128]{3,2,1,0:T(8,128)}, f32[6,4,16,128]{3,2,1,0:T(8,128)}, u32[]{:S(2)}, u32[]{:S(2)}) collective-permute-start(f32[6,4,16,128]{3,2,1,0:T(8,128)} %get-tuple-element.16), channel_id=1, source_target_pairs={{0,1},{1,2},{2,3},{3,4},{4,5},{5,6},{6,7},{7,8},{8,9},{9,10},{10,1... | collective-permute-start | bytes 589832 | tf_op jit(solution)/shard_map/ppermute | solution.py:794
  17.9 9.0 %collective-permute-start.1 = (f32[6,4,16,128]{3,2,1,0:T(8,128)}, f32[6,4,16,128]{3,2,1,0:T(8,128)}, u32[]{:S(2)}, u32[]{:S(2)}) collective-permute-start(f32[6,4,16,128]{3,2,1,0:T(8,128)} %get-tuple-element.17), channel_id=1, source_target_pairs={{1,0},{2,1},{3,2},{4,3},{5,4},{6,5},{7,6},{8,7},{9,8},{10,9},{11,1... | collective-permute-start | bytes 589832 | tf_op jit(solution)/shard_map/ppermute | solution.py:795
  36.9 4.6 %collective-permute-start.4 = (f32[8,16,128]{2,1,0:T(8,128)}, f32[8,16,128]{2,1,0:T(8,128)S(1)}, u32[]{:S(2)}, u32[]{:S(2)}) collective-permute-start(f32[8,16,128]{2,1,0:T(8,128)} %pick_priors.1), channel_id=1, source_target_pairs={{0,6},{1,7},{2,4},{3,5},{4,2},{5,3},{6,0},{7,1},{8,14},{9,15},{10,... | collective-permute-start | bytes 196616 | tf_op jit(solution)/shard_map/ppermute | solution.py:774
  38.2 6.2 %collective-permute-start.3 = (f32[8,16,128]{2,1,0:T(8,128)}, f32[8,16,128]{2,1,0:T(8,128)S(1)}, u32[]{:S(2)}, u32[]{:S(2)}) collective-permute-start(f32[8,16,128]{2,1,0:T(8,128)} %pick_priors.1), channel_id=1, source_target_pairs={{0,4},{1,5},{2,6},{3,7},{4,0},{5,1},{6,2},{7,3},{8,12},{9,13},{10,... | collective-permute-start | bytes 196616 | tf_op jit(solution)/shard_map/ppermute | solution.py:774
  41.5 4.5 %collective-permute-start.2 = (f32[8,16,128]{2,1,0:T(8,128)}, f32[8,16,128]{2,1,0:T(8,128)S(1)}, u32[]{:S(2)}, u32[]{:S(2)}) collective-permute-start(f32[8,16,128]{2,1,0:T(8,128)} %pick_priors.1), channel_id=1, source_target_pairs={{0,2},{1,3},{2,0},{3,1},{4,6},{5,7},{6,4},{7,5},{8,10},{9,11},{10,... | collective-permute-start | bytes 196616 | tf_op jit(solution)/shard_map/ppermute | solution.py:774
  46.9 1.3 %collective-permute-start.5 = (f32[8,16,128]{2,1,0:T(8,128)S(1)}, f32[8,16,128]{2,1,0:T(8,128)S(1)}, u32[]{:S(2)}, u32[]{:S(2)}) collective-permute-start(f32[8,16,128]{2,1,0:T(8,128)S(1)} %add_add_fusion), channel_id=1, source_target_pairs={{0,1},{1,0},{2,3},{3,2},{4,5},{5,4},{6,7},{7,6},{8,9},{9,8},{10,11... | collective-permute-start | bytes 196616 | tf_op jit(solution)/shard_map/ppermute | solution.py:774
  48.2 23.6 %copy-start.2 = (f32[8,16,128]{2,1,0:T(8,128)}, f32[8,16,128]{2,1,0:T(8,128)S(1)}, u32[]{:S(2)}) copy-start(f32[8,16,128]{2,1,0:T(8,128)S(1)} %add.27) | copy-start | bytes 196612
  48.2 23.6 %collective-permute-start.8 = (f32[8,16,128]{2,1,0:T(8,128)S(1)}, f32[8,16,128]{2,1,0:T(8,128)S(1)}, u32[]{:S(2)}, u32[]{:S(2)}) collective-permute-start(f32[8,16,128]{2,1,0:T(8,128)S(1)} %add.27), channel_id=1, source_target_pairs={{0,72},{1,73},{2,74},{3,75},{4,76},{5,77},{6,78},{7,79},{8,64},{9,... | collective-permute-start | bytes 196616 | tf_op jit(solution)/shard_map/ppermute | solution.py:818
  52.0 19.8 %collective-permute-start.7 = (f32[8,16,128]{2,1,0:T(8,128)S(1)}, f32[8,16,128]{2,1,0:T(8,128)}, u32[]{:S(2)}, u32[]{:S(2)}) collective-permute-start(f32[8,16,128]{2,1,0:T(8,128)S(1)} %add.27), channel_id=1, source_target_pairs={{0,8},{1,9},{2,10},{3,11},{4,12},{5,13},{6,14},{7,15},{8,0},{9,1},... | collective-permute-start | bytes 196616 | tf_op jit(solution)/shard_map/ppermute | solution.py:774
  52.0 19.8 %collective-permute-start.6 = (f32[8,16,128]{2,1,0:T(8,128)S(1)}, f32[8,16,128]{2,1,0:T(8,128)}, u32[]{:S(2)}, u32[]{:S(2)}) collective-permute-start(f32[8,16,128]{2,1,0:T(8,128)S(1)} %add.27), channel_id=1, source_target_pairs={{0,64},{16,80},{32,96},{48,112},{64,0},{80,16},{96,32},{112,48},{1... | collective-permute-start | bytes 196616 | tf_op jit(solution)/shard_map/ppermute | solution.py:774
  58.5 19.1 %copy-start = (f32[8,52,16,128]{3,2,1,0:T(8,128)}, f32[8,52,16,128]{3,2,1,0:T(8,128)S(1)}, u32[]{:S(2)}) copy-start(f32[8,52,16,128]{3,2,1,0:T(8,128)S(1)} %all-to-all-done.parts) | copy-start | bytes 10223620
  58.5 24.4 %all-to-all-start.1 = ((f32[8,5,16,128]{3,2,1,0:T(8,128)}), f32[8,5,16,128]{3,2,1,0:T(8,128)}, u32[]{:S(2)}, u32[]{:S(2)}) async-start(f32[8,5,16,128]{3,2,1,0:T(8,128)} %get-tuple-element.24), calls=%async_computation.1 | async-start | bytes 655360 | tf_op jit(solution)/shard_map/all_to_all | solution.py:811
  71.8 0.6 copy-start.3
  73.4 10.0 %copy-start.1 = (f32[2,8,16,128]{3,2,1,0:T(8,128)}, f32[2,8,16,128]{3,2,1,0:T(8,128)S(1)}, u32[]{:S(2)}) copy-start(f32[2,8,16,128]{3,2,1,0:T(8,128)S(1)} %maximum_add_fusion.p0) | copy-start | bytes 393220
  73.4 9.5 %collective-permute-start.11 = (f32[2,8,16,128]{3,2,1,0:T(8,128)S(1)}, f32[2,8,16,128]{3,2,1,0:T(8,128)}, u32[]{:S(2)}, u32[]{:S(2)}) collective-permute-start(f32[2,8,16,128]{3,2,1,0:T(8,128)S(1)} %maximum_add_fusion.p0), channel_id=1, source_target_pairs={{0,48},{16,32},{32,16},{48,0},{64,112},{80,96},{96,80},{112,64},{1... | collective-permute-start | bytes 393224 | tf_op jit(solution)/shard_map/ppermute | solution.py:774
  76.7 6.6 %collective-permute-start.10 = (f32[2,8,16,128]{3,2,1,0:T(8,128)S(1)}, f32[2,8,16,128]{3,2,1,0:T(8,128)}, u32[]{:S(2)}, u32[]{:S(2)}) collective-permute-start(f32[2,8,16,128]{3,2,1,0:T(8,128)S(1)} %maximum_add_fusion.p0), channel_id=1, source_target_pairs={{0,32},{16,48},{32,0},{48,16},{64,96},{80,112},{96,64},{112,80},{1... | collective-permute-start | bytes 393224 | tf_op jit(solution)/shard_map/ppermute | solution.py:774
  77.6 5.8 %collective-permute-start.9 = (f32[2,8,16,128]{3,2,1,0:T(8,128)S(1)}, f32[2,8,16,128]{3,2,1,0:T(8,128)}, u32[]{:S(2)}, u32[]{:S(2)}) collective-permute-start(f32[2,8,16,128]{3,2,1,0:T(8,128)S(1)} %maximum_add_fusion.p0), channel_id=1, source_target_pairs={{0,16},{16,0},{32,48},{48,32},{64,80},{80,64},{96,112},{112,96},{1... | collective-permute-start | bytes 393224 | tf_op jit(solution)/shard_map/ppermute | solution.py:774
